TPU v7x, 32 devices: a whole 2x2x4 slice. The times are simulated.
32 devices in a mesh: grp: 2 (over x), fin: 8 (over z, y), fout: 2 (over core).
Axes of the slice: x: 2, y: 2, z: 4, core: 2. Of those that a mesh axis runs over, the one named last changes fastest.
Arguments:
- tokens: bfloat16 [512, 6144], P(('grp', 'fin'), 'fout'), parts along dimension 0, may hold values from -6 to 6
- w_up: bfloat16 [6144, 24576], P('fout', 'fin'), may hold values from -0.078125 to 0.078125
- w_down: bfloat16 [24576, 6144], P('fin', 'fout'), may hold values from -0.0390625 to 0.0390625
- up_scale: float32 [8, 24576], P(None, 'fin'), may hold values from 0.25 to 4
- down_scale: float32 [8, 6144], P(None, 'fout'), may hold values from 0.25 to 4
- step_group: int32 [16], P('grp'), parts along dimension 0, may hold values from 0 to 7
- req_lengths: int32 [16], P('grp'), parts along dimension 0, may hold values from 1 to 64, 256 in all
Outputs:
- mixed: bfloat16 [512, 6144], P(('grp', 'fin'), 'fout'), parts along dimension 0
There are 2 independent parts, one for each index of `grp`. A program takes and returns all parts, laid end to end along the dimension named above; an argument that names none is the same for every part. Nothing has to cross between parts.
Inputs may be any that keep to these rules, and one draw needn't show every extreme that they name: `req_lengths`: the lengths sum to 256.
All inputs are finite; a program needn't handle non-finite values.
Results may differ from a plain program's by a relative error of at most 0.005.
Values may be sent and summed in bfloat16 or wider, within the bound.
No kernel may reach another device: no remote copies, remote signals or barrier semaphores. Data moves between devices by JAX's collectives and lax.ppermute only.
A program may use at most 128 MiB of HBM per device.

v0:
```python
import jax
import jax.numpy as jnp
from jax import lax
from jax.sharding import PartitionSpec as P


def group_table(first, count, req_lengths, step_group, groups):
    rows = first + jnp.arange(count, dtype=jnp.int32)
    ends = jnp.cumsum(req_lengths)
    request = jnp.sum((rows[:, None] >= ends[None, :]).astype(jnp.int32), axis=1)
    picked = (
        request[:, None] == jnp.arange(req_lengths.shape[0], dtype=jnp.int32)[None, :]
    ).astype(jnp.int32)
    row_group = jnp.sum(picked * step_group[None, :], axis=1)
    return (row_group[:, None] == jnp.arange(groups, dtype=jnp.int32)[None, :]).astype(jnp.float32)


def on_device(tokens, w_up, w_down, up_scale, down_scale, step_group, req_lengths):
    groups = up_scale.shape[0]
    pre = jnp.dot(
        lax.all_gather(tokens, "fin", axis=0, tiled=True), w_up, preferred_element_type=jnp.float32
    )
    total_rows = pre.shape[0]
    half_sum = lax.psum_scatter(pre, "fout", scatter_dimension=0, tiled=True)
    half_rows = half_sum.shape[0]
    onehot_half = group_table(
        lax.axis_index("fout") * half_rows, half_rows, req_lengths, step_group, groups
    )
    scale_one = jnp.dot(onehot_half, up_scale, precision=lax.Precision.HIGHEST)
    half_hidden = jax.nn.gelu(half_sum * scale_one, approximate=True).astype(jnp.bfloat16)
    hidden = lax.all_gather(half_hidden, "fout", axis=0, tiled=True)
    fin_count = lax.axis_size("fin")
    own_rows = total_rows // fin_count
    summed_rows = lax.psum_scatter(
        jnp.dot(hidden, w_down, preferred_element_type=jnp.float32),
        "fin",
        scatter_dimension=0,
        tiled=True,
    )
    onehot_own = group_table(
        lax.axis_index("fin") * own_rows, own_rows, req_lengths, step_group, groups
    )
    scale_two = jnp.dot(onehot_own, down_scale, precision=lax.Precision.HIGHEST)
    return (summed_rows * scale_two).astype(jnp.bfloat16)


def solution(mesh):
    return jax.shard_map(
        on_device,
        mesh=mesh,
        in_specs=(
            P(("grp", "fin"), "fout"),
            P("fout", "fin"),
            P("fin", "fout"),
            P(None, "fin"),
            P(None, "fout"),
            P("grp"),
            P("grp"),
        ),
        out_specs=P(("grp", "fin"), "fout"),
        check_vma=False,
    )
```

profile of v0, /device:TPU:0, one launch (start us, length us, event | category | flops | bytes accessed | tf_op | source)
XLA Modules:
  0.0 186.5 jit_solution(5371787766786748752)
XLA Ops:
  6.5 0.0 copy-start
  6.5 0.0 all-gather.3.cloned.1.call-start
  6.5 0.7 all-gather.3.cloned.1.call-update
  7.3 0.0 reduce-scatter.3.cloned.1.call-start
  7.3 49.2 %all-gather.3.cloned.1.call-done = bf16[256,3072]{1,0:T(8,128)(2,1)} async-done(((bf16[32,3072]{1,0:T(8,128)(2,1)}), bf16[256,3072]{1,0:T(8,128)(2,1)}) %all-gather.3.cloned.1.call-update) | async-done | bytes 1572880 | tf_op jit(solution)/shard_map/all_gather | solution.py:21
  56.5 10.6 %fusion.11 = f32[256,3072]{1,0:T(8,128)} fusion(bf16[256,3072]{1,0:T(8,128)(2,1)} %all-gather.3.cloned.1.call-done, bf16[3072,3072]{1,0:T(8,128)(2,1)} %param.8), kind=kOutput, calls=%fused_computation.24 | convolution fusion | flops 4831838208 | bytes 23592960 | tf_op jit(solution)/shard_map/dot_general | solution.py:20
  67.0 0.0 reduce-scatter.3.cloned.1.call-update
  67.1 0.0 all-gather.5.cloned.1.call-start
  67.1 0.6 copy-done.2
  67.7 0.2 reduce-window.8
  67.9 0.1 convert_reduce_fusion.1
  68.0 0.1 select_reduce_fusion.1
  68.0 8.9 %reduce-scatter.3.cloned.1.call-done = f32[128,3072]{1,0:T(8,128)} async-done(((f32[256,3072]{1,0:T(8,128)}), f32[128,3072]{1,0:T(8,128)}) %reduce-scatter.3.cloned.1.call-update) | async-done | bytes 1572880 | tf_op jit(solution)/shard_map/reduce_scatter | solution.py:24
  77.0 0.0 copy-done
  77.0 3.6 %fusion.8 = bf16[128,3072]{1,0:T(8,128)(2,1)} fusion(f32[128,3072]{1,0:T(8,128)} %reduce-scatter.3.cloned.1.call-done, f32[8,3072]{1,0:T(8,128)S(1)} %copy-done, s32[128]{0:T(128)S(1)} %select_reduce_fusion.1), kind=kOutput, calls=%fused_computation.11 | convolution fusion | flops 41681920 | bytes 2458112 | tf_op jit(solution)/shard_map/dot_general | solution.py:29
  80.5 0.0 all-gather.5.cloned.1.call-update
  80.6 0.0 reduce-scatter.5.cloned.1.call-start
  80.6 11.1 %all-gather.5.cloned.1.call-done = bf16[256,3072]{1,0:T(8,128)(2,1)} async-done(((bf16[128,3072]{1,0:T(8,128)(2,1)}), bf16[256,3072]{1,0:T(8,128)(2,1)}) %all-gather.5.cloned.1.call-update) | async-done | bytes 1572880 | tf_op jit(solution)/shard_map/all_gather | solution.py:31
  91.7 10.6 %fusion.12 = f32[256,3072]{1,0:T(8,128)} fusion(bf16[256,3072]{1,0:T(8,128)(2,1)} %all-gather.5.cloned.1.call-done, bf16[3072,3072]{1,0:T(8,128)(2,1)} %param.9), kind=kOutput, calls=%fused_computation.25 | convolution fusion | flops 4831838208 | bytes 23592960 | tf_op jit(solution)/shard_map/dot_general | solution.py:35
  102.3 0.0 reduce-scatter.5.cloned.1.call-update
  102.3 0.1 convert_reduce_fusion
  102.4 0.1 select_reduce_fusion
  102.5 75.5 %reduce-scatter.5.cloned.1.call-done = f32[32,3072]{1,0:T(8,128)} async-done(((f32[256,3072]{1,0:T(8,128)}), f32[32,3072]{1,0:T(8,128)}) %reduce-scatter.5.cloned.1.call-update) | async-done | bytes 393232 | tf_op jit(solution)/shard_map/reduce_scatter | solution.py:34
  177.9 2.0 %fusion = bf16[32,3072]{1,0:T(8,128)(2,1)} fusion(f32[32,3072]{1,0:T(8,128)} %reduce-scatter.5.cloned.1.call-done, f32[8,3072]{1,0:T(8,128)S(1)} %copy-done.1, s32[32]{0:T(128)S(1)} %select_reduce_fusion), kind=kOutput, calls=%fused_computation.2 | convolution fusion | flops 9634048 | bytes 688256 | tf_op jit(solution)/shard_map/dot_general | solution.py:43
  (7 shorter events, 0.0 us)
Async XLA Ops:
  6.5 70.4 %copy-start = (f32[8,3072]{1,0:T(8,128)S(1)}, f32[8,3072]{1,0:T(8,128)}, u32[]{:S(2)}) copy-start(f32[8,3072]{1,0:T(8,128)} %param.10) | copy-start | bytes 294916
  6.5 49.9 %all-gather.3.cloned.1.call-start = ((), (), s32[]{:S(2)}) async-start(), calls=%async_computation.2 | async-start | bytes 1769472 | tf_op jit(solution)/shard_map/all_gather | solution.py:21
  7.3 69.7 %reduce-scatter.3.cloned.1.call-start = ((), (), s32[]{:S(2)}) async-start(), calls=%async_computation.3 | async-start | bytes 4718592 | tf_op jit(solution)/shard_map/reduce_scatter | solution.py:24
  67.0 0.7 copy-start.2
  67.0 0.9 copy-start.3
  67.1 24.6 %all-gather.5.cloned.1.call-start = ((), (), s32[]{:S(2)}) async-start(), calls=%async_computation.4 | async-start | bytes 2359296 | tf_op jit(solution)/shard_map/all_gather | solution.py:31
  80.6 97.4 %reduce-scatter.5.cloned.1.call-start = ((), (), s32[]{:S(2)}) async-start(), calls=%async_computation.5 | async-start | bytes 3538944 | tf_op jit(solution)/shard_map/reduce_scatter | solution.py:34
  102.3 75.7 %copy-start.1 = (f32[8,3072]{1,0:T(8,128)S(1)}, f32[8,3072]{1,0:T(8,128)}, u32[]{:S(2)}) copy-start(f32[8,3072]{1,0:T(8,128)} %param.11) | copy-start | bytes 294916
Sparse Core Ops, SparseCore 0:
  9.5 46.8 all-gather.2
  67.2 9.7 reduce-scatter.2
  80.7 10.9 all-gather.4
  102.4 75.4 reduce-scatter.4
where the time goes:
time: 187 us
  waiting for transfers between devices  145 us (78%)
  matrix products  26.8 us (14%)
  between operations  13.2 us (7%)
    reduce_scatter x1, waiting for transfers between devices, on_device(): lax.psum_scatter(jnp.dot(hidden, w_down, preferred_element_type=jnp.float...  75.5 us
    all_gather x1, waiting for transfers between devices, on_device(): lax.all_gather(tokens, 'fin', axis=0, tiled=True)  49.2 us
    all_gather x1, waiting for transfers between devices, on_device(): hidden = lax.all_gather(half_hidden, 'fout', axis=0, tiled=True)  11.1 us
    dot_general x1, matrix products, on_device(): jnp.dot(hidden, w_down, preferred_element_type=jnp.float32)  10.6 us
    dot_general x1, matrix products, on_device(): jnp.dot(lax.all_gather(tokens, 'fin', axis=0, tiled=True), w_up, preferre...  10.6 us
    reduce_scatter x1, waiting for transfers between devices, on_device(): half_sum = lax.psum_scatter(pre, 'fout', scatter_dimension=0, tiled=True)  8.92 us
  transfers between devices with their start and end apart: 4, of which 4 were waited for; matrix products, arithmetic and copies ran while one was open for 0% of the time, Pallas kernels for 0%

commit v1 on v0

v1 whole, which is shorter than its diff:
```python
import jax
import jax.numpy as jnp
from jax import lax
from jax.sharding import PartitionSpec as P


def group_table(rows, req_lengths, step_group, groups):
    ends = jnp.cumsum(req_lengths)
    request = jnp.sum((rows[:, None] >= ends[None, :]).astype(jnp.int32), axis=1)
    picked = (
        request[:, None] == jnp.arange(req_lengths.shape[0], dtype=jnp.int32)[None, :]
    ).astype(jnp.int32)
    row_group = jnp.sum(picked * step_group[None, :], axis=1)
    return (row_group[:, None] == jnp.arange(groups, dtype=jnp.int32)[None, :]).astype(jnp.float32)


def scales(rows, req_lengths, step_group, table):
    onehot = group_table(rows, req_lengths, step_group, table.shape[0]).astype(jnp.bfloat16)
    high = table.astype(jnp.bfloat16)
    rest = table - high.astype(jnp.float32)
    middle = rest.astype(jnp.bfloat16)
    low = (rest - middle.astype(jnp.float32)).astype(jnp.bfloat16)
    return jnp.dot(
        jnp.concatenate([onehot] * 3, axis=1),
        jnp.concatenate([high, middle, low], axis=0),
        preferred_element_type=jnp.float32,
    )


def by_collectives(tokens, w_up, w_down, up_scale, down_scale, step_group, req_lengths):
    pre = jnp.dot(
        lax.all_gather(tokens, "fin", axis=0, tiled=True), w_up, preferred_element_type=jnp.float32
    )
    total_rows = pre.shape[0]
    half_sum = lax.psum_scatter(pre, "fout", scatter_dimension=0, tiled=True)
    half_rows = half_sum.shape[0]
    rows = lax.axis_index("fout") * half_rows + jnp.arange(half_rows, dtype=jnp.int32)
    scale_one = scales(rows, req_lengths, step_group, up_scale)
    half_hidden = jax.nn.gelu(half_sum * scale_one, approximate=True).astype(jnp.bfloat16)
    hidden = lax.all_gather(half_hidden, "fout", axis=0, tiled=True)
    summed_rows = lax.psum_scatter(
        jnp.dot(hidden, w_down, preferred_element_type=jnp.float32),
        "fin",
        scatter_dimension=0,
        tiled=True,
    )
    own_rows = total_rows // lax.axis_size("fin")
    rows = lax.axis_index("fin") * own_rows + jnp.arange(own_rows, dtype=jnp.int32)
    scale_two = scales(rows, req_lengths, step_group, down_scale)
    return (summed_rows * scale_two).astype(jnp.bfloat16)


ACROSS = [(z * 2 + y, z * 2 + 1 - y) for z in range(4) for y in range(2)]


def move_y(x):
    return lax.ppermute(x, "fin", ACROSS)


def fetch_z(x, k):
    return lax.ppermute(
        x, "fin", [((z + k) % 4 * 2 + y, z * 2 + y) for z in range(4) for y in range(2)]
    )


def send_z(x, k):
    return lax.ppermute(
        x, "fin", [(z * 2 + y, (z + k) % 4 * 2 + y) for z in range(4) for y in range(2)]
    )


def gather(tokens, width):
    own = tokens
    across = move_y(own)
    singles = [fetch_z(own[:, :width], k) for k in (1, 2, 3)]
    pair = jnp.stack([own[:, width:], across[:, width:]])
    pairs = [fetch_z(pair, k) for k in (1, 2, 3)]
    single_pairs = [move_y(x) for x in singles]
    left = jnp.concatenate([own[:, :width], *singles, across[:, :width], *single_pairs])
    right = jnp.concatenate(
        [own[:, width:], *[p[0] for p in pairs], across[:, width:], *[p[1] for p in pairs]]
    )
    return left, right


def wide(x):
    return x.astype(jnp.float32)


def scatter(over_y, over_z):
    half = jnp.bfloat16
    rows = over_y.shape[0] // 8
    b = over_y.reshape(2, 4, rows, -1)
    a = over_z.reshape(2, 4, rows, -1)
    a_moved = [send_z(a[:, k].astype(half), k) for k in (1, 2, 3)]
    b_across = move_y(b[1, 1:].astype(half))
    b_moved = [
        send_z((b[0, k] + wide(b_across[k - 1])).astype(half), k) for k in (1, 2, 3)
    ]
    a_sum = a[:, 0] + wide(a_moved[0]) + wide(a_moved[1]) + wide(a_moved[2])
    last = move_y(jnp.concatenate([b[1, 0], a_sum[1]], axis=1).astype(half))
    b_sum = b[0, 0] + wide(b_moved[0]) + wide(b_moved[1]) + wide(b_moved[2])
    return jnp.concatenate([b_sum, a_sum[0]], axis=1) + wide(last)


def by_permutes(tokens, w_up, w_down, up_scale, down_scale, step_group, req_lengths):
    place = lax.axis_index("fin")
    z, y = place // 2, place % 2
    own_rows, depth = tokens.shape

    k, j = jnp.arange(4, dtype=jnp.int32), jnp.arange(2, dtype=jnp.int32)
    block = ((z + k) % 4)[None, :] * 2 + (y ^ j)[:, None]
    rows = block.reshape(-1, 1) * own_rows + jnp.arange(own_rows, dtype=jnp.int32)[None, :]
    scale_one = scales(rows.reshape(-1), req_lengths, step_group, up_scale)
    scale_two = scales(rows[0], req_lengths, step_group, down_scale)

    width = depth * 3 // 4 // 128 * 128
    left, right = gather(tokens, width)
    pre = jnp.dot(left, w_up[:width], preferred_element_type=jnp.float32)
    pre = pre + jnp.dot(right, w_up[width:], preferred_element_type=jnp.float32)
    other = lax.ppermute(pre.astype(jnp.bfloat16), "fout", [(0, 1), (1, 0)])
    hidden = jax.nn.gelu((pre + wide(other)) * scale_one, approximate=True)
    hidden = hidden.astype(jnp.bfloat16)
    width = w_down.shape[1] * 3 // 4 // 128 * 128
    over_z = jnp.dot(hidden, w_down[:, width:], preferred_element_type=jnp.float32)
    over_y = jnp.dot(hidden, w_down[:, :width], preferred_element_type=jnp.float32)
    return (scatter(over_y, over_z) * scale_two).astype(jnp.bfloat16)


def solution(mesh):
    on_device = by_permutes if mesh.shape["fin"] == 8 else by_collectives
    return jax.shard_map(
        on_device,
        mesh=mesh,
        in_specs=(
            P(("grp", "fin"), "fout"),
            P("fout", "fin"),
            P("fin", "fout"),
            P(None, "fin"),
            P(None, "fout"),
            P("grp"),
            P("grp"),
        ),
        out_specs=P(("grp", "fin"), "fout"),
        check_vma=False,
    )
```

time: 187 us -> 91.9 us (0.49)
  waiting for transfers between devices: 145 us -> 38.4 us
  starting transfers between devices: 0.13 us -> 22.5 us
  between operations: 13.2 us -> 0.31 us
  other arithmetic: 0.53 us -> 4.42 us
  matrix products: 26.8 us -> 23.6 us
    reduce_scatter x2 -> x0, waiting for transfers between devices: 84.4 us -> none  [the longest x1 75.5 us: on_device(): lax.psum_scatter(jnp.dot(hidden, w_down, preferred_element_type=jnp.float...]
    all_gather x2 -> x0, waiting for transfers between devices: 60.2 us -> none  [the longest x1 49.2 us: on_device(): lax.all_gather(tokens, 'fin', axis=0, tiled=True)]
    ppermute x0 -> x19, waiting for transfers between devices: none -> 38.4 us  [the longest x6 17.5 us: send_z(): lax.ppermute(x, 'fin', [(z * 2 + y, (z + k) % 4 * 2 + y) for z in range(4...]
    ppermute x0 -> x19, starting transfers between devices: none -> 22.5 us  [the longest x6 8.04 us: send_z(): lax.ppermute(x, 'fin', [(z * 2 + y, (z + k) % 4 * 2 + y) for z in range(4...]
    dot_general x4 -> x6, matrix products: 26.8 us -> 23.6 us  [the longest x1 7.56 us: by_permutes(): jnp.dot(hidden, w_down[:, :width], preferred_element_type=jnp.float32)]
  transfers between devices with their start and end apart: 4 -> 19, of which waited for: 4 -> 10; matrix products, arithmetic and copies ran while one was open for 0% -> 10% of each run, Pallas kernels for 0% -> 0%
where the time goes in v1:
time: 91.9 us; the launch traced here: 91.6 us
  waiting for transfers between devices  38.4 us (42%)
  matrix products  23.6 us (26%)
  starting transfers between devices  22.5 us (24%)
  other arithmetic  4.42 us (5%)
  local copies, waits for them, and re-layouts  2.26 us (2%)
    ppermute x6, waiting for transfers between devices, send_z(): lax.ppermute(x, 'fin', [(z * 2 + y, (z + k) % 4 * 2 + y) for z in range(4...  17.5 us
    ppermute x6, waiting for transfers between devices, fetch_z(): lax.ppermute(x, 'fin', [((z + k) % 4 * 2 + y, z * 2 + y) for z in range(4...  15.4 us
    ppermute x6, starting transfers between devices, send_z(): lax.ppermute(x, 'fin', [(z * 2 + y, (z + k) % 4 * 2 + y) for z in range(4...  8.04 us
    dot_general x1, matrix products, by_permutes(): jnp.dot(hidden, w_down[:, :width], preferred_element_type=jnp.float32)  7.56 us
    ppermute x6, starting transfers between devices, fetch_z(): lax.ppermute(x, 'fin', [((z + k) % 4 * 2 + y, z * 2 + y) for z in range(4...  7.48 us
    dot_general x1, matrix products, by_permutes(): pre = jnp.dot(left, w_up[:width], preferred_element_type=jnp.float32)  7.08 us
    ppermute x6, starting transfers between devices, move_y(): return lax.ppermute(x, 'fin', ACROSS)  6.95 us
    dot_general x1, matrix products, by_permutes(): jnp.dot(hidden, w_down[:, width:], preferred_element_type=jnp.float32)  3.73 us
  transfers between devices with their start and end apart: 19, of which 10 were waited for; matrix products, arithmetic and copies ran while one was open for 10% of the time, Pallas kernels for 0%

profile of v1, /device:TPU:0, one launch (start us, length us, event | category | flops | bytes accessed | tf_op | source)
XLA Modules:
  0.0 91.6 jit_solution(11737476894643177876)
XLA Ops:
  0.0 3.0 %collective-permute-start.3 = (bf16[32,3072]{1,0:T(8,128)(2,1)}, bf16[32,3072]{1,0:T(8,128)(2,1)S(1)}, u32[]{:S(2)}, u32[]{:S(2)}) collective-permute-start(bf16[32,3072]{1,0:T(8,128)(2,1)} %param.7), channel_id=1, source_target_pairs={{0,2},{2,0},{4,6},{6,4},{8,10},{10,8},{12,14},{14,12},{1,3},{3,1},... | collective-permute-start | bytes 589832 | tf_op jit(solution)/shard_map/ppermute | solution.py:57
  3.9 3.7 %collective-permute-start = (bf16[32,2304]{1,0:T(8,128)(2,1)S(1)}, bf16[32,2304]{1,0:T(8,128)(2,1)S(1)}, u32[]{:S(2)}, u32[]{:S(2)}) collective-permute-start(bf16[32,2304]{1,0:T(8,128)(2,1)S(1)} %get-tuple-element.11), channel_id=1, source_target_pairs={{4,0},{6,2},{8,4},{10,6},{12,8},{14,10},{0,12},{2,14},{5,1},{7,3},... | collective-permute-start | bytes 442376 | tf_op jit(solution)/shard_map/ppermute | solution.py:61
  12.8 7.0 %collective-permute-done.1 = bf16[32,2304]{1,0:T(8,128)(2,1)S(1)} collective-permute-done((bf16[32,2304]{1,0:T(8,128)(2,1)S(1)}, bf16[32,2304]{1,0:T(8,128)(2,1)S(1)}, u32[]{:S(2)}, u32[]{:S(2)}) %collective-permute-start.1) | collective-permute-done | bytes 147488 | tf_op jit(solution)/shard_map/ppermute | solution.py:61
  20.3 1.6 %collective-permute-start.6 = (bf16[32,2304]{1,0:T(8,128)(2,1)S(1)}, bf16[32,2304]{1,0:T(8,128)(2,1)S(1)}, u32[]{:S(2)}, u32[]{:S(2)}) collective-permute-start(bf16[32,2304]{1,0:T(8,128)(2,1)S(1)} %collective-permute-done.2), channel_id=1, source_target_pairs={{0,2},{2,0},{4,6},{6,4},{8,10},{10,8},{12,14},{14,12},{1,3},{3,1},... | collective-permute-start | bytes 442376 | tf_op jit(solution)/shard_map/ppermute | solution.py:57
  22.0 1.4 %collective-permute-start.7 = (bf16[2,32,768]{2,1,0:T(8,128)(2,1)S(1)}, bf16[2,32,768]{2,1,0:T(8,128)(2,1)S(1)}, u32[]{:S(2)}, u32[]{:S(2)}) collective-permute-start(bf16[2,32,768]{2,1,0:T(8,128)(2,1)S(1)} %pad_maximum_fusion.1), channel_id=1, source_target_pairs={{4,0},{6,2},{8,4},{10,6},{12,8},{14,10},{0,12},{2,14},{5,1},{7,3},... | collective-permute-start | bytes 294920 | tf_op jit(solution)/shard_map/ppermute | solution.py:61
  23.4 3.4 %collective-permute-done.7 = bf16[2,32,768]{2,1,0:T(8,128)(2,1)S(1)} collective-permute-done((bf16[2,32,768]{2,1,0:T(8,128)(2,1)S(1)}, bf16[2,32,768]{2,1,0:T(8,128)(2,1)S(1)}, u32[]{:S(2)}, u32[]{:S(2)}) %collective-permute-start.7) | collective-permute-done | bytes 98336 | tf_op jit(solution)/shard_map/ppermute | solution.py:61
  26.8 1.4 %collective-permute-start.9 = (bf16[2,32,768]{2,1,0:T(8,128)(2,1)S(1)}, bf16[2,32,768]{2,1,0:T(8,128)(2,1)S(1)}, u32[]{:S(2)}, u32[]{:S(2)}) collective-permute-start(bf16[2,32,768]{2,1,0:T(8,128)(2,1)S(1)} %pad_maximum_fusion.1), channel_id=1, source_target_pairs={{12,0},{14,2},{0,4},{2,6},{4,8},{6,10},{8,12},{10,14},{13,1},{15,3... | collective-permute-start | bytes 294920 | tf_op jit(solution)/shard_map/ppermute | solution.py:61
  28.2 2.9 %collective-permute-done.8 = bf16[2,32,768]{2,1,0:T(8,128)(2,1)S(1)} collective-permute-done((bf16[2,32,768]{2,1,0:T(8,128)(2,1)S(1)}, bf16[2,32,768]{2,1,0:T(8,128)(2,1)S(1)}, u32[]{:S(2)}, u32[]{:S(2)}) %collective-permute-start.8) | collective-permute-done | bytes 98336 | tf_op jit(solution)/shard_map/ppermute | solution.py:61
  31.0 2.2 %collective-permute-done.9 = bf16[2,32,768]{2,1,0:T(8,128)(2,1)S(1)} collective-permute-done((bf16[2,32,768]{2,1,0:T(8,128)(2,1)S(1)}, bf16[2,32,768]{2,1,0:T(8,128)(2,1)S(1)}, u32[]{:S(2)}, u32[]{:S(2)}) %collective-permute-start.9) | collective-permute-done | bytes 98336 | tf_op jit(solution)/shard_map/ppermute | solution.py:61
  33.3 3.7 %fusion.6 = f32[256,3072]{1,0:T(8,128)S(1)} fusion(bf16[256,768]{1,0:T(8,128)(2,1)S(1)} %fusion.50, bf16[3072,3072]{1,0:T(8,128)(2,1)} %param.8), kind=kOutput, calls=%fused_computation.7 | convolution fusion | flops 1207959552 | bytes 8257536 | tf_op jit(solution)/shard_map/dot_general | solution.py:120
  37.1 7.1 %fusion.73 = (bf16[256,3072]{1,0:T(8,128)(2,1)S(1)}, f32[256,3072]{1,0:T(8,128)S(1)}) fusion(f32[256,3072]{1,0:T(8,128)S(1)} %fusion.6, bf16[256,2304]{1,0:T(8,128)(2,1)S(1)} %constant_dynamic-update-slice_fusion, bf16[3072,3072]{1,0:T(8,128)(2,1)} %param.8), kind=kOutput, calls=%fused_computation.128 | convolution fusion | flops 3625451520 | bytes 23199744 | tf_op jit(solution)/shard_map/dot_general | solution.py:119
  45.1 2.6 %collective-permute-done.10 = bf16[256,3072]{1,0:T(8,128)(2,1)S(1)} collective-permute-done((bf16[256,3072]{1,0:T(8,128)(2,1)S(1)}, bf16[256,3072]{1,0:T(8,128)(2,1)S(1)}, u32[]{:S(2)}, u32[]{:S(2)}) %collective-permute-start.10) | collective-permute-done | bytes 1572896 | tf_op jit(solution)/shard_map/ppermute | solution.py:121
  47.7 1.3 %fusion.18 = bf16[256,3072]{1,0:T(8,128)(2,1)S(1)} fusion(f32[256,3072]{1,0:T(8,128)S(1)} %fusion.33, f32[256,3072]{1,0:T(8,128)S(1)} %get-tuple-element.22, bf16[256,3072]{1,0:T(8,128)(2,1)S(1)} %collective-permute-done.10), kind=kLoop, calls=%fused_computation.17 | loop fusion | flops 9437184 | bytes 9437184 | tf_op jit(solution)/shard_map/convert_element_type | solution.py:123
  49.0 3.7 %fusion.4 = f32[256,768]{1,0:T(8,128)S(1)} fusion(bf16[256,3072]{1,0:T(8,128)(2,1)S(1)} %fusion.18, bf16[3072,3072]{1,0:T(8,128)(2,1)} %param.9), kind=kOutput, calls=%fused_computation.5 | convolution fusion | flops 1207959552 | bytes 7077888 | tf_op jit(solution)/shard_map/dot_general | solution.py:125
  52.7 7.6 %fusion = f32[256,2304]{1,0:T(8,128)S(1)} fusion(bf16[256,3072]{1,0:T(8,128)(2,1)S(1)} %fusion.18, bf16[3072,3072]{1,0:T(8,128)(2,1)} %param.9), kind=kOutput, calls=%fused_computation | convolution fusion | flops 3623878656 | bytes 18087936 | tf_op jit(solution)/shard_map/dot_general | solution.py:126
  60.3 1.9 %collective-permute-start.17 = (bf16[2,32,768]{2,1,0:T(8,128)(2,1)S(1)}, bf16[2,32,768]{2,1,0:T(8,128)(2,1)S(1)}, u32[]{:S(2)}, u32[]{:S(2)}) collective-permute-start(bf16[2,32,768]{2,1,0:T(8,128)(2,1)S(1)} %get-tuple-element.9), channel_id=1, source_target_pairs={{0,12},{2,14},{4,0},{6,2},{8,4},{10,6},{12,8},{14,10},{1,13},{3,15... | collective-permute-start | bytes 294920 | tf_op jit(solution)/shard_map/ppermute | solution.py:67
  63.0 1.0 %collective-permute-start.11 = (bf16[3,32,2304]{2,1,0:T(8,128)(2,1)S(1)}, bf16[3,32,2304]{2,1,0:T(8,128)(2,1)S(1)}, u32[]{:S(2)}, u32[]{:S(2)}) collective-permute-start(bf16[3,32,2304]{2,1,0:T(8,128)(2,1)S(1)} %slice_bitcast_fusion), channel_id=1, source_target_pairs={{0,2},{2,0},{4,6},{6,4},{8,10},{10,8},{12,14},{14,12},{1,3},{3,1},... | collective-permute-start | bytes 1327112 | tf_op jit(solution)/shard_map/ppermute | solution.py:57
  64.0 1.4 %collective-permute-done.17 = bf16[2,32,768]{2,1,0:T(8,128)(2,1)S(1)} collective-permute-done((bf16[2,32,768]{2,1,0:T(8,128)(2,1)S(1)}, bf16[2,32,768]{2,1,0:T(8,128)(2,1)S(1)}, u32[]{:S(2)}, u32[]{:S(2)}) %collective-permute-start.17) | collective-permute-done | bytes 98336 | tf_op jit(solution)/shard_map/ppermute | solution.py:67
  65.4 6.2 %collective-permute-done.16 = bf16[2,32,768]{2,1,0:T(8,128)(2,1)S(1)} collective-permute-done((bf16[2,32,768]{2,1,0:T(8,128)(2,1)S(1)}, bf16[2,32,768]{2,1,0:T(8,128)(2,1)S(1)}, u32[]{:S(2)}, u32[]{:S(2)}) %collective-permute-start.16) | collective-permute-done | bytes 98336 | tf_op jit(solution)/shard_map/ppermute | solution.py:67
  72.0 3.0 %collective-permute-done.11 = bf16[3,32,2304]{2,1,0:T(8,128)(2,1)S(1)} collective-permute-done((bf16[3,32,2304]{2,1,0:T(8,128)(2,1)S(1)}, bf16[3,32,2304]{2,1,0:T(8,128)(2,1)S(1)}, u32[]{:S(2)}, u32[]{:S(2)}) %collective-permute-start.11) | collective-permute-done | bytes 442400 | tf_op jit(solution)/shard_map/ppermute | solution.py:57
  75.1 4.4 %collective-permute-start.14 = (bf16[32,2304]{1,0:T(8,128)(2,1)S(1)}, bf16[32,2304]{1,0:T(8,128)(2,1)S(1)}, u32[]{:S(2)}, u32[]{:S(2)}) collective-permute-start(bf16[32,2304]{1,0:T(8,128)(2,1)S(1)} %get-tuple-element.6), channel_id=1, source_target_pairs={{0,12},{2,14},{4,0},{6,2},{8,4},{10,6},{12,8},{14,10},{1,13},{3,15... | collective-permute-start | bytes 442376 | tf_op jit(solution)/shard_map/ppermute | solution.py:67
  79.5 1.1 %collective-permute-start.13 = (bf16[32,2304]{1,0:T(8,128)(2,1)S(1)}, bf16[32,2304]{1,0:T(8,128)(2,1)S(1)}, u32[]{:S(2)}, u32[]{:S(2)}) collective-permute-start(bf16[32,2304]{1,0:T(8,128)(2,1)S(1)} %get-tuple-element.7), channel_id=1, source_target_pairs={{0,8},{2,10},{4,12},{6,14},{8,0},{10,2},{12,4},{14,6},{1,9},{3,11}... | collective-permute-start | bytes 442376 | tf_op jit(solution)/shard_map/ppermute | solution.py:67
  80.6 4.3 %collective-permute-done.14 = bf16[32,2304]{1,0:T(8,128)(2,1)S(1)} collective-permute-done((bf16[32,2304]{1,0:T(8,128)(2,1)S(1)}, bf16[32,2304]{1,0:T(8,128)(2,1)S(1)}, u32[]{:S(2)}, u32[]{:S(2)}) %collective-permute-start.14) | collective-permute-done | bytes 147488 | tf_op jit(solution)/shard_map/ppermute | solution.py:67
  84.9 5.6 %collective-permute-done.13 = bf16[32,2304]{1,0:T(8,128)(2,1)S(1)} collective-permute-done((bf16[32,2304]{1,0:T(8,128)(2,1)S(1)}, bf16[32,2304]{1,0:T(8,128)(2,1)S(1)}, u32[]{:S(2)}, u32[]{:S(2)}) %collective-permute-start.13) | collective-permute-done | bytes 147488 | tf_op jit(solution)/shard_map/ppermute | solution.py:67
  (69 shorter events, 10.0 us)
Async XLA Ops:
  0.0 21.9 %collective-permute-start.3 = (bf16[32,3072]{1,0:T(8,128)(2,1)}, bf16[32,3072]{1,0:T(8,128)(2,1)S(1)}, u32[]{:S(2)}, u32[]{:S(2)}) collective-permute-start(bf16[32,3072]{1,0:T(8,128)(2,1)} %param.7), channel_id=1, source_target_pairs={{0,2},{2,0},{4,6},{6,4},{8,10},{10,8},{12,14},{14,12},{1,3},{3,1},... | collective-permute-start | bytes 589832 | tf_op jit(solution)/shard_map/ppermute | solution.py:57
  3.9 8.3 %collective-permute-start = (bf16[32,2304]{1,0:T(8,128)(2,1)S(1)}, bf16[32,2304]{1,0:T(8,128)(2,1)S(1)}, u32[]{:S(2)}, u32[]{:S(2)}) collective-permute-start(bf16[32,2304]{1,0:T(8,128)(2,1)S(1)} %get-tuple-element.11), channel_id=1, source_target_pairs={{4,0},{6,2},{8,4},{10,6},{12,8},{14,10},{0,12},{2,14},{5,1},{7,3},... | collective-permute-start | bytes 442376 | tf_op jit(solution)/shard_map/ppermute | solution.py:61
  7.6 12.2 %collective-permute-start.1 = (bf16[32,2304]{1,0:T(8,128)(2,1)S(1)}, bf16[32,2304]{1,0:T(8,128)(2,1)S(1)}, u32[]{:S(2)}, u32[]{:S(2)}) collective-permute-start(bf16[32,2304]{1,0:T(8,128)(2,1)S(1)} %get-tuple-element.11), channel_id=1, source_target_pairs={{8,0},{10,2},{12,4},{14,6},{0,8},{2,10},{4,12},{6,14},{9,1},{11,3}... | collective-permute-start | bytes 442376 | tf_op jit(solution)/shard_map/ppermute | solution.py:61
  7.6 12.7 %collective-permute-start.2 = (bf16[32,2304]{1,0:T(8,128)(2,1)S(1)}, bf16[32,2304]{1,0:T(8,128)(2,1)S(1)}, u32[]{:S(2)}, u32[]{:S(2)}) collective-permute-start(bf16[32,2304]{1,0:T(8,128)(2,1)S(1)} %get-tuple-element.11), channel_id=1, source_target_pairs={{12,0},{14,2},{0,4},{2,6},{4,8},{6,10},{8,12},{10,14},{13,1},{15,3... | collective-permute-start | bytes 442376 | tf_op jit(solution)/shard_map/ppermute | solution.py:61
  12.2 24.7 %collective-permute-start.4 = (bf16[32,2304]{1,0:T(8,128)(2,1)S(1)}, bf16[32,2304]{1,0:T(8,128)(2,1)S(1)}, u32[]{:S(2)}, u32[]{:S(2)}) collective-permute-start(bf16[32,2304]{1,0:T(8,128)(2,1)S(1)} %collective-permute-done), channel_id=1, source_target_pairs={{0,2},{2,0},{4,6},{6,4},{8,10},{10,8},{12,14},{14,12},{1,3},{3,1},... | collective-permute-start | bytes 442376 | tf_op jit(solution)/shard_map/ppermute | solution.py:57
  19.8 17.2 %collective-permute-start.5 = (bf16[32,2304]{1,0:T(8,128)(2,1)S(1)}, bf16[32,2304]{1,0:T(8,128)(2,1)S(1)}, u32[]{:S(2)}, u32[]{:S(2)}) collective-permute-start(bf16[32,2304]{1,0:T(8,128)(2,1)S(1)} %collective-permute-done.1), channel_id=1, source_target_pairs={{0,2},{2,0},{4,6},{6,4},{8,10},{10,8},{12,14},{14,12},{1,3},{3,1},... | collective-permute-start | bytes 442376 | tf_op jit(solution)/shard_map/ppermute | solution.py:57
  20.3 16.7 %collective-permute-start.6 = (bf16[32,2304]{1,0:T(8,128)(2,1)S(1)}, bf16[32,2304]{1,0:T(8,128)(2,1)S(1)}, u32[]{:S(2)}, u32[]{:S(2)}) collective-permute-start(bf16[32,2304]{1,0:T(8,128)(2,1)S(1)} %collective-permute-done.2), channel_id=1, source_target_pairs={{0,2},{2,0},{4,6},{6,4},{8,10},{10,8},{12,14},{14,12},{1,3},{3,1},... | collective-permute-start | bytes 442376 | tf_op jit(solution)/shard_map/ppermute | solution.py:57
  22.0 4.8 %collective-permute-start.7 = (bf16[2,32,768]{2,1,0:T(8,128)(2,1)S(1)}, bf16[2,32,768]{2,1,0:T(8,128)(2,1)S(1)}, u32[]{:S(2)}, u32[]{:S(2)}) collective-permute-start(bf16[2,32,768]{2,1,0:T(8,128)(2,1)S(1)} %pad_maximum_fusion.1), channel_id=1, source_target_pairs={{4,0},{6,2},{8,4},{10,6},{12,8},{14,10},{0,12},{2,14},{5,1},{7,3},... | collective-permute-start | bytes 294920 | tf_op jit(solution)/shard_map/ppermute | solution.py:61
  23.4 7.6 %collective-permute-start.8 = (bf16[2,32,768]{2,1,0:T(8,128)(2,1)S(1)}, bf16[2,32,768]{2,1,0:T(8,128)(2,1)S(1)}, u32[]{:S(2)}, u32[]{:S(2)}) collective-permute-start(bf16[2,32,768]{2,1,0:T(8,128)(2,1)S(1)} %pad_maximum_fusion.1), channel_id=1, source_target_pairs={{8,0},{10,2},{12,4},{14,6},{0,8},{2,10},{4,12},{6,14},{9,1},{11,3}... | collective-permute-start | bytes 294920 | tf_op jit(solution)/shard_map/ppermute | solution.py:61
  26.8 6.4 %collective-permute-start.9 = (bf16[2,32,768]{2,1,0:T(8,128)(2,1)S(1)}, bf16[2,32,768]{2,1,0:T(8,128)(2,1)S(1)}, u32[]{:S(2)}, u32[]{:S(2)}) collective-permute-start(bf16[2,32,768]{2,1,0:T(8,128)(2,1)S(1)} %pad_maximum_fusion.1), channel_id=1, source_target_pairs={{12,0},{14,2},{0,4},{2,6},{4,8},{6,10},{8,12},{10,14},{13,1},{15,3... | collective-permute-start | bytes 294920 | tf_op jit(solution)/shard_map/ppermute | solution.py:61
  37.1 7.2 %copy-start = (f32[8,3072]{1,0:T(8,128)S(1)}, f32[8,3072]{1,0:T(8,128)}, u32[]{:S(2)}) copy-start(f32[8,3072]{1,0:T(8,128)} %param.10) | copy-start | bytes 294916
  44.2 0.9 copy-start.1
  44.2 3.5 %collective-permute-start.10 = (bf16[256,3072]{1,0:T(8,128)(2,1)S(1)}, bf16[256,3072]{1,0:T(8,128)(2,1)S(1)}, u32[]{:S(2)}, u32[]{:S(2)}) collective-permute-start(bf16[256,3072]{1,0:T(8,128)(2,1)S(1)} %get-tuple-element.21), channel_id=1, source_target_pairs={{0,1},{1,0},{2,3},{3,2},{4,5},{5,4},{6,7},{7,6},{8,9},{9,8},{10,11... | collective-permute-start | bytes 4718600 | tf_op jit(solution)/shard_map/ppermute | solution.py:121
  60.3 5.1 %collective-permute-start.17 = (bf16[2,32,768]{2,1,0:T(8,128)(2,1)S(1)}, bf16[2,32,768]{2,1,0:T(8,128)(2,1)S(1)}, u32[]{:S(2)}, u32[]{:S(2)}) collective-permute-start(bf16[2,32,768]{2,1,0:T(8,128)(2,1)S(1)} %get-tuple-element.9), channel_id=1, source_target_pairs={{0,12},{2,14},{4,0},{6,2},{8,4},{10,6},{12,8},{14,10},{1,13},{3,15... | collective-permute-start | bytes 294920 | tf_op jit(solution)/shard_map/ppermute | solution.py:67
  62.2 9.4 %collective-permute-start.16 = (bf16[2,32,768]{2,1,0:T(8,128)(2,1)S(1)}, bf16[2,32,768]{2,1,0:T(8,128)(2,1)S(1)}, u32[]{:S(2)}, u32[]{:S(2)}) collective-permute-start(bf16[2,32,768]{2,1,0:T(8,128)(2,1)S(1)} %get-tuple-element.10), channel_id=1, source_target_pairs={{0,8},{2,10},{4,12},{6,14},{8,0},{10,2},{12,4},{14,6},{1,9},{3,11}... | collective-permute-start | bytes 294920 | tf_op jit(solution)/shard_map/ppermute | solution.py:67
  62.2 9.4 %collective-permute-start.15 = (bf16[2,32,768]{2,1,0:T(8,128)(2,1)S(1)}, bf16[2,32,768]{2,1,0:T(8,128)(2,1)S(1)}, u32[]{:S(2)}, u32[]{:S(2)}) collective-permute-start(bf16[2,32,768]{2,1,0:T(8,128)(2,1)S(1)} %get-tuple-element.8), channel_id=1, source_target_pairs={{0,4},{2,6},{4,8},{6,10},{8,12},{10,14},{12,0},{14,2},{1,5},{3,7},... | collective-permute-start | bytes 294920 | tf_op jit(solution)/shard_map/ppermute | solution.py:67
  63.0 12.0 %collective-permute-start.11 = (bf16[3,32,2304]{2,1,0:T(8,128)(2,1)S(1)}, bf16[3,32,2304]{2,1,0:T(8,128)(2,1)S(1)}, u32[]{:S(2)}, u32[]{:S(2)}) collective-permute-start(bf16[3,32,2304]{2,1,0:T(8,128)(2,1)S(1)} %slice_bitcast_fusion), channel_id=1, source_target_pairs={{0,2},{2,0},{4,6},{6,4},{8,10},{10,8},{12,14},{14,12},{1,3},{3,1},... | collective-permute-start | bytes 1327112 | tf_op jit(solution)/shard_map/ppermute | solution.py:57
  71.7 18.9 %collective-permute-start.18 = (bf16[32,3072]{1,0:T(8,128)(2,1)S(1)}, bf16[32,3072]{1,0:T(8,128)(2,1)S(1)}, u32[]{:S(2)}, u32[]{:S(2)}) collective-permute-start(bf16[32,3072]{1,0:T(8,128)(2,1)S(1)} %pad_maximum_fusion), channel_id=1, source_target_pairs={{0,2},{2,0},{4,6},{6,4},{8,10},{10,8},{12,14},{14,12},{1,3},{3,1},... | collective-permute-start | bytes 589832 | tf_op jit(solution)/shard_map/ppermute | solution.py:57
  75.1 9.8 %collective-permute-start.14 = (bf16[32,2304]{1,0:T(8,128)(2,1)S(1)}, bf16[32,2304]{1,0:T(8,128)(2,1)S(1)}, u32[]{:S(2)}, u32[]{:S(2)}) collective-permute-start(bf16[32,2304]{1,0:T(8,128)(2,1)S(1)} %get-tuple-element.6), channel_id=1, source_target_pairs={{0,12},{2,14},{4,0},{6,2},{8,4},{10,6},{12,8},{14,10},{1,13},{3,15... | collective-permute-start | bytes 442376 | tf_op jit(solution)/shard_map/ppermute | solution.py:67
  79.5 11.1 %collective-permute-start.13 = (bf16[32,2304]{1,0:T(8,128)(2,1)S(1)}, bf16[32,2304]{1,0:T(8,128)(2,1)S(1)}, u32[]{:S(2)}, u32[]{:S(2)}) collective-permute-start(bf16[32,2304]{1,0:T(8,128)(2,1)S(1)} %get-tuple-element.7), channel_id=1, source_target_pairs={{0,8},{2,10},{4,12},{6,14},{8,0},{10,2},{12,4},{14,6},{1,9},{3,11}... | collective-permute-start | bytes 442376 | tf_op jit(solution)/shard_map/ppermute | solution.py:67
  80.6 9.9 %collective-permute-start.12 = (bf16[32,2304]{1,0:T(8,128)(2,1)S(1)}, bf16[32,2304]{1,0:T(8,128)(2,1)S(1)}, u32[]{:S(2)}, u32[]{:S(2)}) collective-permute-start(bf16[32,2304]{1,0:T(8,128)(2,1)S(1)} %get-tuple-element.5), channel_id=1, source_target_pairs={{0,4},{2,6},{4,8},{6,10},{8,12},{10,14},{12,0},{14,2},{1,5},{3,7},... | collective-permute-start | bytes 442376 | tf_op jit(solution)/shard_map/ppermute | solution.py:67

commit v2 on v1

v2 whole, which is shorter than its diff:
```python
import math
import jax
import jax.numpy as jnp
from jax import lax
from jax.experimental import pallas as pl
from jax.experimental.pallas import tpu as pltpu
from jax.sharding import PartitionSpec as P


def group_table(rows, req_lengths, step_group, groups):
    place = jnp.arange(req_lengths.shape[0], dtype=jnp.int32)
    before = place[None, :] < place[:, None]
    starts = jnp.sum(jnp.where(before, req_lengths[None, :], 0), axis=1)
    ends = starts + req_lengths
    held = (rows[:, None] >= starts[None, :]) & (rows[:, None] < ends[None, :])
    row_group = jnp.sum(jnp.where(held, step_group[None, :], 0), axis=1)
    return (row_group[:, None] == jnp.arange(groups, dtype=jnp.int32)[None, :]).astype(jnp.float32)


def scales(rows, req_lengths, step_group, table):
    onehot = group_table(rows, req_lengths, step_group, table.shape[0]).astype(jnp.bfloat16)
    high = lax.reduce_precision(table, 8, 7)
    middle = lax.reduce_precision(table - high, 8, 7)
    low = table - high - middle
    return jnp.dot(
        jnp.concatenate([onehot] * 3, axis=1),
        jnp.concatenate([high, middle, low], axis=0).astype(jnp.bfloat16),
        preferred_element_type=jnp.float32,
    )


def by_collectives(tokens, w_up, w_down, up_scale, down_scale, step_group, req_lengths):
    pre = jnp.dot(
        lax.all_gather(tokens, "fin", axis=0, tiled=True), w_up, preferred_element_type=jnp.float32
    )
    total_rows = pre.shape[0]
    half_sum = lax.psum_scatter(pre, "fout", scatter_dimension=0, tiled=True)
    half_rows = half_sum.shape[0]
    rows = lax.axis_index("fout") * half_rows + jnp.arange(half_rows, dtype=jnp.int32)
    scale_one = scales(rows, req_lengths, step_group, up_scale)
    half_hidden = jax.nn.gelu(half_sum * scale_one, approximate=True).astype(jnp.bfloat16)
    hidden = lax.all_gather(half_hidden, "fout", axis=0, tiled=True)
    summed_rows = lax.psum_scatter(
        jnp.dot(hidden, w_down, preferred_element_type=jnp.float32),
        "fin",
        scatter_dimension=0,
        tiled=True,
    )
    own_rows = total_rows // lax.axis_size("fin")
    rows = lax.axis_index("fin") * own_rows + jnp.arange(own_rows, dtype=jnp.int32)
    scale_two = scales(rows, req_lengths, step_group, down_scale)
    return (summed_rows * scale_two).astype(jnp.bfloat16)


ACROSS = [(z * 2 + y, z * 2 + 1 - y) for z in range(4) for y in range(2)]


def move_y(x):
    return lax.ppermute(x, "fin", ACROSS)


def fetch_z(x, k):
    return lax.ppermute(
        x, "fin", [((z + k) % 4 * 2 + y, z * 2 + y) for z in range(4) for y in range(2)]
    )


def send_z(x, k):
    return lax.ppermute(
        x, "fin", [(z * 2 + y, (z + k) % 4 * 2 + y) for z in range(4) for y in range(2)]
    )


def wide(x):
    return x.astype(jnp.float32)


VMEM = pl.BlockSpec(memory_space=pltpu.VMEM)
HBM = pl.BlockSpec(memory_space=pltpu.HBM)
ANY = pl.BlockSpec(memory_space=pl.ANY)
TILE = 512
AHEAD = 3


def params(mib):
    return pltpu.CompilerParams(vmem_limit_bytes=mib * 2**20)


def dot(a, b):
    return jnp.dot(a, b, preferred_element_type=jnp.float32)


def load_kernel(*refs):
    w_ref, out_ref, sems = refs[0], refs[-2], refs[-1]
    step = out_ref.shape[0] // sems.shape[0]
    moving = [
        pltpu.make_async_copy(
            w_ref.at[pl.ds(i * step, step)], out_ref.at[pl.ds(i * step, step)], sems.at[i]
        )
        for i in range(sems.shape[0])
    ]
    for c in moving:
        c.start()
    for c in moving:
        c.wait()


def load(w, after):
    return pl.pallas_call(
        load_kernel,
        in_specs=[HBM] + [ANY] * len(after),
        out_specs=VMEM,
        out_shape=pltpu.VMEM(w.shape, w.dtype),
        scratch_shapes=[pltpu.SemaphoreType.DMA((4,))],
        compiler_params=params(2),
        cost_estimate=pl.CostEstimate(flops=0, bytes_accessed=4 * w.size, transcendentals=0),
    )(w, *after)


def up_kernel(start, x_ref, w_ref, out_ref):
    for lo in range(0, out_ref.shape[1], TILE):
        at = slice(start + lo, start + lo + TILE)
        out_ref[:, lo : lo + TILE] = dot(x_ref[...], w_ref[:, at])


def up(x, w, start, count):
    rows = x.shape[0]
    return pl.pallas_call(
        lambda *refs: up_kernel(start, *refs),
        in_specs=[VMEM] * 2,
        out_specs=VMEM,
        out_shape=jax.ShapeDtypeStruct((rows, count), jnp.float32),
        compiler_params=params(2),
        cost_estimate=pl.CostEstimate(
            flops=2 * rows * w.shape[0] * count, bytes_accessed=4 * rows * count, transcendentals=0
        ),
    )(x, w)


def tiles(w_ref, first_row, first_column, held_ref, sems):
    count, rows, width = held_ref.shape
    moving = [
        pltpu.make_async_copy(
            w_ref.at[pl.ds(first_row, rows), pl.ds(first_column + i * width, width)],
            held_ref.at[i],
            sems.at[i],
        )
        for i in range(count)
    ]
    for c in moving[:AHEAD]:
        c.start()
    return moving


def arrive(moving, i):
    moving[i].wait()
    if i + AHEAD < len(moving):
        moving[i + AHEAD].start()


def activate(own_ref, other_ref, scale_ref, hidden_ref):
    for lo in range(0, hidden_ref.shape[1], TILE):
        at = slice(lo, lo + TILE)
        v = (own_ref[:, at] + other_ref[:, at]) * scale_ref[:, at]
        inner = math.sqrt(2 / math.pi) * (v + 0.044715 * (v * v * v))
        hidden_ref[:, at] = (0.5 * v * (1 + jnp.tanh(inner))).astype(hidden_ref.dtype)


def down_first_kernel(own_ref, other_ref, scale_ref, w_ref, out_ref, hidden_ref, held_ref, sems):
    moving = tiles(w_ref, 0, 0, held_ref, sems)
    activate(own_ref, other_ref, scale_ref, hidden_ref)
    width = held_ref.shape[2]
    for i in range(len(moving)):
        arrive(moving, i)
        out_ref[:, i * width : (i + 1) * width] = dot(hidden_ref[...], held_ref[i])


def held(rows, width, tile):
    count = width // tile
    return [pltpu.VMEM((count, rows, tile), jnp.bfloat16), pltpu.SemaphoreType.DMA((count,))]


def cost(rows, count, width):
    return pl.CostEstimate(
        flops=2 * rows * count * width, bytes_accessed=2 * count * width, transcendentals=rows * count
    )


def down_first(own, other, scale, w):
    rows, count = own.shape
    width = w.shape[1]
    return pl.pallas_call(
        down_first_kernel,
        in_specs=[VMEM] * 3 + [HBM],
        out_specs=VMEM,
        out_shape=jax.ShapeDtypeStruct((rows, width), jnp.float32),
        scratch_shapes=[pltpu.VMEM((rows, count), jnp.bfloat16)] + held(count, width, TILE),
        compiler_params=params(13),
        cost_estimate=cost(rows, count, width),
    )(own, other, scale, w)


def over_z_kernel(
    own_ref, other_ref, scale_ref, w_ref, sum_ref,
    kept_ref, one_ref, two_ref, three_ref, hidden_ref, held_ref, sems,
):
    first_column = w_ref.shape[1] - kept_ref.shape[2]
    moving = tiles(w_ref, w_ref.shape[0] - own_ref.shape[1], first_column, held_ref, sems)
    activate(own_ref, other_ref, scale_ref, hidden_ref)
    rows = kept_ref.shape[1]
    step = held_ref.shape[2]
    for i in range(len(moving)):
        at = slice(first_column + i * step, first_column + (i + 1) * step)
        out = slice(i * step, (i + 1) * step)
        arrive(moving, i)
        terms = sum_ref[:, at] + dot(hidden_ref[...], held_ref[i])
        for j in range(2):
            base = j * 4 * rows
            kept_ref[j, :, out] = terms[base : base + rows]
            for k, ref in enumerate((one_ref, two_ref, three_ref)):
                low = base + (k + 1) * rows
                ref[j, :, out] = terms[low : low + rows].astype(jnp.bfloat16)


def over_z_terms(own, other, scale, w, total, width):
    rows, count = own.shape
    blocks = (2, rows // 8, width)
    moved = jax.ShapeDtypeStruct(blocks, jnp.bfloat16)
    return pl.pallas_call(
        over_z_kernel,
        in_specs=[VMEM] * 3 + [HBM, VMEM],
        out_specs=[VMEM] * 5,
        out_shape=[
            jax.ShapeDtypeStruct(blocks, jnp.float32),
            moved,
            moved,
            moved,
            jax.ShapeDtypeStruct((rows, count), jnp.bfloat16),
        ],
        scratch_shapes=held(count, width, width // 2),
        compiler_params=params(6),
        cost_estimate=cost(rows, count, width),
    )(own, other, scale, w, total)


def over_y_kernel(hidden_ref, w_ref, sum_ref, *out):
    kept, crossing, held_ref, sems = out[:4], out[4:8], out[8], out[9]
    moving = tiles(w_ref, w_ref.shape[0] - hidden_ref.shape[1], 0, held_ref, sems)
    rows = kept[0].shape[0]
    step = held_ref.shape[2]
    for i in range(len(moving)):
        at = slice(i * step, (i + 1) * step)
        arrive(moving, i)
        terms = sum_ref[:, at] + dot(hidden_ref[...], held_ref[i])
        for k in range(4):
            low = (4 + k) * rows
            kept[k][:, at] = terms[k * rows : (k + 1) * rows]
            crossing[k][:, at] = terms[low : low + rows].astype(jnp.bfloat16)


def over_y_terms(hidden, w, total, width):
    rows, count = hidden.shape
    block = (rows // 8, width)
    return pl.pallas_call(
        over_y_kernel,
        in_specs=[VMEM, HBM, VMEM],
        out_specs=[VMEM] * 8,
        out_shape=[jax.ShapeDtypeStruct(block, jnp.float32)] * 4
        + [jax.ShapeDtypeStruct(block, jnp.bfloat16)] * 4,
        scratch_shapes=held(count, width, width // 2),
        compiler_params=params(10),
        cost_estimate=cost(rows, count, width),
    )(hidden, w, total)


def swap_cores(x):
    return lax.ppermute(x, "fout", [(0, 1), (1, 0)])


def by_permutes(tokens, w_up, w_down, up_scale, down_scale, step_group, req_lengths):
    place = lax.axis_index("fin")
    z, y = place // 2, place % 2
    own_rows, depth = tokens.shape
    half = jnp.bfloat16

    k, j = jnp.arange(4, dtype=jnp.int32), jnp.arange(2, dtype=jnp.int32)
    block = ((z + k) % 4)[None, :] * 2 + (y ^ j)[:, None]
    rows = block.reshape(-1, 1) * own_rows + jnp.arange(own_rows, dtype=jnp.int32)[None, :]
    scale_one = scales(rows.reshape(-1), req_lengths, step_group, up_scale)
    scale_two = scales(rows[0], req_lengths, step_group, down_scale)

    w_up = pltpu.with_memory_space_constraint(w_up, pltpu.HBM)
    w_down = pltpu.with_memory_space_constraint(w_down, pltpu.HBM)
    across = move_y(tokens)
    singles = [fetch_z(tokens, k) for k in (1, 2, 3)]
    up_held = load(w_up, singles)
    single_pairs = [move_y(x) for x in singles]
    full = jnp.concatenate([tokens, *singles, across, *single_pairs])

    count = w_up.shape[1] // 2
    pre = [up(full, up_held, i * count, count) for i in range(2)]
    other = [swap_cores(p) for p in pre]
    width = w_down.shape[1] * 3 // 4 // 128 * 128
    total = down_first(pre[0], other[0], scale_one[:, :count], w_down)
    a_kept, *a_sent, hidden = over_z_terms(
        pre[1], other[1], scale_one[:, count:], w_down, total, w_down.shape[1] - width
    )
    b_terms = over_y_terms(hidden, w_down, total, width)
    b_kept, b_last, b_sent = b_terms[:4], b_terms[4], b_terms[5:]

    a_moved = [send_z(x, k + 1) for k, x in enumerate(a_sent)]
    b_across = [move_y(x) for x in b_sent]
    b_moved = [send_z((b_kept[k] + wide(b_across[k - 1])).astype(half), k) for k in (1, 2, 3)]
    a_sum = a_kept + wide(a_moved[0]) + wide(a_moved[1]) + wide(a_moved[2])
    last = move_y(jnp.concatenate([b_last, a_sum[1].astype(half)], axis=1))
    b_sum = b_kept[0] + wide(b_moved[0]) + wide(b_moved[1]) + wide(b_moved[2])
    summed = jnp.concatenate([b_sum, a_sum[0]], axis=1) + wide(last)
    return (summed * scale_two).astype(half)


def solution(mesh):
    on_device = by_permutes if mesh.shape["fin"] == 8 else by_collectives
    return jax.shard_map(
        on_device,
        mesh=mesh,
        in_specs=(
            P(("grp", "fin"), "fout"),
            P("fout", "fin"),
            P("fin", "fout"),
            P(None, "fin"),
            P(None, "fout"),
            P("grp"),
            P("grp"),
        ),
        out_specs=P(("grp", "fin"), "fout"),
        check_vma=False,
    )
```

time: 91.9 us -> 74.9 us (0.82)
  Pallas kernels: 0 us -> 23.6 us
  matrix products: 23.6 us -> 0.85 us
  waiting for transfers between devices: 38.4 us -> 17.1 us
  starting transfers between devices: 22.5 us -> 26.3 us
    pallas_call x0 -> x6, Pallas kernels: none -> 23.6 us  [the longest x1 6.5 us: load(): pl.pallas_call(load_kernel, in_specs=[HBM] + [ANY] * len(after), out_spec...]
    dot_general x4 -> x0, matrix products: 22.1 us -> none  [the longest x1 7.56 us: by_permutes(): jnp.dot(hidden, w_down[:, :width], preferred_element_type=jnp.float32)]
    ppermute x6, waiting for transfers between devices: 17.5 us -> 4.65 us  [send_z(): lax.ppermute(x, 'fin', [(z * 2 + y, (z + k) % 4 * 2 + y) for z in range(4...]
    ppermute x6 -> x3, waiting for transfers between devices: 15.4 us -> 4.19 us  [fetch_z(): lax.ppermute(x, 'fin', [((z + k) % 4 * 2 + y, z * 2 + y) for z in range(4...]
    ppermute x6 -> x8, waiting for transfers between devices: 3.02 us -> 8.27 us  [move_y(): return lax.ppermute(x, 'fin', ACROSS)]
    ppermute x1 -> x2, waiting for transfers between devices: 2.57 us -> 0.01 us  [swap_cores(): return lax.ppermute(x, 'fout', [(0, 1), (1, 0)])]
    ppermute x6, starting transfers between devices: 8.04 us -> 10.4 us  [send_z(): lax.ppermute(x, 'fin', [(z * 2 + y, (z + k) % 4 * 2 + y) for z in range(4...]
    ppermute x6 -> x8, starting transfers between devices: 6.95 us -> 8.3 us  [move_y(): return lax.ppermute(x, 'fin', ACROSS)]
  transfers between devices with their start and end apart: 19 -> 19, of which waited for: 10 -> 7; matrix products, arithmetic and copies ran while one was open for 10% -> 9% of each run, Pallas kernels for 0% -> 25%
where the time goes in v2:
time: 74.9 us; the launch traced here: 74.7 us
  starting transfers between devices  26.3 us (35%)
  Pallas kernels  23.6 us (32%)
  waiting for transfers between devices  17.1 us (23%)
  other arithmetic  5.06 us (7%)
  local copies, waits for them, and re-layouts  1.47 us (2%)
  matrix products  0.85 us (1%)
    ppermute x6, starting transfers between devices, send_z(): lax.ppermute(x, 'fin', [(z * 2 + y, (z + k) % 4 * 2 + y) for z in range(4...  10.4 us
    ppermute x8, starting transfers between devices, move_y(): return lax.ppermute(x, 'fin', ACROSS)  8.3 us
    ppermute x8, waiting for transfers between devices, move_y(): return lax.ppermute(x, 'fin', ACROSS)  8.27 us
    ppermute x3, starting transfers between devices, fetch_z(): lax.ppermute(x, 'fin', [((z + k) % 4 * 2 + y, z * 2 + y) for z in range(4...  6.96 us
    pallas_call x1, Pallas kernels, load(): pl.pallas_call(load_kernel, in_specs=[HBM] + [ANY] * len(after), out_spec...  6.5 us
    pallas_call x2, Pallas kernels, up(): pl.pallas_call(lambda *refs: up_kernel(start, *refs), in_specs=[VMEM] * 2...  5.32 us
    pallas_call x1, Pallas kernels, down_first(): pl.pallas_call(down_first_kernel, in_specs=[VMEM] * 3 + [HBM], out_specs=...  4.9 us
    ppermute x6, waiting for transfers between devices, send_z(): lax.ppermute(x, 'fin', [(z * 2 + y, (z + k) % 4 * 2 + y) for z in range(4...  4.65 us
  transfers between devices with their start and end apart: 19, of which 7 were waited for; matrix products, arithmetic and copies ran while one was open for 9% of the time, Pallas kernels for 25%

profile of v2, /device:TPU:0, one launch (start us, length us, event | category | flops | bytes accessed | tf_op | source)
XLA Modules:
  0.0 74.7 jit_solution(15722592897597746055)
XLA Ops:
  0.0 3.0 %collective-permute-start.2 = (bf16[32,3072]{1,0:T(8,128)(2,1)}, bf16[32,3072]{1,0:T(8,128)(2,1)S(1)}, u32[]{:S(2)}, u32[]{:S(2)}) collective-permute-start(bf16[32,3072]{1,0:T(8,128)(2,1)} %param.7), channel_id=1, source_target_pairs={{12,0},{14,2},{0,4},{2,6},{4,8},{6,10},{8,12},{10,14},{13,1},{15,3... | collective-permute-start | bytes 589832 | tf_op jit(solution)/shard_map/ppermute | solution.py:63
  3.0 2.6 %collective-permute-start.1 = (bf16[32,3072]{1,0:T(8,128)(2,1)}, bf16[32,3072]{1,0:T(8,128)(2,1)S(1)}, u32[]{:S(2)}, u32[]{:S(2)}) collective-permute-start(bf16[32,3072]{1,0:T(8,128)(2,1)} %param.7), channel_id=1, source_target_pairs={{8,0},{10,2},{12,4},{14,6},{0,8},{2,10},{4,12},{6,14},{9,1},{11,3}... | collective-permute-start | bytes 589832 | tf_op jit(solution)/shard_map/ppermute | solution.py:63
  5.6 1.3 %collective-permute-start = (bf16[32,3072]{1,0:T(8,128)(2,1)}, bf16[32,3072]{1,0:T(8,128)(2,1)S(1)}, u32[]{:S(2)}, u32[]{:S(2)}) collective-permute-start(bf16[32,3072]{1,0:T(8,128)(2,1)} %param.7), channel_id=1, source_target_pairs={{4,0},{6,2},{8,4},{10,6},{12,8},{14,10},{0,12},{2,14},{5,1},{7,3},... | collective-permute-start | bytes 589832 | tf_op jit(solution)/shard_map/ppermute | solution.py:63
  7.0 1.5 %collective-permute-start.3 = (bf16[32,3072]{1,0:T(8,128)(2,1)}, bf16[32,3072]{1,0:T(8,128)(2,1)S(1)}, u32[]{:S(2)}, u32[]{:S(2)}) collective-permute-start(bf16[32,3072]{1,0:T(8,128)(2,1)} %param.7), channel_id=1, source_target_pairs={{0,2},{2,0},{4,6},{6,4},{8,10},{10,8},{12,14},{14,12},{1,3},{3,1},... | collective-permute-start | bytes 589832 | tf_op jit(solution)/shard_map/ppermute | solution.py:59
  14.5 4.2 %collective-permute-done.1.refs_2_ = bf16[32,3072]{1,0:T(8,128)(2,1)S(1)} collective-permute-done((bf16[32,3072]{1,0:T(8,128)(2,1)}, bf16[32,3072]{1,0:T(8,128)(2,1)S(1)}, u32[]{:S(2)}, u32[]{:S(2)}) %collective-permute-start.1) | collective-permute-done | bytes 196640 | tf_op jit(solution)/shard_map/ppermute | solution.py:63
  18.7 1.5 %collective-permute-start.5 = (bf16[32,3072]{1,0:T(8,128)(2,1)S(1)}, bf16[32,3072]{1,0:T(8,128)(2,1)S(1)}, u32[]{:S(2)}, u32[]{:S(2)}) collective-permute-start(bf16[32,3072]{1,0:T(8,128)(2,1)S(1)} %collective-permute-done.1.refs_2_), channel_id=1, source_target_pairs={{0,2},{2,0},{4,6},{6,4},{8,10},{10,8},{12,14},{14,12},{1,3},{3,1},... | collective-permute-start | bytes 589832 | tf_op jit(solution)/shard_map/ppermute | solution.py:59
  20.8 6.5 %shard_map.73.refs_1_ = bf16[3072,3072]{1,0:T(8,128)(2,1)S(1)} custom-call(bf16[3072,3072]{1,0:T(8,128)(2,1)} %refs_0_.1, bf16[32,3072]{1,0:T(8,128)(2,1)S(1)} %collective-permute-done.refs_1_, bf16[32,3072]{1,0:T(8,128)(2,1)S(1)} %collective-permute-done.1.refs_2_, bf16[32,3072]{1,0:T(8,128)(2,1)S(1)} %collective-permute-done.2.refs_3_), custom_call_target="tpu_custom_call" | custom-call | bytes 37748736 | tf_op jit(solution)/shard_map/pallas_call | solution.py:109
  27.3 2.3 %collective-permute-done.4 = bf16[32,3072]{1,0:T(8,128)(2,1)S(1)} collective-permute-done((bf16[32,3072]{1,0:T(8,128)(2,1)S(1)}, bf16[32,3072]{1,0:T(8,128)(2,1)S(1)}, u32[]{:S(2)}, u32[]{:S(2)}) %collective-permute-start.4) | collective-permute-done | bytes 196640 | tf_op jit(solution)/shard_map/ppermute | solution.py:59
  29.7 2.7 %shard_map.75.own_ref = f32[256,1536]{1,0:T(8,128)S(1)} custom-call(bf16[256,3072]{1,0:T(8,128)(2,1)S(1)} %constant_dynamic-update-slice_fusion.refs_0_, bf16[3072,3072]{1,0:T(8,128)(2,1)S(1)} %shard_map.73.refs_1_), custom_call_target="tpu_custom_call" | custom-call | flops 2415919104 | bytes 1572864 | tf_op jit(solution)/shard_map/pallas_call | solution.py:128
  32.5 2.7 %shard_map.74.own_ref = f32[256,1536]{1,0:T(8,128)S(1)} custom-call(bf16[256,3072]{1,0:T(8,128)(2,1)S(1)} %constant_dynamic-update-slice_fusion.refs_0_, bf16[3072,3072]{1,0:T(8,128)(2,1)S(1)} %shard_map.73.refs_1_), custom_call_target="tpu_custom_call" | custom-call | flops 2415919104 | bytes 1572864 | tf_op jit(solution)/shard_map/pallas_call | solution.py:128
  36.6 4.9 %shard_map.76.sum_ref = f32[256,3072]{1,0:T(8,128)S(1)} custom-call(f32[256,1536]{1,0:T(8,128)S(1)} %shard_map.75.own_ref, f32[256,1536]{1,0:T(8,128)S(1)} %collective-permute-done.8.other_ref, f32[256,1536]{1,0:T(8,128)S(1)} %get-tuple-element.31.scale_ref, bf16[3072,3072]{1,0:T(8,128)(2,1)} %w_ref.5), custom_call_target="tpu_custom_call" | custom-call | flops 2415919104 | bytes 9437184 | tf_op jit(solution)/shard_map/pallas_call | solution.py:192
  41.5 2.5 %shard_map.77 = (f32[2,32,768]{2,1,0:T(8,128)S(1)}, bf16[2,32,768]{2,1,0:T(8,128)(2,1)S(1)}, bf16[2,32,768]{2,1,0:T(8,128)(2,1)S(1)}, bf16[2,32,768]{2,1,0:T(8,128)(2,1)S(1)}, bf16[256,1536]{1,0:T(8,128)(2,1)S(1)}) custom-call(f32[256,1536]{1,0:T(8,128)S(1)} %shard_map.74.own_ref, f32[256,1536]{1,0:T(8,128)S(1)} %collective-permute-done.7.other_ref, ...), custom_call_target="tpu_custom_call" | custom-call | flops 603979776 | bytes 2359296 | tf_op jit(solution)/shard_map/pallas_call | solution.py:229
  44.0 3.1 %collective-permute-start.15 = (bf16[2,32,768]{2,1,0:T(8,128)(2,1)S(1)}, bf16[2,32,768]{2,1,0:T(8,128)(2,1)S(1)}, u32[]{:S(2)}, u32[]{:S(2)}) collective-permute-start(bf16[2,32,768]{2,1,0:T(8,128)(2,1)S(1)} %get-tuple-element.27), channel_id=1, source_target_pairs={{0,4},{2,6},{4,8},{6,10},{8,12},{10,14},{12,0},{14,2},{1,5},{3,7},... | collective-permute-start | bytes 294920 | tf_op jit(solution)/shard_map/ppermute | solution.py:69
  47.1 2.2 %collective-permute-start.16 = (bf16[2,32,768]{2,1,0:T(8,128)(2,1)S(1)}, bf16[2,32,768]{2,1,0:T(8,128)(2,1)S(1)}, u32[]{:S(2)}, u32[]{:S(2)}) collective-permute-start(bf16[2,32,768]{2,1,0:T(8,128)(2,1)S(1)} %get-tuple-element.28), channel_id=1, source_target_pairs={{0,8},{2,10},{4,12},{6,14},{8,0},{10,2},{12,4},{14,6},{1,9},{3,11}... | collective-permute-start | bytes 294920 | tf_op jit(solution)/shard_map/ppermute | solution.py:69
  49.8 4.4 %shard_map.78 = (f32[32,2304]{1,0:T(8,128)S(1)}, f32[32,2304]{1,0:T(8,128)S(1)}, f32[32,2304]{1,0:T(8,128)S(1)}, f32[32,2304]{1,0:T(8,128)S(1)}, bf16[32,2304]{1...) custom-call(bf16[256,1536]{1,0:T(8,128)(2,1)S(1)} %get-tuple-element., ...), custom_call_target="tpu_custom_call" | custom-call | flops 1811939328 | bytes 7077888 | tf_op jit(solution)/shard_map/pallas_call | solution.py:264
  54.2 1.6 %collective-permute-start.9 = (bf16[32,2304]{1,0:T(8,128)(2,1)S(1)}, bf16[32,2304]{1,0:T(8,128)(2,1)S(1)}, u32[]{:S(2)}, u32[]{:S(2)}) collective-permute-start(bf16[32,2304]{1,0:T(8,128)(2,1)S(1)} %get-tuple-element.21), channel_id=1, source_target_pairs={{0,2},{2,0},{4,6},{6,4},{8,10},{10,8},{12,14},{14,12},{1,3},{3,1},... | collective-permute-start | bytes 442376 | tf_op jit(solution)/shard_map/ppermute | solution.py:59
  56.3 1.5 %collective-permute-start.13 = (bf16[32,2304]{1,0:T(8,128)(2,1)S(1)}, bf16[32,2304]{1,0:T(8,128)(2,1)S(1)}, u32[]{:S(2)}, u32[]{:S(2)}) collective-permute-start(bf16[32,2304]{1,0:T(8,128)(2,1)S(1)} %get-tuple-element.25), channel_id=1, source_target_pairs={{0,2},{2,0},{4,6},{6,4},{8,10},{10,8},{12,14},{14,12},{1,3},{3,1},... | collective-permute-start | bytes 442376 | tf_op jit(solution)/shard_map/ppermute | solution.py:59
  58.5 2.6 %collective-permute-done.9 = bf16[32,2304]{1,0:T(8,128)(2,1)S(1)} collective-permute-done((bf16[32,2304]{1,0:T(8,128)(2,1)S(1)}, bf16[32,2304]{1,0:T(8,128)(2,1)S(1)}, u32[]{:S(2)}, u32[]{:S(2)}) %collective-permute-start.9) | collective-permute-done | bytes 147488 | tf_op jit(solution)/shard_map/ppermute | solution.py:59
  61.1 1.7 %collective-permute-start.10 = (bf16[32,2304]{1,0:T(8,128)(2,1)S(1)}, bf16[32,2304]{1,0:T(8,128)(2,1)S(1)}, u32[]{:S(2)}, u32[]{:S(2)}) collective-permute-start(bf16[32,2304]{1,0:T(8,128)(2,1)S(1)} %add_convert_fusion.2), channel_id=1, source_target_pairs={{0,4},{2,6},{4,8},{6,10},{8,12},{10,14},{12,0},{14,2},{1,5},{3,7},... | collective-permute-start | bytes 442376 | tf_op jit(solution)/shard_map/ppermute | solution.py:69
  62.7 1.5 %collective-permute-done.11 = bf16[32,2304]{1,0:T(8,128)(2,1)S(1)} collective-permute-done((bf16[32,2304]{1,0:T(8,128)(2,1)S(1)}, bf16[32,2304]{1,0:T(8,128)(2,1)S(1)}, u32[]{:S(2)}, u32[]{:S(2)}) %collective-permute-start.11) | collective-permute-done | bytes 147488 | tf_op jit(solution)/shard_map/ppermute | solution.py:59
  64.2 1.2 %collective-permute-start.12 = (bf16[32,2304]{1,0:T(8,128)(2,1)S(1)}, bf16[32,2304]{1,0:T(8,128)(2,1)S(1)}, u32[]{:S(2)}, u32[]{:S(2)}) collective-permute-start(bf16[32,2304]{1,0:T(8,128)(2,1)S(1)} %add_convert_fusion.1), channel_id=1, source_target_pairs={{0,8},{2,10},{4,12},{6,14},{8,0},{10,2},{12,4},{14,6},{1,9},{3,11}... | collective-permute-start | bytes 442376 | tf_op jit(solution)/shard_map/ppermute | solution.py:69
  65.4 1.9 %collective-permute-done.13 = bf16[32,2304]{1,0:T(8,128)(2,1)S(1)} collective-permute-done((bf16[32,2304]{1,0:T(8,128)(2,1)S(1)}, bf16[32,2304]{1,0:T(8,128)(2,1)S(1)}, u32[]{:S(2)}, u32[]{:S(2)}) %collective-permute-start.13) | collective-permute-done | bytes 147488 | tf_op jit(solution)/shard_map/ppermute | solution.py:59
  67.4 1.8 %collective-permute-start.14 = (bf16[32,2304]{1,0:T(8,128)(2,1)S(1)}, bf16[32,2304]{1,0:T(8,128)(2,1)S(1)}, u32[]{:S(2)}, u32[]{:S(2)}) collective-permute-start(bf16[32,2304]{1,0:T(8,128)(2,1)S(1)} %add_convert_fusion), channel_id=1, source_target_pairs={{0,12},{2,14},{4,0},{6,2},{8,4},{10,6},{12,8},{14,10},{1,13},{3,15... | collective-permute-start | bytes 442376 | tf_op jit(solution)/shard_map/ppermute | solution.py:69
  69.3 4.5 %collective-permute-done.12 = bf16[32,2304]{1,0:T(8,128)(2,1)S(1)} collective-permute-done((bf16[32,2304]{1,0:T(8,128)(2,1)S(1)}, bf16[32,2304]{1,0:T(8,128)(2,1)S(1)}, u32[]{:S(2)}, u32[]{:S(2)}) %collective-permute-start.12) | collective-permute-done | bytes 147488 | tf_op jit(solution)/shard_map/ppermute | solution.py:69
  (57 shorter events, 10.8 us)
Async XLA Ops:
  0.0 13.9 %collective-permute-start.2 = (bf16[32,3072]{1,0:T(8,128)(2,1)}, bf16[32,3072]{1,0:T(8,128)(2,1)S(1)}, u32[]{:S(2)}, u32[]{:S(2)}) collective-permute-start(bf16[32,3072]{1,0:T(8,128)(2,1)} %param.7), channel_id=1, source_target_pairs={{12,0},{14,2},{0,4},{2,6},{4,8},{6,10},{8,12},{10,14},{13,1},{15,3... | collective-permute-start | bytes 589832 | tf_op jit(solution)/shard_map/ppermute | solution.py:63
  3.0 15.7 %collective-permute-start.1 = (bf16[32,3072]{1,0:T(8,128)(2,1)}, bf16[32,3072]{1,0:T(8,128)(2,1)S(1)}, u32[]{:S(2)}, u32[]{:S(2)}) collective-permute-start(bf16[32,3072]{1,0:T(8,128)(2,1)} %param.7), channel_id=1, source_target_pairs={{8,0},{10,2},{12,4},{14,6},{0,8},{2,10},{4,12},{6,14},{9,1},{11,3}... | collective-permute-start | bytes 589832 | tf_op jit(solution)/shard_map/ppermute | solution.py:63
  5.6 14.6 %collective-permute-start = (bf16[32,3072]{1,0:T(8,128)(2,1)}, bf16[32,3072]{1,0:T(8,128)(2,1)S(1)}, u32[]{:S(2)}, u32[]{:S(2)}) collective-permute-start(bf16[32,3072]{1,0:T(8,128)(2,1)} %param.7), channel_id=1, source_target_pairs={{4,0},{6,2},{8,4},{10,6},{12,8},{14,10},{0,12},{2,14},{5,1},{7,3},... | collective-permute-start | bytes 589832 | tf_op jit(solution)/shard_map/ppermute | solution.py:63
  7.0 20.3 %collective-permute-start.3 = (bf16[32,3072]{1,0:T(8,128)(2,1)}, bf16[32,3072]{1,0:T(8,128)(2,1)S(1)}, u32[]{:S(2)}, u32[]{:S(2)}) collective-permute-start(bf16[32,3072]{1,0:T(8,128)(2,1)} %param.7), channel_id=1, source_target_pairs={{0,2},{2,0},{4,6},{6,4},{8,10},{10,8},{12,14},{14,12},{1,3},{3,1},... | collective-permute-start | bytes 589832 | tf_op jit(solution)/shard_map/ppermute | solution.py:59
  13.9 15.8 %collective-permute-start.6 = (bf16[32,3072]{1,0:T(8,128)(2,1)S(1)}, bf16[32,3072]{1,0:T(8,128)(2,1)S(1)}, u32[]{:S(2)}, u32[]{:S(2)}) collective-permute-start(bf16[32,3072]{1,0:T(8,128)(2,1)S(1)} %collective-permute-done.2.refs_3_), channel_id=1, source_target_pairs={{0,2},{2,0},{4,6},{6,4},{8,10},{10,8},{12,14},{14,12},{1,3},{3,1},... | collective-permute-start | bytes 589832 | tf_op jit(solution)/shard_map/ppermute | solution.py:59
  18.7 11.0 %collective-permute-start.5 = (bf16[32,3072]{1,0:T(8,128)(2,1)S(1)}, bf16[32,3072]{1,0:T(8,128)(2,1)S(1)}, u32[]{:S(2)}, u32[]{:S(2)}) collective-permute-start(bf16[32,3072]{1,0:T(8,128)(2,1)S(1)} %collective-permute-done.1.refs_2_), channel_id=1, source_target_pairs={{0,2},{2,0},{4,6},{6,4},{8,10},{10,8},{12,14},{14,12},{1,3},{3,1},... | collective-permute-start | bytes 589832 | tf_op jit(solution)/shard_map/ppermute | solution.py:59
  20.2 9.4 %collective-permute-start.4 = (bf16[32,3072]{1,0:T(8,128)(2,1)S(1)}, bf16[32,3072]{1,0:T(8,128)(2,1)S(1)}, u32[]{:S(2)}, u32[]{:S(2)}) collective-permute-start(bf16[32,3072]{1,0:T(8,128)(2,1)S(1)} %collective-permute-done.refs_1_), channel_id=1, source_target_pairs={{0,2},{2,0},{4,6},{6,4},{8,10},{10,8},{12,14},{14,12},{1,3},{3,1},... | collective-permute-start | bytes 589832 | tf_op jit(solution)/shard_map/ppermute | solution.py:59
  32.4 3.3 %copy-start = (f32[8,3072]{1,0:T(8,128)S(1)}, f32[8,3072]{1,0:T(8,128)}, u32[]{:S(2)}) copy-start(f32[8,3072]{1,0:T(8,128)} %param.10) | copy-start | bytes 294916
  32.4 4.2 %collective-permute-start.8 = (f32[256,1536]{1,0:T(8,128)S(1)}, f32[256,1536]{1,0:T(8,128)S(1)}, u32[]{:S(2)}, u32[]{:S(2)}) collective-permute-start(f32[256,1536]{1,0:T(8,128)S(1)} %shard_map.75.own_ref), channel_id=1, source_target_pairs={{0,1},{1,0},{2,3},{3,2},{4,5},{5,4},{6,7},{7,6},{8,9},{9,8},{10,11... | collective-permute-start | bytes 4718600 | tf_op jit(solution)/shard_map/ppermute | solution.py:277
  35.2 6.4 %collective-permute-start.7 = (f32[256,1536]{1,0:T(8,128)S(1)}, f32[256,1536]{1,0:T(8,128)S(1)}, u32[]{:S(2)}, u32[]{:S(2)}) collective-permute-start(f32[256,1536]{1,0:T(8,128)S(1)} %shard_map.74.own_ref), channel_id=1, source_target_pairs={{0,1},{1,0},{2,3},{3,2},{4,5},{5,4},{6,7},{7,6},{8,9},{9,8},{10,11... | collective-permute-start | bytes 4718600 | tf_op jit(solution)/shard_map/ppermute | solution.py:277
  44.0 12.3 %collective-permute-start.15 = (bf16[2,32,768]{2,1,0:T(8,128)(2,1)S(1)}, bf16[2,32,768]{2,1,0:T(8,128)(2,1)S(1)}, u32[]{:S(2)}, u32[]{:S(2)}) collective-permute-start(bf16[2,32,768]{2,1,0:T(8,128)(2,1)S(1)} %get-tuple-element.27), channel_id=1, source_target_pairs={{0,4},{2,6},{4,8},{6,10},{8,12},{10,14},{12,0},{14,2},{1,5},{3,7},... | collective-permute-start | bytes 294920 | tf_op jit(solution)/shard_map/ppermute | solution.py:69
  47.1 10.7 %collective-permute-start.16 = (bf16[2,32,768]{2,1,0:T(8,128)(2,1)S(1)}, bf16[2,32,768]{2,1,0:T(8,128)(2,1)S(1)}, u32[]{:S(2)}, u32[]{:S(2)}) collective-permute-start(bf16[2,32,768]{2,1,0:T(8,128)(2,1)S(1)} %get-tuple-element.28), channel_id=1, source_target_pairs={{0,8},{2,10},{4,12},{6,14},{8,0},{10,2},{12,4},{14,6},{1,9},{3,11}... | collective-permute-start | bytes 294920 | tf_op jit(solution)/shard_map/ppermute | solution.py:69
  49.4 8.4 %collective-permute-start.17 = (bf16[2,32,768]{2,1,0:T(8,128)(2,1)S(1)}, bf16[2,32,768]{2,1,0:T(8,128)(2,1)S(1)}, u32[]{:S(2)}, u32[]{:S(2)}) collective-permute-start(bf16[2,32,768]{2,1,0:T(8,128)(2,1)S(1)} %get-tuple-element.29), channel_id=1, source_target_pairs={{0,12},{2,14},{4,0},{6,2},{8,4},{10,6},{12,8},{14,10},{1,13},{3,15... | collective-permute-start | bytes 294920 | tf_op jit(solution)/shard_map/ppermute | solution.py:69
  54.2 6.8 %collective-permute-start.9 = (bf16[32,2304]{1,0:T(8,128)(2,1)S(1)}, bf16[32,2304]{1,0:T(8,128)(2,1)S(1)}, u32[]{:S(2)}, u32[]{:S(2)}) collective-permute-start(bf16[32,2304]{1,0:T(8,128)(2,1)S(1)} %get-tuple-element.21), channel_id=1, source_target_pairs={{0,2},{2,0},{4,6},{6,4},{8,10},{10,8},{12,14},{14,12},{1,3},{3,1},... | collective-permute-start | bytes 442376 | tf_op jit(solution)/shard_map/ppermute | solution.py:59
  55.8 8.4 %collective-permute-start.11 = (bf16[32,2304]{1,0:T(8,128)(2,1)S(1)}, bf16[32,2304]{1,0:T(8,128)(2,1)S(1)}, u32[]{:S(2)}, u32[]{:S(2)}) collective-permute-start(bf16[32,2304]{1,0:T(8,128)(2,1)S(1)} %get-tuple-element.23), channel_id=1, source_target_pairs={{0,2},{2,0},{4,6},{6,4},{8,10},{10,8},{12,14},{14,12},{1,3},{3,1},... | collective-permute-start | bytes 442376 | tf_op jit(solution)/shard_map/ppermute | solution.py:59
  56.3 11.1 %collective-permute-start.13 = (bf16[32,2304]{1,0:T(8,128)(2,1)S(1)}, bf16[32,2304]{1,0:T(8,128)(2,1)S(1)}, u32[]{:S(2)}, u32[]{:S(2)}) collective-permute-start(bf16[32,2304]{1,0:T(8,128)(2,1)S(1)} %get-tuple-element.25), channel_id=1, source_target_pairs={{0,2},{2,0},{4,6},{6,4},{8,10},{10,8},{12,14},{14,12},{1,3},{3,1},... | collective-permute-start | bytes 442376 | tf_op jit(solution)/shard_map/ppermute | solution.py:59
  57.9 16.0 %collective-permute-start.18 = (bf16[32,3072]{1,0:T(8,128)(2,1)S(1)}, bf16[32,3072]{1,0:T(8,128)(2,1)S(1)}, u32[]{:S(2)}, u32[]{:S(2)}) collective-permute-start(bf16[32,3072]{1,0:T(8,128)(2,1)S(1)} %pad_maximum_fusion), channel_id=1, source_target_pairs={{0,2},{2,0},{4,6},{6,4},{8,10},{10,8},{12,14},{14,12},{1,3},{3,1},... | collective-permute-start | bytes 589832 | tf_op jit(solution)/shard_map/ppermute | solution.py:59
  61.1 8.3 %collective-permute-start.10 = (bf16[32,2304]{1,0:T(8,128)(2,1)S(1)}, bf16[32,2304]{1,0:T(8,128)(2,1)S(1)}, u32[]{:S(2)}, u32[]{:S(2)}) collective-permute-start(bf16[32,2304]{1,0:T(8,128)(2,1)S(1)} %add_convert_fusion.2), channel_id=1, source_target_pairs={{0,4},{2,6},{4,8},{6,10},{8,12},{10,14},{12,0},{14,2},{1,5},{3,7},... | collective-permute-start | bytes 442376 | tf_op jit(solution)/shard_map/ppermute | solution.py:69
  64.2 9.6 %collective-permute-start.12 = (bf16[32,2304]{1,0:T(8,128)(2,1)S(1)}, bf16[32,2304]{1,0:T(8,128)(2,1)S(1)}, u32[]{:S(2)}, u32[]{:S(2)}) collective-permute-start(bf16[32,2304]{1,0:T(8,128)(2,1)S(1)} %add_convert_fusion.1), channel_id=1, source_target_pairs={{0,8},{2,10},{4,12},{6,14},{8,0},{10,2},{12,4},{14,6},{1,9},{3,11}... | collective-permute-start | bytes 442376 | tf_op jit(solution)/shard_map/ppermute | solution.py:69
  67.4 6.5 %collective-permute-start.14 = (bf16[32,2304]{1,0:T(8,128)(2,1)S(1)}, bf16[32,2304]{1,0:T(8,128)(2,1)S(1)}, u32[]{:S(2)}, u32[]{:S(2)}) collective-permute-start(bf16[32,2304]{1,0:T(8,128)(2,1)S(1)} %add_convert_fusion), channel_id=1, source_target_pairs={{0,12},{2,14},{4,0},{6,2},{8,4},{10,6},{12,8},{14,10},{1,13},{3,15... | collective-permute-start | bytes 442376 | tf_op jit(solution)/shard_map/ppermute | solution.py:69

commit v3 on v2

--- a/solution.py
+++ b/solution.py
@@ -52,22 +52,15 @@
     return (summed_rows * scale_two).astype(jnp.bfloat16)
 
 
-ACROSS = [(z * 2 + y, z * 2 + 1 - y) for z in range(4) for y in range(2)]
-
-
 def move_y(x):
-    return lax.ppermute(x, "fin", ACROSS)
-
-
-def fetch_z(x, k):
     return lax.ppermute(
-        x, "fin", [((z + k) % 4 * 2 + y, z * 2 + y) for z in range(4) for y in range(2)]
-    )
-
-
-def send_z(x, k):
+        x, "fin", [(z * 2 + y, z * 2 + 1 - y) for z in range(4) for y in range(2)]
+    )
+
+
+def move_z(x, k):
     return lax.ppermute(
-        x, "fin", [(z * 2 + y, (z + k) % 4 * 2 + y) for z in range(4) for y in range(2)]
+        x, "fin", [(z * 2 + y, (z ^ k) * 2 + y) for z in range(4) for y in range(2)]
     )
 
 
@@ -79,7 +72,6 @@
 HBM = pl.BlockSpec(memory_space=pltpu.HBM)
 ANY = pl.BlockSpec(memory_space=pl.ANY)
 TILE = 512
-AHEAD = 3
 
 
 def params(mib):
@@ -137,25 +129,32 @@
     )(x, w)
 
 
-def tiles(w_ref, first_row, first_column, held_ref, sems):
-    count, rows, width = held_ref.shape
-    moving = [
-        pltpu.make_async_copy(
-            w_ref.at[pl.ds(first_row, rows), pl.ds(first_column + i * width, width)],
-            held_ref.at[i],
-            sems.at[i],
-        )
-        for i in range(count)
-    ]
-    for c in moving[:AHEAD]:
-        c.start()
-    return moving
-
-
-def arrive(moving, i):
-    moving[i].wait()
-    if i + AHEAD < len(moving):
-        moving[i + AHEAD].start()
+def up_and_load_kernel(start, x_ref, w_ref, next_ref, out_ref, held_ref, sem):
+    rows, width = held_ref.shape
+    moving = pltpu.make_async_copy(
+        next_ref.at[pl.ds(0, rows), pl.ds(0, width)], held_ref, sem
+    )
+    moving.start()
+    up_kernel(start, x_ref, w_ref, out_ref)
+    moving.wait()
+
+
+def up_and_load(x, w, start, count, w_next, held):
+    rows = x.shape[0]
+    return pl.pallas_call(
+        lambda *refs: up_and_load_kernel(start, *refs),
+        in_specs=[VMEM, VMEM, HBM],
+        out_specs=[VMEM] * 2,
+        out_shape=[
+            jax.ShapeDtypeStruct((rows, count), jnp.float32),
+            pltpu.VMEM(held, w_next.dtype),
+        ],
+        scratch_shapes=[pltpu.SemaphoreType.DMA],
+        compiler_params=params(2),
+        cost_estimate=pl.CostEstimate(
+            flops=2 * rows * w.shape[0] * count, bytes_accessed=4 * rows * count, transcendentals=0
+        ),
+    )(x, w, w_next)
 
 
 def activate(own_ref, other_ref, scale_ref, hidden_ref):
@@ -166,18 +165,34 @@
         hidden_ref[:, at] = (0.5 * v * (1 + jnp.tanh(inner))).astype(hidden_ref.dtype)
 
 
-def down_first_kernel(own_ref, other_ref, scale_ref, w_ref, out_ref, hidden_ref, held_ref, sems):
-    moving = tiles(w_ref, 0, 0, held_ref, sems)
+def down_first_kernel(
+    own_ref, other_ref, scale_ref, held_ref, w_ref, out_ref, next_ref, hidden_ref, rest_ref, sems
+):
+    rows, width = held_ref.shape
+    rest = pltpu.make_async_copy(
+        w_ref.at[pl.ds(0, rows), pl.ds(width, rest_ref.shape[1])], rest_ref, sems.at[0]
+    )
+    step = next_ref.shape[0] // 2
+    following = [
+        pltpu.make_async_copy(
+            w_ref.at[pl.ds(rows + i * step, step)], next_ref.at[pl.ds(i * step, step)], sems.at[1 + i]
+        )
+        for i in range(2)
+    ]
+    rest.start()
+    for c in following:
+        c.start()
     activate(own_ref, other_ref, scale_ref, hidden_ref)
-    width = held_ref.shape[2]
-    for i in range(len(moving)):
-        arrive(moving, i)
-        out_ref[:, i * width : (i + 1) * width] = dot(hidden_ref[...], held_ref[i])
-
-
-def held(rows, width, tile):
-    count = width // tile
-    return [pltpu.VMEM((count, rows, tile), jnp.bfloat16), pltpu.SemaphoreType.DMA((count,))]
+    for lo in range(0, width, TILE):
+        at = slice(lo, lo + TILE)
+        out_ref[:, at] = dot(hidden_ref[...], held_ref[:, at])
+    rest.wait()
+    for lo in range(0, rest_ref.shape[1], TILE):
+        out_ref[:, width + lo : width + lo + TILE] = dot(
+            hidden_ref[...], rest_ref[:, lo : lo + TILE]
+        )
+    for c in following:
+        c.wait()
 
 
 def cost(rows, count, width):
@@ -186,34 +201,39 @@
     )
 
 
-def down_first(own, other, scale, w):
+def down_first(own, other, scale, held, w):
     rows, count = own.shape
     width = w.shape[1]
     return pl.pallas_call(
         down_first_kernel,
-        in_specs=[VMEM] * 3 + [HBM],
-        out_specs=VMEM,
-        out_shape=jax.ShapeDtypeStruct((rows, width), jnp.float32),
-        scratch_shapes=[pltpu.VMEM((rows, count), jnp.bfloat16)] + held(count, width, TILE),
-        compiler_params=params(13),
+        in_specs=[VMEM] * 4 + [HBM],
+        out_specs=[VMEM] * 2,
+        out_shape=[
+            jax.ShapeDtypeStruct((rows, width), jnp.float32),
+            pltpu.VMEM((w.shape[0] - count, width), w.dtype),
+        ],
+        scratch_shapes=[
+            pltpu.VMEM((rows, count), jnp.bfloat16),
+            pltpu.VMEM((count, width - held.shape[1]), jnp.bfloat16),
+            pltpu.SemaphoreType.DMA((3,)),
+        ],
+        compiler_params=params(8),
         cost_estimate=cost(rows, count, width),
-    )(own, other, scale, w)
+    )(own, other, scale, held, w)
 
 
 def over_z_kernel(
     own_ref, other_ref, scale_ref, w_ref, sum_ref,
-    kept_ref, one_ref, two_ref, three_ref, hidden_ref, held_ref, sems,
+    kept_ref, one_ref, two_ref, three_ref, hidden_ref,
 ):
     first_column = w_ref.shape[1] - kept_ref.shape[2]
-    moving = tiles(w_ref, w_ref.shape[0] - own_ref.shape[1], first_column, held_ref, sems)
     activate(own_ref, other_ref, scale_ref, hidden_ref)
     rows = kept_ref.shape[1]
-    step = held_ref.shape[2]
-    for i in range(len(moving)):
-        at = slice(first_column + i * step, first_column + (i + 1) * step)
-        out = slice(i * step, (i + 1) * step)
-        arrive(moving, i)
-        terms = sum_ref[:, at] + dot(hidden_ref[...], held_ref[i])
+    step = 256
+    for lo in range(0, kept_ref.shape[2], step):
+        at = slice(first_column + lo, first_column + lo + step)
+        out = slice(lo, lo + step)
+        terms = sum_ref[:, at] + dot(hidden_ref[...], w_ref[:, at])
         for j in range(2):
             base = j * 4 * rows
             kept_ref[j, :, out] = terms[base : base + rows]
@@ -228,7 +248,7 @@
     moved = jax.ShapeDtypeStruct(blocks, jnp.bfloat16)
     return pl.pallas_call(
         over_z_kernel,
-        in_specs=[VMEM] * 3 + [HBM, VMEM],
+        in_specs=[VMEM] * 5,
         out_specs=[VMEM] * 5,
         out_shape=[
             jax.ShapeDtypeStruct(blocks, jnp.float32),
@@ -237,21 +257,18 @@
             moved,
             jax.ShapeDtypeStruct((rows, count), jnp.bfloat16),
         ],
-        scratch_shapes=held(count, width, width // 2),
-        compiler_params=params(6),
+        compiler_params=params(2),
         cost_estimate=cost(rows, count, width),
     )(own, other, scale, w, total)
 
 
 def over_y_kernel(hidden_ref, w_ref, sum_ref, *out):
-    kept, crossing, held_ref, sems = out[:4], out[4:8], out[8], out[9]
-    moving = tiles(w_ref, w_ref.shape[0] - hidden_ref.shape[1], 0, held_ref, sems)
-    rows = kept[0].shape[0]
-    step = held_ref.shape[2]
-    for i in range(len(moving)):
-        at = slice(i * step, (i + 1) * step)
-        arrive(moving, i)
-        terms = sum_ref[:, at] + dot(hidden_ref[...], held_ref[i])
+    kept, crossing = out[:4], out[4:]
+    rows, width = kept[0].shape
+    step = 256
+    for lo in range(0, width, step):
+        at = slice(lo, lo + step)
+        terms = sum_ref[:, at] + dot(hidden_ref[...], w_ref[:, at])
         for k in range(4):
             low = (4 + k) * rows
             kept[k][:, at] = terms[k * rows : (k + 1) * rows]
@@ -263,12 +280,11 @@
     block = (rows // 8, width)
     return pl.pallas_call(
         over_y_kernel,
-        in_specs=[VMEM, HBM, VMEM],
+        in_specs=[VMEM] * 3,
         out_specs=[VMEM] * 8,
         out_shape=[jax.ShapeDtypeStruct(block, jnp.float32)] * 4
         + [jax.ShapeDtypeStruct(block, jnp.bfloat16)] * 4,
-        scratch_shapes=held(count, width, width // 2),
-        compiler_params=params(10),
+        compiler_params=params(2),
         cost_estimate=cost(rows, count, width),
     )(hidden, w, total)
 
@@ -284,33 +300,36 @@
     half = jnp.bfloat16
 
     k, j = jnp.arange(4, dtype=jnp.int32), jnp.arange(2, dtype=jnp.int32)
-    block = ((z + k) % 4)[None, :] * 2 + (y ^ j)[:, None]
+    block = (z ^ k)[None, :] * 2 + (y ^ j)[:, None]
     rows = block.reshape(-1, 1) * own_rows + jnp.arange(own_rows, dtype=jnp.int32)[None, :]
     scale_one = scales(rows.reshape(-1), req_lengths, step_group, up_scale)
     scale_two = scales(rows[0], req_lengths, step_group, down_scale)
 
     w_up = pltpu.with_memory_space_constraint(w_up, pltpu.HBM)
     w_down = pltpu.with_memory_space_constraint(w_down, pltpu.HBM)
-    across = move_y(tokens)
-    singles = [fetch_z(tokens, k) for k in (1, 2, 3)]
-    up_held = load(w_up, singles)
-    single_pairs = [move_y(x) for x in singles]
-    full = jnp.concatenate([tokens, *singles, across, *single_pairs])
+    two, one, across = move_z(tokens, 2), move_z(tokens, 1), move_y(tokens)
+    up_held = load(w_up, [one, two])
+    one_across, two_across, three = move_y(one), move_y(two), move_z(two, 1)
+    full = jnp.concatenate(
+        [tokens, one, two, three, across, one_across, two_across, move_y(three)]
+    )
 
     count = w_up.shape[1] // 2
-    pre = [up(full, up_held, i * count, count) for i in range(2)]
+    first = up(full, up_held, 0, count)
+    second, down_held = up_and_load(full, up_held, count, count, w_down, (count, count))
+    pre = [first, second]
     other = [swap_cores(p) for p in pre]
     width = w_down.shape[1] * 3 // 4 // 128 * 128
-    total = down_first(pre[0], other[0], scale_one[:, :count], w_down)
+    total, down_rest = down_first(pre[0], other[0], scale_one[:, :count], down_held, w_down)
     a_kept, *a_sent, hidden = over_z_terms(
-        pre[1], other[1], scale_one[:, count:], w_down, total, w_down.shape[1] - width
-    )
-    b_terms = over_y_terms(hidden, w_down, total, width)
+        pre[1], other[1], scale_one[:, count:], down_rest, total, w_down.shape[1] - width
+    )
+    b_terms = over_y_terms(hidden, down_rest, total, width)
     b_kept, b_last, b_sent = b_terms[:4], b_terms[4], b_terms[5:]
 
-    a_moved = [send_z(x, k + 1) for k, x in enumerate(a_sent)]
-    b_across = [move_y(x) for x in b_sent]
-    b_moved = [send_z((b_kept[k] + wide(b_across[k - 1])).astype(half), k) for k in (1, 2, 3)]
+    a_moved = [move_z(a_sent[k - 1], k) for k in (3, 2, 1)]
+    b_across = [move_y(b_sent[k - 1]) for k in (3, 2, 1)]
+    b_moved = [move_z((b_kept[k] + wide(b_across[3 - k])).astype(half), k) for k in (3, 2, 1)]
     a_sum = a_kept + wide(a_moved[0]) + wide(a_moved[1]) + wide(a_moved[2])
     last = move_y(jnp.concatenate([b_last, a_sum[1].astype(half)], axis=1))
     b_sum = b_kept[0] + wide(b_moved[0]) + wide(b_moved[1]) + wide(b_moved[2])

time: 74.9 us -> 74 us (0.988)
  Pallas kernels: 23.6 us -> 21.4 us
  starting transfers between devices: 26.3 us -> 27.4 us
  other arithmetic: 5.06 us -> 4.29 us
    pallas_call x2 -> x1, Pallas kernels: 5.32 us -> 2.59 us  [up(): pl.pallas_call(lambda *refs: up_kernel(start, *refs), in_specs=[VMEM] * 2...]
    ppermute x17, starting transfers between devices: 25.7 us -> 26.7 us  [the longest x9 16.4 us: move_z(): lax.ppermute(x, 'fin', [(z * 2 + y, (z ^ k) * 2 + y) for z in range(4) fo...]
    pallas_call x3 -> x4, Pallas kernels: 11.8 us -> 12.3 us  [the longest x1 6.51 us: down_first(): pl.pallas_call(down_first_kernel, in_specs=[VMEM] * 4 + [HBM], out_specs=...]
  transfers between devices with their start and end apart: 19 -> 19, of which waited for: 7 -> 7; matrix products, arithmetic and copies ran while one was open for 9% -> 9% of each run, Pallas kernels for 25% -> 24%
where the time goes in v3:
time: 74 us; the launch traced here: 73.8 us
  starting transfers between devices  27.4 us (37%)
  Pallas kernels  21.4 us (29%)
  waiting for transfers between devices  16.8 us (23%)
  other arithmetic  4.29 us (6%)
  local copies, waits for them, and re-layouts  2.14 us (3%)
  matrix products  1.53 us (2%)
    ppermute x9, starting transfers between devices, move_z(): lax.ppermute(x, 'fin', [(z * 2 + y, (z ^ k) * 2 + y) for z in range(4) fo...  16.4 us
    ppermute x9, waiting for transfers between devices, move_z(): lax.ppermute(x, 'fin', [(z * 2 + y, (z ^ k) * 2 + y) for z in range(4) fo...  11.4 us
    ppermute x8, starting transfers between devices, move_y(): lax.ppermute(x, 'fin', [(z * 2 + y, z * 2 + 1 - y) for z in range(4) for...  10.3 us
    pallas_call x1, Pallas kernels, down_first(): pl.pallas_call(down_first_kernel, in_specs=[VMEM] * 4 + [HBM], out_specs=...  6.51 us
    pallas_call x1, Pallas kernels, load(): pl.pallas_call(load_kernel, in_specs=[HBM] + [ANY] * len(after), out_spec...  6.5 us
    ppermute x8, waiting for transfers between devices, move_y(): lax.ppermute(x, 'fin', [(z * 2 + y, z * 2 + 1 - y) for z in range(4) for...  5.39 us
    pallas_call x1, Pallas kernels, up_and_load(): pl.pallas_call(lambda *refs: up_and_load_kernel(start, *refs), in_specs=[...  2.61 us
    pallas_call x1, Pallas kernels, up(): pl.pallas_call(lambda *refs: up_kernel(start, *refs), in_specs=[VMEM] * 2...  2.59 us
  transfers between devices with their start and end apart: 19, of which 7 were waited for; matrix products, arithmetic and copies ran while one was open for 9% of the time, Pallas kernels for 24%

profile of v3, /device:TPU:0, one launch (start us, length us, event | category | flops | bytes accessed | tf_op | source)
XLA Modules:
  0.0 73.8 jit_solution(15718922077098673926)
XLA Ops:
  0.0 4.0 %collective-permute-start.1 = (bf16[32,3072]{1,0:T(8,128)(2,1)}, bf16[32,3072]{1,0:T(8,128)(2,1)S(1)}, u32[]{:S(2)}, u32[]{:S(2)}) collective-permute-start(bf16[32,3072]{1,0:T(8,128)(2,1)} %param.7), channel_id=1, source_target_pairs={{0,8},{2,10},{4,12},{6,14},{8,0},{10,2},{12,4},{14,6},{1,9},{3,11}... | collective-permute-start | bytes 589832 | tf_op jit(solution)/shard_map/ppermute | solution.py:62
  4.0 1.6 %collective-permute-start = (bf16[32,3072]{1,0:T(8,128)(2,1)}, bf16[32,3072]{1,0:T(8,128)(2,1)S(1)}, u32[]{:S(2)}, u32[]{:S(2)}) collective-permute-start(bf16[32,3072]{1,0:T(8,128)(2,1)} %param.7), channel_id=1, source_target_pairs={{0,4},{2,6},{4,0},{6,2},{8,12},{10,14},{12,8},{14,10},{1,5},{3,7},... | collective-permute-start | bytes 589832 | tf_op jit(solution)/shard_map/ppermute | solution.py:62
  5.6 1.5 %collective-permute-start.3 = (bf16[32,3072]{1,0:T(8,128)(2,1)}, bf16[32,3072]{1,0:T(8,128)(2,1)S(1)}, u32[]{:S(2)}, u32[]{:S(2)}) collective-permute-start(bf16[32,3072]{1,0:T(8,128)(2,1)} %param.7), channel_id=1, source_target_pairs={{0,2},{2,0},{4,6},{6,4},{8,10},{10,8},{12,14},{14,12},{1,3},{3,1},... | collective-permute-start | bytes 589832 | tf_op jit(solution)/shard_map/ppermute | solution.py:56
  12.4 1.1 %collective-permute-done.1.refs_2_ = bf16[32,3072]{1,0:T(8,128)(2,1)S(1)} collective-permute-done((bf16[32,3072]{1,0:T(8,128)(2,1)}, bf16[32,3072]{1,0:T(8,128)(2,1)S(1)}, u32[]{:S(2)}, u32[]{:S(2)}) %collective-permute-start.1) | collective-permute-done | bytes 196640 | tf_op jit(solution)/shard_map/ppermute | solution.py:62
  14.2 1.5 %collective-permute-start.5 = (bf16[32,3072]{1,0:T(8,128)(2,1)S(1)}, bf16[32,3072]{1,0:T(8,128)(2,1)S(1)}, u32[]{:S(2)}, u32[]{:S(2)}) collective-permute-start(bf16[32,3072]{1,0:T(8,128)(2,1)S(1)} %collective-permute-done.1.refs_2_), channel_id=1, source_target_pairs={{0,2},{2,0},{4,6},{6,4},{8,10},{10,8},{12,14},{14,12},{1,3},{3,1},... | collective-permute-start | bytes 589832 | tf_op jit(solution)/shard_map/ppermute | solution.py:56
  16.2 6.5 %shard_map.73.refs_1_ = bf16[3072,3072]{1,0:T(8,128)(2,1)S(1)} custom-call(bf16[3072,3072]{1,0:T(8,128)(2,1)} %refs_0_.1, bf16[32,3072]{1,0:T(8,128)(2,1)S(1)} %collective-permute-done.refs_1_, bf16[32,3072]{1,0:T(8,128)(2,1)S(1)} %collective-permute-done.1.refs_2_), custom_call_target="tpu_custom_call" | custom-call | bytes 37748736 | tf_op jit(solution)/shard_map/pallas_call | solution.py:101
  22.8 1.6 %collective-permute-start.6 = (bf16[32,3072]{1,0:T(8,128)(2,1)S(1)}, bf16[32,3072]{1,0:T(8,128)(2,1)S(1)}, u32[]{:S(2)}, u32[]{:S(2)}) collective-permute-start(bf16[32,3072]{1,0:T(8,128)(2,1)S(1)} %collective-permute-done.2), channel_id=1, source_target_pairs={{0,2},{2,0},{4,6},{6,4},{8,10},{10,8},{12,14},{14,12},{1,3},{3,1},... | collective-permute-start | bytes 589832 | tf_op jit(solution)/shard_map/ppermute | solution.py:56
  25.3 3.9 %collective-permute-done.6 = bf16[32,3072]{1,0:T(8,128)(2,1)S(1)} collective-permute-done((bf16[32,3072]{1,0:T(8,128)(2,1)S(1)}, bf16[32,3072]{1,0:T(8,128)(2,1)S(1)}, u32[]{:S(2)}, u32[]{:S(2)}) %collective-permute-start.6) | collective-permute-done | bytes 196640 | tf_op jit(solution)/shard_map/ppermute | solution.py:56
  29.2 2.6 %shard_map.75.own_ref = f32[256,1536]{1,0:T(8,128)S(1)} custom-call(bf16[256,3072]{1,0:T(8,128)(2,1)S(1)} %constant_dynamic-update-slice_fusion.refs_0_, bf16[3072,3072]{1,0:T(8,128)(2,1)S(1)} %shard_map.73.refs_1_), custom_call_target="tpu_custom_call" | custom-call | flops 2415919104 | bytes 1572864 | tf_op jit(solution)/shard_map/pallas_call | solution.py:120
  31.9 2.6 %shard_map.74 = (f32[256,1536]{1,0:T(8,128)S(1)}, bf16[1536,1536]{1,0:T(8,128)(2,1)S(1)}) custom-call(bf16[256,3072]{1,0:T(8,128)(2,1)S(1)} %constant_dynamic-update-slice_fusion.refs_0_, bf16[3072,3072]{1,0:T(8,128)(2,1)S(1)} %shard_map.73.refs_1_, bf16[3072,3072]{1,0:T(8,128)(2,1)} %w_ref.1), custom_call_target="tpu_custom_call" | custom-call | flops 2415919104 | bytes 1572864 | tf_op jit(solution)/shard_map/pallas_call | solution.py:144
  36.6 6.5 %shard_map.76 = (f32[256,3072]{1,0:T(8,128)S(1)}, bf16[1536,3072]{1,0:T(8,128)(2,1)S(1)}) custom-call(f32[256,1536]{1,0:T(8,128)S(1)} %shard_map.75.own_ref, f32[256,1536]{1,0:T(8,128)S(1)} %collective-permute-done.8.other_ref, f32[256,1536]{1,0:T(8,128)S(1)} %get-tuple-element.39.scale_ref, bf16[1536,1536]{1,0:T(8,128)(2,1)S(1)} %get-tuple-element.23.held_ref, ...), custom_call_target="tpu_custom_call" | custom-call | flops 2415919104 | bytes 9437184 | tf_op jit(solution)/shard_map/pallas_call | solution.py:207
  43.1 1.2 %shard_map.77 = (f32[2,32,768]{2,1,0:T(8,128)S(1)}, bf16[2,32,768]{2,1,0:T(8,128)(2,1)S(1)}, bf16[2,32,768]{2,1,0:T(8,128)(2,1)S(1)}, bf16[2,32,768]{2,1,0:T(8,128)(2,1)S(1)}, bf16[256,1536]{1,0:T(8,128)(2,1)S(1)}) custom-call(f32[256,1536]{1,0:T(8,128)S(1)} %get-tuple-element.22.own_ref, f32[256,1536]{1,0:T(8,128)S(1)} %collective-permute-done.7.other_ref, ...), custom_call_target="tpu_custom_call" | custom-call | flops 603979776 | bytes 2359296 | tf_op jit(solution)/shard_map/pallas_call | solution.py:249
  44.3 3.1 %collective-permute-start.15 = (bf16[2,32,768]{2,1,0:T(8,128)(2,1)S(1)}, bf16[2,32,768]{2,1,0:T(8,128)(2,1)S(1)}, u32[]{:S(2)}, u32[]{:S(2)}) collective-permute-start(bf16[2,32,768]{2,1,0:T(8,128)(2,1)S(1)} %get-tuple-element.35), channel_id=1, source_target_pairs={{0,12},{2,14},{4,8},{6,10},{8,4},{10,6},{12,0},{14,2},{1,13},{3,15... | collective-permute-start | bytes 294920 | tf_op jit(solution)/shard_map/ppermute | solution.py:62
  47.7 1.0 %collective-permute-start.17 = (bf16[2,32,768]{2,1,0:T(8,128)(2,1)S(1)}, bf16[2,32,768]{2,1,0:T(8,128)(2,1)S(1)}, u32[]{:S(2)}, u32[]{:S(2)}) collective-permute-start(bf16[2,32,768]{2,1,0:T(8,128)(2,1)S(1)} %get-tuple-element.37), channel_id=1, source_target_pairs={{0,4},{2,6},{4,0},{6,2},{8,12},{10,14},{12,8},{14,10},{1,5},{3,7},... | collective-permute-start | bytes 294920 | tf_op jit(solution)/shard_map/ppermute | solution.py:62
  48.8 2.0 %shard_map.78 = (f32[32,2304]{1,0:T(8,128)S(1)}, f32[32,2304]{1,0:T(8,128)S(1)}, f32[32,2304]{1,0:T(8,128)S(1)}, f32[32,2304]{1,0:T(8,128)S(1)}, bf16[32,2304]{1...) custom-call(bf16[256,1536]{1,0:T(8,128)(2,1)S(1)} %get-tuple-element., ...), custom_call_target="tpu_custom_call" | custom-call | flops 1811939328 | bytes 7077888 | tf_op jit(solution)/shard_map/pallas_call | solution.py:281
  50.8 1.6 %collective-permute-start.9 = (bf16[32,2304]{1,0:T(8,128)(2,1)S(1)}, bf16[32,2304]{1,0:T(8,128)(2,1)S(1)}, u32[]{:S(2)}, u32[]{:S(2)}) collective-permute-start(bf16[32,2304]{1,0:T(8,128)(2,1)S(1)} %get-tuple-element.29), channel_id=1, source_target_pairs={{0,2},{2,0},{4,6},{6,4},{8,10},{10,8},{12,14},{14,12},{1,3},{3,1},... | collective-permute-start | bytes 442376 | tf_op jit(solution)/shard_map/ppermute | solution.py:56
  52.9 1.5 %collective-permute-start.13 = (bf16[32,2304]{1,0:T(8,128)(2,1)S(1)}, bf16[32,2304]{1,0:T(8,128)(2,1)S(1)}, u32[]{:S(2)}, u32[]{:S(2)}) collective-permute-start(bf16[32,2304]{1,0:T(8,128)(2,1)S(1)} %get-tuple-element.33), channel_id=1, source_target_pairs={{0,2},{2,0},{4,6},{6,4},{8,10},{10,8},{12,14},{14,12},{1,3},{3,1},... | collective-permute-start | bytes 442376 | tf_op jit(solution)/shard_map/ppermute | solution.py:56
  54.4 2.6 %collective-permute-done.16 = bf16[2,32,768]{2,1,0:T(8,128)(2,1)S(1)} collective-permute-done((bf16[2,32,768]{2,1,0:T(8,128)(2,1)S(1)}, bf16[2,32,768]{2,1,0:T(8,128)(2,1)S(1)}, u32[]{:S(2)}, u32[]{:S(2)}) %collective-permute-start.16) | collective-permute-done | bytes 98336 | tf_op jit(solution)/shard_map/ppermute | solution.py:62
  57.0 1.6 %collective-permute-start.18 = (bf16[32,3072]{1,0:T(8,128)(2,1)S(1)}, bf16[32,3072]{1,0:T(8,128)(2,1)S(1)}, u32[]{:S(2)}, u32[]{:S(2)}) collective-permute-start(bf16[32,3072]{1,0:T(8,128)(2,1)S(1)} %pad_maximum_fusion), channel_id=1, source_target_pairs={{0,2},{2,0},{4,6},{6,4},{8,10},{10,8},{12,14},{14,12},{1,3},{3,1},... | collective-permute-start | bytes 589832 | tf_op jit(solution)/shard_map/ppermute | solution.py:56
  58.7 2.7 %collective-permute-start.10 = (bf16[32,2304]{1,0:T(8,128)(2,1)S(1)}, bf16[32,2304]{1,0:T(8,128)(2,1)S(1)}, u32[]{:S(2)}, u32[]{:S(2)}) collective-permute-start(bf16[32,2304]{1,0:T(8,128)(2,1)S(1)} %add_convert_fusion.2), channel_id=1, source_target_pairs={{0,12},{2,14},{4,8},{6,10},{8,4},{10,6},{12,0},{14,2},{1,13},{3,15... | collective-permute-start | bytes 442376 | tf_op jit(solution)/shard_map/ppermute | solution.py:62
  61.4 1.9 %collective-permute-start.12 = (bf16[32,2304]{1,0:T(8,128)(2,1)S(1)}, bf16[32,2304]{1,0:T(8,128)(2,1)S(1)}, u32[]{:S(2)}, u32[]{:S(2)}) collective-permute-start(bf16[32,2304]{1,0:T(8,128)(2,1)S(1)} %add_convert_fusion.1), channel_id=1, source_target_pairs={{0,8},{2,10},{4,12},{6,14},{8,0},{10,2},{12,4},{14,6},{1,9},{3,11}... | collective-permute-start | bytes 442376 | tf_op jit(solution)/shard_map/ppermute | solution.py:62
  64.0 1.1 %collective-permute-start.14 = (bf16[32,2304]{1,0:T(8,128)(2,1)S(1)}, bf16[32,2304]{1,0:T(8,128)(2,1)S(1)}, u32[]{:S(2)}, u32[]{:S(2)}) collective-permute-start(bf16[32,2304]{1,0:T(8,128)(2,1)S(1)} %add_convert_fusion), channel_id=1, source_target_pairs={{0,4},{2,6},{4,0},{6,2},{8,12},{10,14},{12,8},{14,10},{1,5},{3,7},... | collective-permute-start | bytes 442376 | tf_op jit(solution)/shard_map/ppermute | solution.py:62
  65.0 2.3 %collective-permute-done.10 = bf16[32,2304]{1,0:T(8,128)(2,1)S(1)} collective-permute-done((bf16[32,2304]{1,0:T(8,128)(2,1)S(1)}, bf16[32,2304]{1,0:T(8,128)(2,1)S(1)}, u32[]{:S(2)}, u32[]{:S(2)}) %collective-permute-start.10) | collective-permute-done | bytes 147488 | tf_op jit(solution)/shard_map/ppermute | solution.py:62
  67.4 5.4 %collective-permute-done.12 = bf16[32,2304]{1,0:T(8,128)(2,1)S(1)} collective-permute-done((bf16[32,2304]{1,0:T(8,128)(2,1)S(1)}, bf16[32,2304]{1,0:T(8,128)(2,1)S(1)}, u32[]{:S(2)}, u32[]{:S(2)}) %collective-permute-start.12) | collective-permute-done | bytes 147488 | tf_op jit(solution)/shard_map/ppermute | solution.py:62
  (56 shorter events, 12.2 us)
Async XLA Ops:
  0.0 13.5 %collective-permute-start.1 = (bf16[32,3072]{1,0:T(8,128)(2,1)}, bf16[32,3072]{1,0:T(8,128)(2,1)S(1)}, u32[]{:S(2)}, u32[]{:S(2)}) collective-permute-start(bf16[32,3072]{1,0:T(8,128)(2,1)} %param.7), channel_id=1, source_target_pairs={{0,8},{2,10},{4,12},{6,14},{8,0},{10,2},{12,4},{14,6},{1,9},{3,11}... | collective-permute-start | bytes 589832 | tf_op jit(solution)/shard_map/ppermute | solution.py:62
  4.0 11.7 %collective-permute-start = (bf16[32,3072]{1,0:T(8,128)(2,1)}, bf16[32,3072]{1,0:T(8,128)(2,1)S(1)}, u32[]{:S(2)}, u32[]{:S(2)}) collective-permute-start(bf16[32,3072]{1,0:T(8,128)(2,1)} %param.7), channel_id=1, source_target_pairs={{0,4},{2,6},{4,0},{6,2},{8,12},{10,14},{12,8},{14,10},{1,5},{3,7},... | collective-permute-start | bytes 589832 | tf_op jit(solution)/shard_map/ppermute | solution.py:62
  5.6 18.8 %collective-permute-start.3 = (bf16[32,3072]{1,0:T(8,128)(2,1)}, bf16[32,3072]{1,0:T(8,128)(2,1)S(1)}, u32[]{:S(2)}, u32[]{:S(2)}) collective-permute-start(bf16[32,3072]{1,0:T(8,128)(2,1)} %param.7), channel_id=1, source_target_pairs={{0,2},{2,0},{4,6},{6,4},{8,10},{10,8},{12,14},{14,12},{1,3},{3,1},... | collective-permute-start | bytes 589832 | tf_op jit(solution)/shard_map/ppermute | solution.py:56
  13.5 9.3 %collective-permute-start.2 = (bf16[32,3072]{1,0:T(8,128)(2,1)S(1)}, bf16[32,3072]{1,0:T(8,128)(2,1)S(1)}, u32[]{:S(2)}, u32[]{:S(2)}) collective-permute-start(bf16[32,3072]{1,0:T(8,128)(2,1)S(1)} %collective-permute-done.1.refs_2_), channel_id=1, source_target_pairs={{0,4},{2,6},{4,0},{6,2},{8,12},{10,14},{12,8},{14,10},{1,5},{3,7},... | collective-permute-start | bytes 589832 | tf_op jit(solution)/shard_map/ppermute | solution.py:62
  14.2 11.0 %collective-permute-start.5 = (bf16[32,3072]{1,0:T(8,128)(2,1)S(1)}, bf16[32,3072]{1,0:T(8,128)(2,1)S(1)}, u32[]{:S(2)}, u32[]{:S(2)}) collective-permute-start(bf16[32,3072]{1,0:T(8,128)(2,1)S(1)} %collective-permute-done.1.refs_2_), channel_id=1, source_target_pairs={{0,2},{2,0},{4,6},{6,4},{8,10},{10,8},{12,14},{14,12},{1,3},{3,1},... | collective-permute-start | bytes 589832 | tf_op jit(solution)/shard_map/ppermute | solution.py:56
  15.7 9.5 %collective-permute-start.4 = (bf16[32,3072]{1,0:T(8,128)(2,1)S(1)}, bf16[32,3072]{1,0:T(8,128)(2,1)S(1)}, u32[]{:S(2)}, u32[]{:S(2)}) collective-permute-start(bf16[32,3072]{1,0:T(8,128)(2,1)S(1)} %collective-permute-done.refs_1_), channel_id=1, source_target_pairs={{0,2},{2,0},{4,6},{6,4},{8,10},{10,8},{12,14},{14,12},{1,3},{3,1},... | collective-permute-start | bytes 589832 | tf_op jit(solution)/shard_map/ppermute | solution.py:56
  22.8 6.4 %collective-permute-start.6 = (bf16[32,3072]{1,0:T(8,128)(2,1)S(1)}, bf16[32,3072]{1,0:T(8,128)(2,1)S(1)}, u32[]{:S(2)}, u32[]{:S(2)}) collective-permute-start(bf16[32,3072]{1,0:T(8,128)(2,1)S(1)} %collective-permute-done.2), channel_id=1, source_target_pairs={{0,2},{2,0},{4,6},{6,4},{8,10},{10,8},{12,14},{14,12},{1,3},{3,1},... | collective-permute-start | bytes 589832 | tf_op jit(solution)/shard_map/ppermute | solution.py:56
  31.8 4.8 %collective-permute-start.8 = (f32[256,1536]{1,0:T(8,128)S(1)}, f32[256,1536]{1,0:T(8,128)S(1)}, u32[]{:S(2)}, u32[]{:S(2)}) collective-permute-start(f32[256,1536]{1,0:T(8,128)S(1)} %shard_map.75.own_ref), channel_id=1, source_target_pairs={{0,1},{1,0},{2,3},{3,2},{4,5},{5,4},{6,7},{7,6},{8,9},{9,8},{10,11... | collective-permute-start | bytes 4718600 | tf_op jit(solution)/shard_map/ppermute | solution.py:293
  34.5 8.6 %collective-permute-start.7 = (f32[256,1536]{1,0:T(8,128)S(1)}, f32[256,1536]{1,0:T(8,128)S(1)}, u32[]{:S(2)}, u32[]{:S(2)}) collective-permute-start(f32[256,1536]{1,0:T(8,128)S(1)} %get-tuple-element.22.own_ref), channel_id=1, source_target_pairs={{0,1},{1,0},{2,3},{3,2},{4,5},{5,4},{6,7},{7,6},{8,9},{9,8},{10,11... | collective-permute-start | bytes 4718600 | tf_op jit(solution)/shard_map/ppermute | solution.py:293
  35.6 0.9 %copy-start = (f32[8,3072]{1,0:T(8,128)S(1)}, f32[8,3072]{1,0:T(8,128)}, u32[]{:S(2)}) copy-start(f32[8,3072]{1,0:T(8,128)} %param.11) | copy-start | bytes 294916
  44.3 8.6 %collective-permute-start.15 = (bf16[2,32,768]{2,1,0:T(8,128)(2,1)S(1)}, bf16[2,32,768]{2,1,0:T(8,128)(2,1)S(1)}, u32[]{:S(2)}, u32[]{:S(2)}) collective-permute-start(bf16[2,32,768]{2,1,0:T(8,128)(2,1)S(1)} %get-tuple-element.35), channel_id=1, source_target_pairs={{0,12},{2,14},{4,8},{6,10},{8,4},{10,6},{12,0},{14,2},{1,13},{3,15... | collective-permute-start | bytes 294920 | tf_op jit(solution)/shard_map/ppermute | solution.py:62
  47.4 9.6 %collective-permute-start.16 = (bf16[2,32,768]{2,1,0:T(8,128)(2,1)S(1)}, bf16[2,32,768]{2,1,0:T(8,128)(2,1)S(1)}, u32[]{:S(2)}, u32[]{:S(2)}) collective-permute-start(bf16[2,32,768]{2,1,0:T(8,128)(2,1)S(1)} %get-tuple-element.36), channel_id=1, source_target_pairs={{0,8},{2,10},{4,12},{6,14},{8,0},{10,2},{12,4},{14,6},{1,9},{3,11}... | collective-permute-start | bytes 294920 | tf_op jit(solution)/shard_map/ppermute | solution.py:62
  47.7 9.2 %collective-permute-start.17 = (bf16[2,32,768]{2,1,0:T(8,128)(2,1)S(1)}, bf16[2,32,768]{2,1,0:T(8,128)(2,1)S(1)}, u32[]{:S(2)}, u32[]{:S(2)}) collective-permute-start(bf16[2,32,768]{2,1,0:T(8,128)(2,1)S(1)} %get-tuple-element.37), channel_id=1, source_target_pairs={{0,4},{2,6},{4,0},{6,2},{8,12},{10,14},{12,8},{14,10},{1,5},{3,7},... | collective-permute-start | bytes 294920 | tf_op jit(solution)/shard_map/ppermute | solution.py:62
  50.8 7.8 %collective-permute-start.9 = (bf16[32,2304]{1,0:T(8,128)(2,1)S(1)}, bf16[32,2304]{1,0:T(8,128)(2,1)S(1)}, u32[]{:S(2)}, u32[]{:S(2)}) collective-permute-start(bf16[32,2304]{1,0:T(8,128)(2,1)S(1)} %get-tuple-element.29), channel_id=1, source_target_pairs={{0,2},{2,0},{4,6},{6,4},{8,10},{10,8},{12,14},{14,12},{1,3},{3,1},... | collective-permute-start | bytes 442376 | tf_op jit(solution)/shard_map/ppermute | solution.py:56
  52.4 9.0 %collective-permute-start.11 = (bf16[32,2304]{1,0:T(8,128)(2,1)S(1)}, bf16[32,2304]{1,0:T(8,128)(2,1)S(1)}, u32[]{:S(2)}, u32[]{:S(2)}) collective-permute-start(bf16[32,2304]{1,0:T(8,128)(2,1)S(1)} %get-tuple-element.31), channel_id=1, source_target_pairs={{0,2},{2,0},{4,6},{6,4},{8,10},{10,8},{12,14},{14,12},{1,3},{3,1},... | collective-permute-start | bytes 442376 | tf_op jit(solution)/shard_map/ppermute | solution.py:56
  52.9 11.1 %collective-permute-start.13 = (bf16[32,2304]{1,0:T(8,128)(2,1)S(1)}, bf16[32,2304]{1,0:T(8,128)(2,1)S(1)}, u32[]{:S(2)}, u32[]{:S(2)}) collective-permute-start(bf16[32,2304]{1,0:T(8,128)(2,1)S(1)} %get-tuple-element.33), channel_id=1, source_target_pairs={{0,2},{2,0},{4,6},{6,4},{8,10},{10,8},{12,14},{14,12},{1,3},{3,1},... | collective-permute-start | bytes 442376 | tf_op jit(solution)/shard_map/ppermute | solution.py:56
  57.0 15.8 %collective-permute-start.18 = (bf16[32,3072]{1,0:T(8,128)(2,1)S(1)}, bf16[32,3072]{1,0:T(8,128)(2,1)S(1)}, u32[]{:S(2)}, u32[]{:S(2)}) collective-permute-start(bf16[32,3072]{1,0:T(8,128)(2,1)S(1)} %pad_maximum_fusion), channel_id=1, source_target_pairs={{0,2},{2,0},{4,6},{6,4},{8,10},{10,8},{12,14},{14,12},{1,3},{3,1},... | collective-permute-start | bytes 589832 | tf_op jit(solution)/shard_map/ppermute | solution.py:56
  58.7 8.7 %collective-permute-start.10 = (bf16[32,2304]{1,0:T(8,128)(2,1)S(1)}, bf16[32,2304]{1,0:T(8,128)(2,1)S(1)}, u32[]{:S(2)}, u32[]{:S(2)}) collective-permute-start(bf16[32,2304]{1,0:T(8,128)(2,1)S(1)} %add_convert_fusion.2), channel_id=1, source_target_pairs={{0,12},{2,14},{4,8},{6,10},{8,4},{10,6},{12,0},{14,2},{1,13},{3,15... | collective-permute-start | bytes 442376 | tf_op jit(solution)/shard_map/ppermute | solution.py:62
  61.4 11.4 %collective-permute-start.12 = (bf16[32,2304]{1,0:T(8,128)(2,1)S(1)}, bf16[32,2304]{1,0:T(8,128)(2,1)S(1)}, u32[]{:S(2)}, u32[]{:S(2)}) collective-permute-start(bf16[32,2304]{1,0:T(8,128)(2,1)S(1)} %add_convert_fusion.1), channel_id=1, source_target_pairs={{0,8},{2,10},{4,12},{6,14},{8,0},{10,2},{12,4},{14,6},{1,9},{3,11}... | collective-permute-start | bytes 442376 | tf_op jit(solution)/shard_map/ppermute | solution.py:62
  64.0 8.8 %collective-permute-start.14 = (bf16[32,2304]{1,0:T(8,128)(2,1)S(1)}, bf16[32,2304]{1,0:T(8,128)(2,1)S(1)}, u32[]{:S(2)}, u32[]{:S(2)}) collective-permute-start(bf16[32,2304]{1,0:T(8,128)(2,1)S(1)} %add_convert_fusion), channel_id=1, source_target_pairs={{0,4},{2,6},{4,0},{6,2},{8,12},{10,14},{12,8},{14,10},{1,5},{3,7},... | collective-permute-start | bytes 442376 | tf_op jit(solution)/shard_map/ppermute | solution.py:62

commit v4 on v3

--- a/solution.py
+++ b/solution.py
@@ -109,44 +109,34 @@
     )(w, *after)
 
 
-def up_kernel(start, x_ref, w_ref, out_ref):
+def up_kernel(start, x_ref, w_ref, out_ref, sent_ref):
     for lo in range(0, out_ref.shape[1], TILE):
         at = slice(start + lo, start + lo + TILE)
-        out_ref[:, lo : lo + TILE] = dot(x_ref[...], w_ref[:, at])
-
-
-def up(x, w, start, count):
-    rows = x.shape[0]
-    return pl.pallas_call(
-        lambda *refs: up_kernel(start, *refs),
-        in_specs=[VMEM] * 2,
-        out_specs=VMEM,
-        out_shape=jax.ShapeDtypeStruct((rows, count), jnp.float32),
-        compiler_params=params(2),
-        cost_estimate=pl.CostEstimate(
-            flops=2 * rows * w.shape[0] * count, bytes_accessed=4 * rows * count, transcendentals=0
-        ),
-    )(x, w)
-
-
-def up_and_load_kernel(start, x_ref, w_ref, next_ref, out_ref, held_ref, sem):
+        out = slice(lo, lo + TILE)
+        terms = dot(x_ref[...], w_ref[:, at])
+        out_ref[:, out] = terms
+        sent_ref[:, out] = terms.astype(jnp.bfloat16)
+
+
+def up_and_load_kernel(start, x_ref, w_ref, next_ref, out_ref, sent_ref, held_ref, sem):
     rows, width = held_ref.shape
     moving = pltpu.make_async_copy(
-        next_ref.at[pl.ds(0, rows), pl.ds(0, width)], held_ref, sem
+        next_ref.at[pl.ds(0, rows), pl.ds(start, width)], held_ref, sem
     )
     moving.start()
-    up_kernel(start, x_ref, w_ref, out_ref)
+    up_kernel(start, x_ref, w_ref, out_ref, sent_ref)
     moving.wait()
 
 
-def up_and_load(x, w, start, count, w_next, held):
+def up(x, w, start, count, w_next, held):
     rows = x.shape[0]
     return pl.pallas_call(
         lambda *refs: up_and_load_kernel(start, *refs),
         in_specs=[VMEM, VMEM, HBM],
-        out_specs=[VMEM] * 2,
+        out_specs=[VMEM] * 3,
         out_shape=[
             jax.ShapeDtypeStruct((rows, count), jnp.float32),
+            jax.ShapeDtypeStruct((rows, count), jnp.bfloat16),
             pltpu.VMEM(held, w_next.dtype),
         ],
         scratch_shapes=[pltpu.SemaphoreType.DMA],
@@ -160,38 +150,31 @@
 def activate(own_ref, other_ref, scale_ref, hidden_ref):
     for lo in range(0, hidden_ref.shape[1], TILE):
         at = slice(lo, lo + TILE)
-        v = (own_ref[:, at] + other_ref[:, at]) * scale_ref[:, at]
+        v = (own_ref[:, at] + other_ref[:, at].astype(jnp.float32)) * scale_ref[:, at]
         inner = math.sqrt(2 / math.pi) * (v + 0.044715 * (v * v * v))
         hidden_ref[:, at] = (0.5 * v * (1 + jnp.tanh(inner))).astype(hidden_ref.dtype)
 
 
 def down_first_kernel(
-    own_ref, other_ref, scale_ref, held_ref, w_ref, out_ref, next_ref, hidden_ref, rest_ref, sems
+    own_ref, other_ref, scale_ref, left_ref, right_ref, w_ref, out_ref, next_ref, hidden_ref, sems
 ):
-    rows, width = held_ref.shape
-    rest = pltpu.make_async_copy(
-        w_ref.at[pl.ds(0, rows), pl.ds(width, rest_ref.shape[1])], rest_ref, sems.at[0]
-    )
-    step = next_ref.shape[0] // 2
-    following = [
+    rows, width = left_ref.shape
+    step = next_ref.shape[0] // 4
+    moving = [
         pltpu.make_async_copy(
-            w_ref.at[pl.ds(rows + i * step, step)], next_ref.at[pl.ds(i * step, step)], sems.at[1 + i]
+            w_ref.at[pl.ds(rows + i * step, step)], next_ref.at[pl.ds(i * step, step)], sems.at[i]
         )
-        for i in range(2)
+        for i in range(4)
     ]
-    rest.start()
-    for c in following:
+    for c in moving:
         c.start()
     activate(own_ref, other_ref, scale_ref, hidden_ref)
-    for lo in range(0, width, TILE):
-        at = slice(lo, lo + TILE)
-        out_ref[:, at] = dot(hidden_ref[...], held_ref[:, at])
-    rest.wait()
-    for lo in range(0, rest_ref.shape[1], TILE):
-        out_ref[:, width + lo : width + lo + TILE] = dot(
-            hidden_ref[...], rest_ref[:, lo : lo + TILE]
-        )
-    for c in following:
+    for i, ref in enumerate((left_ref, right_ref)):
+        for lo in range(0, width, TILE):
+            out_ref[:, i * width + lo : i * width + lo + TILE] = dot(
+                hidden_ref[...], ref[:, lo : lo + TILE]
+            )
+    for c in moving:
         c.wait()
 
 
@@ -201,12 +184,12 @@
     )
 
 
-def down_first(own, other, scale, held, w):
+def down_first(own, other, scale, left, right, w):
     rows, count = own.shape
     width = w.shape[1]
     return pl.pallas_call(
         down_first_kernel,
-        in_specs=[VMEM] * 4 + [HBM],
+        in_specs=[VMEM] * 5 + [HBM],
         out_specs=[VMEM] * 2,
         out_shape=[
             jax.ShapeDtypeStruct((rows, width), jnp.float32),
@@ -214,12 +197,11 @@
         ],
         scratch_shapes=[
             pltpu.VMEM((rows, count), jnp.bfloat16),
-            pltpu.VMEM((count, width - held.shape[1]), jnp.bfloat16),
-            pltpu.SemaphoreType.DMA((3,)),
+            pltpu.SemaphoreType.DMA((4,)),
         ],
-        compiler_params=params(8),
+        compiler_params=params(2),
         cost_estimate=cost(rows, count, width),
-    )(own, other, scale, held, w)
+    )(own, other, scale, left, right, w)
 
 
 def over_z_kernel(
@@ -315,12 +297,12 @@
     )
 
     count = w_up.shape[1] // 2
-    first = up(full, up_held, 0, count)
-    second, down_held = up_and_load(full, up_held, count, count, w_down, (count, count))
-    pre = [first, second]
-    other = [swap_cores(p) for p in pre]
+    pre, sent, down_held = zip(
+        *[up(full, up_held, i * count, count, w_down, (count, count)) for i in range(2)]
+    )
+    other = [swap_cores(x) for x in sent]
     width = w_down.shape[1] * 3 // 4 // 128 * 128
-    total, down_rest = down_first(pre[0], other[0], scale_one[:, :count], down_held, w_down)
+    total, down_rest = down_first(pre[0], other[0], scale_one[:, :count], *down_held, w_down)
     a_kept, *a_sent, hidden = over_z_terms(
         pre[1], other[1], scale_one[:, count:], down_rest, total, w_down.shape[1] - width
     )

time: 74 us -> 71 us (0.959)
  Pallas kernels: 21.4 us -> 19.7 us
  waiting for transfers between devices: 16.8 us -> 15.7 us
  other arithmetic: 4.29 us -> 5.2 us
    pallas_call x3, Pallas kernels: 11.7 us -> 9.89 us  [the longest x2 5.22 us: up(): pl.pallas_call(lambda *refs: up_and_load_kernel(start, *refs), in_specs=[...]
    ppermute x9, waiting for transfers between devices: 11.4 us -> 10.3 us  [move_z(): lax.ppermute(x, 'fin', [(z * 2 + y, (z ^ k) * 2 + y) for z in range(4) fo...]
    another operation x2, other arithmetic: 0.94 us -> 1.83 us
    unnamed x9 -> x7, local copies, waits for them, and re-layouts: 1.7 us -> 1.06 us
  transfers between devices with their start and end apart: 19 -> 19, of which waited for: 7 -> 6; matrix products, arithmetic and copies ran while one was open for 9% -> 10% of each run, Pallas kernels for 24% -> 22%
where the time goes in v4:
time: 71 us; the launch traced here: 70.7 us
  starting transfers between devices  26.9 us (38%)
  Pallas kernels  19.7 us (28%)
  waiting for transfers between devices  15.7 us (22%)
  other arithmetic  5.2 us (7%)
  matrix products  1.54 us (2%)
  local copies, waits for them, and re-layouts  1.46 us (2%)
    ppermute x9, starting transfers between devices, move_z(): lax.ppermute(x, 'fin', [(z * 2 + y, (z ^ k) * 2 + y) for z in range(4) fo...  16.2 us
    ppermute x9, waiting for transfers between devices, move_z(): lax.ppermute(x, 'fin', [(z * 2 + y, (z ^ k) * 2 + y) for z in range(4) fo...  10.3 us
    ppermute x8, starting transfers between devices, move_y(): lax.ppermute(x, 'fin', [(z * 2 + y, z * 2 + 1 - y) for z in range(4) for...  10.1 us
    pallas_call x1, Pallas kernels, load(): pl.pallas_call(load_kernel, in_specs=[HBM] + [ANY] * len(after), out_spec...  6.5 us
    ppermute x8, waiting for transfers between devices, move_y(): lax.ppermute(x, 'fin', [(z * 2 + y, z * 2 + 1 - y) for z in range(4) for...  5.38 us
    pallas_call x2, Pallas kernels, up(): pl.pallas_call(lambda *refs: up_and_load_kernel(start, *refs), in_specs=[...  5.22 us
    pallas_call x1, Pallas kernels, down_first(): pl.pallas_call(down_first_kernel, in_specs=[VMEM] * 5 + [HBM], out_specs=...  4.67 us
    pallas_call x1, Pallas kernels, over_y_terms(): pl.pallas_call(over_y_kernel, in_specs=[VMEM] * 3, out_specs=[VMEM] * 8,...  2.01 us
  transfers between devices with their start and end apart: 19, of which 6 were waited for; matrix products, arithmetic and copies ran while one was open for 10% of the time, Pallas kernels for 22%

profile of v4, /device:TPU:0, one launch (start us, length us, event | category | flops | bytes accessed | tf_op | source)
XLA Modules:
  0.0 70.7 jit_solution(5037920390260498690)
XLA Ops:
  0.0 4.0 %collective-permute-start.1 = (bf16[32,3072]{1,0:T(8,128)(2,1)}, bf16[32,3072]{1,0:T(8,128)(2,1)S(1)}, u32[]{:S(2)}, u32[]{:S(2)}) collective-permute-start(bf16[32,3072]{1,0:T(8,128)(2,1)} %param.7), channel_id=1, source_target_pairs={{0,8},{2,10},{4,12},{6,14},{8,0},{10,2},{12,4},{14,6},{1,9},{3,11}... | collective-permute-start | bytes 589832 | tf_op jit(solution)/shard_map/ppermute | solution.py:62
  4.0 1.6 %collective-permute-start = (bf16[32,3072]{1,0:T(8,128)(2,1)}, bf16[32,3072]{1,0:T(8,128)(2,1)S(1)}, u32[]{:S(2)}, u32[]{:S(2)}) collective-permute-start(bf16[32,3072]{1,0:T(8,128)(2,1)} %param.7), channel_id=1, source_target_pairs={{0,4},{2,6},{4,0},{6,2},{8,12},{10,14},{12,8},{14,10},{1,5},{3,7},... | collective-permute-start | bytes 589832 | tf_op jit(solution)/shard_map/ppermute | solution.py:62
  5.6 1.5 %collective-permute-start.3 = (bf16[32,3072]{1,0:T(8,128)(2,1)}, bf16[32,3072]{1,0:T(8,128)(2,1)S(1)}, u32[]{:S(2)}, u32[]{:S(2)}) collective-permute-start(bf16[32,3072]{1,0:T(8,128)(2,1)} %param.7), channel_id=1, source_target_pairs={{0,2},{2,0},{4,6},{6,4},{8,10},{10,8},{12,14},{14,12},{1,3},{3,1},... | collective-permute-start | bytes 589832 | tf_op jit(solution)/shard_map/ppermute | solution.py:56
  7.1 1.0 %constant_dynamic-update-slice_fusion.7 = bf16[256,3072]{1,0:T(8,128)(2,1)S(1)} fusion(bf16[32,3072]{1,0:T(8,128)(2,1)} %param.7), kind=kLoop, calls=%fused_computation.41 | loop fusion | bytes 393216
  14.4 1.3 %collective-permute-start.5 = (bf16[32,3072]{1,0:T(8,128)(2,1)S(1)}, bf16[32,3072]{1,0:T(8,128)(2,1)S(1)}, u32[]{:S(2)}, u32[]{:S(2)}) collective-permute-start(bf16[32,3072]{1,0:T(8,128)(2,1)S(1)} %collective-permute-done.1.refs_2_), channel_id=1, source_target_pairs={{0,2},{2,0},{4,6},{6,4},{8,10},{10,8},{12,14},{14,12},{1,3},{3,1},... | collective-permute-start | bytes 589832 | tf_op jit(solution)/shard_map/ppermute | solution.py:56
  16.5 6.5 %shard_map.73.refs_1_ = bf16[3072,3072]{1,0:T(8,128)(2,1)S(1)} custom-call(bf16[3072,3072]{1,0:T(8,128)(2,1)} %refs_0_.1, bf16[32,3072]{1,0:T(8,128)(2,1)S(1)} %collective-permute-done.refs_1_, bf16[32,3072]{1,0:T(8,128)(2,1)S(1)} %collective-permute-done.1.refs_2_), custom_call_target="tpu_custom_call" | custom-call | bytes 37748736 | tf_op jit(solution)/shard_map/pallas_call | solution.py:101
  23.0 1.3 %collective-permute-start.6 = (bf16[32,3072]{1,0:T(8,128)(2,1)S(1)}, bf16[32,3072]{1,0:T(8,128)(2,1)S(1)}, u32[]{:S(2)}, u32[]{:S(2)}) collective-permute-start(bf16[32,3072]{1,0:T(8,128)(2,1)S(1)} %collective-permute-done.2), channel_id=1, source_target_pairs={{0,2},{2,0},{4,6},{6,4},{8,10},{10,8},{12,14},{14,12},{1,3},{3,1},... | collective-permute-start | bytes 589832 | tf_op jit(solution)/shard_map/ppermute | solution.py:56
  25.3 3.9 %collective-permute-done.6 = bf16[32,3072]{1,0:T(8,128)(2,1)S(1)} collective-permute-done((bf16[32,3072]{1,0:T(8,128)(2,1)S(1)}, bf16[32,3072]{1,0:T(8,128)(2,1)S(1)}, u32[]{:S(2)}, u32[]{:S(2)}) %collective-permute-start.6) | collective-permute-done | bytes 196640 | tf_op jit(solution)/shard_map/ppermute | solution.py:56
  29.2 2.6 %shard_map.75 = (f32[256,1536]{1,0:T(8,128)S(1)}, bf16[256,1536]{1,0:T(8,128)(2,1)S(1)}, bf16[1536,1536]{1,0:T(8,128)(2,1)S(1)}) custom-call(bf16[256,3072]{1,0:T(8,128)(2,1)S(1)} %constant_dynamic-update-slice_fusion.refs_0_, bf16[3072,3072]{1,0:T(8,128)(2,1)S(1)} %shard_map.73.refs_1_, bf16[3072,3072]{1,0:T(8,128)(2,1)} %w_ref.1), custom_call_target="tpu_custom_call" | custom-call | flops 2415919104 | bytes 1572864 | tf_op jit(solution)/shard_map/pallas_call | solution.py:133
  31.9 2.6 %shard_map.74 = (f32[256,1536]{1,0:T(8,128)S(1)}, bf16[256,1536]{1,0:T(8,128)(2,1)S(1)}, bf16[1536,1536]{1,0:T(8,128)(2,1)S(1)}) custom-call(bf16[256,3072]{1,0:T(8,128)(2,1)S(1)} %constant_dynamic-update-slice_fusion.refs_0_, bf16[3072,3072]{1,0:T(8,128)(2,1)S(1)} %shard_map.73.refs_1_, bf16[3072,3072]{1,0:T(8,128)(2,1)} %w_ref.1), custom_call_target="tpu_custom_call" | custom-call | flops 2415919104 | bytes 1572864 | tf_op jit(solution)/shard_map/pallas_call | solution.py:133
  35.3 4.7 %shard_map.76 = (f32[256,3072]{1,0:T(8,128)S(1)}, bf16[1536,3072]{1,0:T(8,128)(2,1)S(1)}) custom-call(f32[256,1536]{1,0:T(8,128)S(1)} %get-tuple-element.28.own_ref, bf16[256,1536]{1,0:T(8,128)(2,1)S(1)} %collective-permute-done.8.other_ref, f32[256,1536]{1,0:T(8,128)S(1)} %get-tuple-element.47.scale_ref, bf16[1536,1536]{1,0:T(8,128)(2,1)S(1)} %get-tuple-element.30.left_ref, ...), custom_call_target="tpu_custom_call" | custom-call | flops 2415919104 | bytes 9437184 | tf_op jit(solution)/shard_map/pallas_call | solution.py:190
  40.0 1.3 %shard_map.77 = (f32[2,32,768]{2,1,0:T(8,128)S(1)}, bf16[2,32,768]{2,1,0:T(8,128)(2,1)S(1)}, bf16[2,32,768]{2,1,0:T(8,128)(2,1)S(1)}, bf16[2,32,768]{2,1,0:T(8,128)(2,1)S(1)}, bf16[256,1536]{1,0:T(8,128)(2,1)S(1)}) custom-call(f32[256,1536]{1,0:T(8,128)S(1)} %get-tuple-element.26.own_ref, bf16[256,1536]{1,0:T(8,128)(2,1)S(1)} %collective-permute-done.7.other_ref, ...), custom_call_target="tpu_custom_call" | custom-call | flops 603979776 | bytes 2359296 | tf_op jit(solution)/shard_map/pallas_call | solution.py:231
  41.2 3.1 %collective-permute-start.15 = (bf16[2,32,768]{2,1,0:T(8,128)(2,1)S(1)}, bf16[2,32,768]{2,1,0:T(8,128)(2,1)S(1)}, u32[]{:S(2)}, u32[]{:S(2)}) collective-permute-start(bf16[2,32,768]{2,1,0:T(8,128)(2,1)S(1)} %get-tuple-element.43), channel_id=1, source_target_pairs={{0,12},{2,14},{4,8},{6,10},{8,4},{10,6},{12,0},{14,2},{1,13},{3,15... | collective-permute-start | bytes 294920 | tf_op jit(solution)/shard_map/ppermute | solution.py:62
  44.7 1.0 %collective-permute-start.17 = (bf16[2,32,768]{2,1,0:T(8,128)(2,1)S(1)}, bf16[2,32,768]{2,1,0:T(8,128)(2,1)S(1)}, u32[]{:S(2)}, u32[]{:S(2)}) collective-permute-start(bf16[2,32,768]{2,1,0:T(8,128)(2,1)S(1)} %get-tuple-element.45), channel_id=1, source_target_pairs={{0,4},{2,6},{4,0},{6,2},{8,12},{10,14},{12,8},{14,10},{1,5},{3,7},... | collective-permute-start | bytes 294920 | tf_op jit(solution)/shard_map/ppermute | solution.py:62
  45.7 2.0 %shard_map.78 = (f32[32,2304]{1,0:T(8,128)S(1)}, f32[32,2304]{1,0:T(8,128)S(1)}, f32[32,2304]{1,0:T(8,128)S(1)}, f32[32,2304]{1,0:T(8,128)S(1)}, bf16[32,2304]{1...) custom-call(bf16[256,1536]{1,0:T(8,128)(2,1)S(1)} %get-tuple-element., ...), custom_call_target="tpu_custom_call" | custom-call | flops 1811939328 | bytes 7077888 | tf_op jit(solution)/shard_map/pallas_call | solution.py:263
  47.7 1.6 %collective-permute-start.9 = (bf16[32,2304]{1,0:T(8,128)(2,1)S(1)}, bf16[32,2304]{1,0:T(8,128)(2,1)S(1)}, u32[]{:S(2)}, u32[]{:S(2)}) collective-permute-start(bf16[32,2304]{1,0:T(8,128)(2,1)S(1)} %get-tuple-element.37), channel_id=1, source_target_pairs={{0,2},{2,0},{4,6},{6,4},{8,10},{10,8},{12,14},{14,12},{1,3},{3,1},... | collective-permute-start | bytes 442376 | tf_op jit(solution)/shard_map/ppermute | solution.py:56
  49.8 1.5 %collective-permute-start.13 = (bf16[32,2304]{1,0:T(8,128)(2,1)S(1)}, bf16[32,2304]{1,0:T(8,128)(2,1)S(1)}, u32[]{:S(2)}, u32[]{:S(2)}) collective-permute-start(bf16[32,2304]{1,0:T(8,128)(2,1)S(1)} %get-tuple-element.41), channel_id=1, source_target_pairs={{0,2},{2,0},{4,6},{6,4},{8,10},{10,8},{12,14},{14,12},{1,3},{3,1},... | collective-permute-start | bytes 442376 | tf_op jit(solution)/shard_map/ppermute | solution.py:56
  51.3 2.6 %collective-permute-done.16 = bf16[2,32,768]{2,1,0:T(8,128)(2,1)S(1)} collective-permute-done((bf16[2,32,768]{2,1,0:T(8,128)(2,1)S(1)}, bf16[2,32,768]{2,1,0:T(8,128)(2,1)S(1)}, u32[]{:S(2)}, u32[]{:S(2)}) %collective-permute-start.16) | collective-permute-done | bytes 98336 | tf_op jit(solution)/shard_map/ppermute | solution.py:62
  54.0 1.6 %collective-permute-start.18 = (bf16[32,3072]{1,0:T(8,128)(2,1)S(1)}, bf16[32,3072]{1,0:T(8,128)(2,1)S(1)}, u32[]{:S(2)}, u32[]{:S(2)}) collective-permute-start(bf16[32,3072]{1,0:T(8,128)(2,1)S(1)} %pad_maximum_fusion), channel_id=1, source_target_pairs={{0,2},{2,0},{4,6},{6,4},{8,10},{10,8},{12,14},{14,12},{1,3},{3,1},... | collective-permute-start | bytes 589832 | tf_op jit(solution)/shard_map/ppermute | solution.py:56
  55.6 2.7 %collective-permute-start.10 = (bf16[32,2304]{1,0:T(8,128)(2,1)S(1)}, bf16[32,2304]{1,0:T(8,128)(2,1)S(1)}, u32[]{:S(2)}, u32[]{:S(2)}) collective-permute-start(bf16[32,2304]{1,0:T(8,128)(2,1)S(1)} %add_convert_fusion.2), channel_id=1, source_target_pairs={{0,12},{2,14},{4,8},{6,10},{8,4},{10,6},{12,0},{14,2},{1,13},{3,15... | collective-permute-start | bytes 442376 | tf_op jit(solution)/shard_map/ppermute | solution.py:62
  58.3 1.9 %collective-permute-start.12 = (bf16[32,2304]{1,0:T(8,128)(2,1)S(1)}, bf16[32,2304]{1,0:T(8,128)(2,1)S(1)}, u32[]{:S(2)}, u32[]{:S(2)}) collective-permute-start(bf16[32,2304]{1,0:T(8,128)(2,1)S(1)} %add_convert_fusion.1), channel_id=1, source_target_pairs={{0,8},{2,10},{4,12},{6,14},{8,0},{10,2},{12,4},{14,6},{1,9},{3,11}... | collective-permute-start | bytes 442376 | tf_op jit(solution)/shard_map/ppermute | solution.py:62
  60.9 1.1 %collective-permute-start.14 = (bf16[32,2304]{1,0:T(8,128)(2,1)S(1)}, bf16[32,2304]{1,0:T(8,128)(2,1)S(1)}, u32[]{:S(2)}, u32[]{:S(2)}) collective-permute-start(bf16[32,2304]{1,0:T(8,128)(2,1)S(1)} %add_convert_fusion), channel_id=1, source_target_pairs={{0,4},{2,6},{4,0},{6,2},{8,12},{10,14},{12,8},{14,10},{1,5},{3,7},... | collective-permute-start | bytes 442376 | tf_op jit(solution)/shard_map/ppermute | solution.py:62
  62.0 2.3 %collective-permute-done.10 = bf16[32,2304]{1,0:T(8,128)(2,1)S(1)} collective-permute-done((bf16[32,2304]{1,0:T(8,128)(2,1)S(1)}, bf16[32,2304]{1,0:T(8,128)(2,1)S(1)}, u32[]{:S(2)}, u32[]{:S(2)}) %collective-permute-start.10) | collective-permute-done | bytes 147488 | tf_op jit(solution)/shard_map/ppermute | solution.py:62
  64.3 5.4 %collective-permute-done.12 = bf16[32,2304]{1,0:T(8,128)(2,1)S(1)} collective-permute-done((bf16[32,2304]{1,0:T(8,128)(2,1)S(1)}, bf16[32,2304]{1,0:T(8,128)(2,1)S(1)}, u32[]{:S(2)}, u32[]{:S(2)}) %collective-permute-start.12) | collective-permute-done | bytes 147488 | tf_op jit(solution)/shard_map/ppermute | solution.py:62
  (54 shorter events, 11.5 us)
Async XLA Ops:
  0.0 13.9 %collective-permute-start.1 = (bf16[32,3072]{1,0:T(8,128)(2,1)}, bf16[32,3072]{1,0:T(8,128)(2,1)S(1)}, u32[]{:S(2)}, u32[]{:S(2)}) collective-permute-start(bf16[32,3072]{1,0:T(8,128)(2,1)} %param.7), channel_id=1, source_target_pairs={{0,8},{2,10},{4,12},{6,14},{8,0},{10,2},{12,4},{14,6},{1,9},{3,11}... | collective-permute-start | bytes 589832 | tf_op jit(solution)/shard_map/ppermute | solution.py:62
  4.0 11.7 %collective-permute-start = (bf16[32,3072]{1,0:T(8,128)(2,1)}, bf16[32,3072]{1,0:T(8,128)(2,1)S(1)}, u32[]{:S(2)}, u32[]{:S(2)}) collective-permute-start(bf16[32,3072]{1,0:T(8,128)(2,1)} %param.7), channel_id=1, source_target_pairs={{0,4},{2,6},{4,0},{6,2},{8,12},{10,14},{12,8},{14,10},{1,5},{3,7},... | collective-permute-start | bytes 589832 | tf_op jit(solution)/shard_map/ppermute | solution.py:62
  5.6 18.8 %collective-permute-start.3 = (bf16[32,3072]{1,0:T(8,128)(2,1)}, bf16[32,3072]{1,0:T(8,128)(2,1)S(1)}, u32[]{:S(2)}, u32[]{:S(2)}) collective-permute-start(bf16[32,3072]{1,0:T(8,128)(2,1)} %param.7), channel_id=1, source_target_pairs={{0,2},{2,0},{4,6},{6,4},{8,10},{10,8},{12,14},{14,12},{1,3},{3,1},... | collective-permute-start | bytes 589832 | tf_op jit(solution)/shard_map/ppermute | solution.py:56
  13.9 9.1 %collective-permute-start.2 = (bf16[32,3072]{1,0:T(8,128)(2,1)S(1)}, bf16[32,3072]{1,0:T(8,128)(2,1)S(1)}, u32[]{:S(2)}, u32[]{:S(2)}) collective-permute-start(bf16[32,3072]{1,0:T(8,128)(2,1)S(1)} %collective-permute-done.1.refs_2_), channel_id=1, source_target_pairs={{0,4},{2,6},{4,0},{6,2},{8,12},{10,14},{12,8},{14,10},{1,5},{3,7},... | collective-permute-start | bytes 589832 | tf_op jit(solution)/shard_map/ppermute | solution.py:62
  14.4 10.8 %collective-permute-start.5 = (bf16[32,3072]{1,0:T(8,128)(2,1)S(1)}, bf16[32,3072]{1,0:T(8,128)(2,1)S(1)}, u32[]{:S(2)}, u32[]{:S(2)}) collective-permute-start(bf16[32,3072]{1,0:T(8,128)(2,1)S(1)} %collective-permute-done.1.refs_2_), channel_id=1, source_target_pairs={{0,2},{2,0},{4,6},{6,4},{8,10},{10,8},{12,14},{14,12},{1,3},{3,1},... | collective-permute-start | bytes 589832 | tf_op jit(solution)/shard_map/ppermute | solution.py:56
  15.7 9.5 %collective-permute-start.4 = (bf16[32,3072]{1,0:T(8,128)(2,1)S(1)}, bf16[32,3072]{1,0:T(8,128)(2,1)S(1)}, u32[]{:S(2)}, u32[]{:S(2)}) collective-permute-start(bf16[32,3072]{1,0:T(8,128)(2,1)S(1)} %collective-permute-done.refs_1_), channel_id=1, source_target_pairs={{0,2},{2,0},{4,6},{6,4},{8,10},{10,8},{12,14},{14,12},{1,3},{3,1},... | collective-permute-start | bytes 589832 | tf_op jit(solution)/shard_map/ppermute | solution.py:56
  23.0 6.1 %collective-permute-start.6 = (bf16[32,3072]{1,0:T(8,128)(2,1)S(1)}, bf16[32,3072]{1,0:T(8,128)(2,1)S(1)}, u32[]{:S(2)}, u32[]{:S(2)}) collective-permute-start(bf16[32,3072]{1,0:T(8,128)(2,1)S(1)} %collective-permute-done.2), channel_id=1, source_target_pairs={{0,2},{2,0},{4,6},{6,4},{8,10},{10,8},{12,14},{14,12},{1,3},{3,1},... | collective-permute-start | bytes 589832 | tf_op jit(solution)/shard_map/ppermute | solution.py:56
  31.8 3.5 %collective-permute-start.8 = (bf16[256,1536]{1,0:T(8,128)(2,1)S(1)}, bf16[256,1536]{1,0:T(8,128)(2,1)S(1)}, u32[]{:S(2)}, u32[]{:S(2)}) collective-permute-start(bf16[256,1536]{1,0:T(8,128)(2,1)S(1)} %get-tuple-element.29), channel_id=1, source_target_pairs={{0,1},{1,0},{2,3},{3,2},{4,5},{5,4},{6,7},{7,6},{8,9},{9,8},{10,11... | collective-permute-start | bytes 2359304 | tf_op jit(solution)/shard_map/ppermute | solution.py:275
  34.5 5.5 %collective-permute-start.7 = (bf16[256,1536]{1,0:T(8,128)(2,1)S(1)}, bf16[256,1536]{1,0:T(8,128)(2,1)S(1)}, u32[]{:S(2)}, u32[]{:S(2)}) collective-permute-start(bf16[256,1536]{1,0:T(8,128)(2,1)S(1)} %get-tuple-element.27), channel_id=1, source_target_pairs={{0,1},{1,0},{2,3},{3,2},{4,5},{5,4},{6,7},{7,6},{8,9},{9,8},{10,11... | collective-permute-start | bytes 2359304 | tf_op jit(solution)/shard_map/ppermute | solution.py:275
  41.2 8.6 %collective-permute-start.15 = (bf16[2,32,768]{2,1,0:T(8,128)(2,1)S(1)}, bf16[2,32,768]{2,1,0:T(8,128)(2,1)S(1)}, u32[]{:S(2)}, u32[]{:S(2)}) collective-permute-start(bf16[2,32,768]{2,1,0:T(8,128)(2,1)S(1)} %get-tuple-element.43), channel_id=1, source_target_pairs={{0,12},{2,14},{4,8},{6,10},{8,4},{10,6},{12,0},{14,2},{1,13},{3,15... | collective-permute-start | bytes 294920 | tf_op jit(solution)/shard_map/ppermute | solution.py:62
  44.3 9.6 %collective-permute-start.16 = (bf16[2,32,768]{2,1,0:T(8,128)(2,1)S(1)}, bf16[2,32,768]{2,1,0:T(8,128)(2,1)S(1)}, u32[]{:S(2)}, u32[]{:S(2)}) collective-permute-start(bf16[2,32,768]{2,1,0:T(8,128)(2,1)S(1)} %get-tuple-element.44), channel_id=1, source_target_pairs={{0,8},{2,10},{4,12},{6,14},{8,0},{10,2},{12,4},{14,6},{1,9},{3,11}... | collective-permute-start | bytes 294920 | tf_op jit(solution)/shard_map/ppermute | solution.py:62
  44.7 9.2 %collective-permute-start.17 = (bf16[2,32,768]{2,1,0:T(8,128)(2,1)S(1)}, bf16[2,32,768]{2,1,0:T(8,128)(2,1)S(1)}, u32[]{:S(2)}, u32[]{:S(2)}) collective-permute-start(bf16[2,32,768]{2,1,0:T(8,128)(2,1)S(1)} %get-tuple-element.45), channel_id=1, source_target_pairs={{0,4},{2,6},{4,0},{6,2},{8,12},{10,14},{12,8},{14,10},{1,5},{3,7},... | collective-permute-start | bytes 294920 | tf_op jit(solution)/shard_map/ppermute | solution.py:62
  47.7 7.9 %collective-permute-start.9 = (bf16[32,2304]{1,0:T(8,128)(2,1)S(1)}, bf16[32,2304]{1,0:T(8,128)(2,1)S(1)}, u32[]{:S(2)}, u32[]{:S(2)}) collective-permute-start(bf16[32,2304]{1,0:T(8,128)(2,1)S(1)} %get-tuple-element.37), channel_id=1, source_target_pairs={{0,2},{2,0},{4,6},{6,4},{8,10},{10,8},{12,14},{14,12},{1,3},{3,1},... | collective-permute-start | bytes 442376 | tf_op jit(solution)/shard_map/ppermute | solution.py:56
  49.3 9.0 %collective-permute-start.11 = (bf16[32,2304]{1,0:T(8,128)(2,1)S(1)}, bf16[32,2304]{1,0:T(8,128)(2,1)S(1)}, u32[]{:S(2)}, u32[]{:S(2)}) collective-permute-start(bf16[32,2304]{1,0:T(8,128)(2,1)S(1)} %get-tuple-element.39), channel_id=1, source_target_pairs={{0,2},{2,0},{4,6},{6,4},{8,10},{10,8},{12,14},{14,12},{1,3},{3,1},... | collective-permute-start | bytes 442376 | tf_op jit(solution)/shard_map/ppermute | solution.py:56
  49.8 11.1 %collective-permute-start.13 = (bf16[32,2304]{1,0:T(8,128)(2,1)S(1)}, bf16[32,2304]{1,0:T(8,128)(2,1)S(1)}, u32[]{:S(2)}, u32[]{:S(2)}) collective-permute-start(bf16[32,2304]{1,0:T(8,128)(2,1)S(1)} %get-tuple-element.41), channel_id=1, source_target_pairs={{0,2},{2,0},{4,6},{6,4},{8,10},{10,8},{12,14},{14,12},{1,3},{3,1},... | collective-permute-start | bytes 442376 | tf_op jit(solution)/shard_map/ppermute | solution.py:56
  54.0 15.8 %collective-permute-start.18 = (bf16[32,3072]{1,0:T(8,128)(2,1)S(1)}, bf16[32,3072]{1,0:T(8,128)(2,1)S(1)}, u32[]{:S(2)}, u32[]{:S(2)}) collective-permute-start(bf16[32,3072]{1,0:T(8,128)(2,1)S(1)} %pad_maximum_fusion), channel_id=1, source_target_pairs={{0,2},{2,0},{4,6},{6,4},{8,10},{10,8},{12,14},{14,12},{1,3},{3,1},... | collective-permute-start | bytes 589832 | tf_op jit(solution)/shard_map/ppermute | solution.py:56
  55.6 8.7 %collective-permute-start.10 = (bf16[32,2304]{1,0:T(8,128)(2,1)S(1)}, bf16[32,2304]{1,0:T(8,128)(2,1)S(1)}, u32[]{:S(2)}, u32[]{:S(2)}) collective-permute-start(bf16[32,2304]{1,0:T(8,128)(2,1)S(1)} %add_convert_fusion.2), channel_id=1, source_target_pairs={{0,12},{2,14},{4,8},{6,10},{8,4},{10,6},{12,0},{14,2},{1,13},{3,15... | collective-permute-start | bytes 442376 | tf_op jit(solution)/shard_map/ppermute | solution.py:62
  58.3 11.4 %collective-permute-start.12 = (bf16[32,2304]{1,0:T(8,128)(2,1)S(1)}, bf16[32,2304]{1,0:T(8,128)(2,1)S(1)}, u32[]{:S(2)}, u32[]{:S(2)}) collective-permute-start(bf16[32,2304]{1,0:T(8,128)(2,1)S(1)} %add_convert_fusion.1), channel_id=1, source_target_pairs={{0,8},{2,10},{4,12},{6,14},{8,0},{10,2},{12,4},{14,6},{1,9},{3,11}... | collective-permute-start | bytes 442376 | tf_op jit(solution)/shard_map/ppermute | solution.py:62
  60.9 8.8 %collective-permute-start.14 = (bf16[32,2304]{1,0:T(8,128)(2,1)S(1)}, bf16[32,2304]{1,0:T(8,128)(2,1)S(1)}, u32[]{:S(2)}, u32[]{:S(2)}) collective-permute-start(bf16[32,2304]{1,0:T(8,128)(2,1)S(1)} %add_convert_fusion), channel_id=1, source_target_pairs={{0,4},{2,6},{4,0},{6,2},{8,12},{10,14},{12,8},{14,10},{1,5},{3,7},... | collective-permute-start | bytes 442376 | tf_op jit(solution)/shard_map/ppermute | solution.py:62

commit v5 on v4

--- a/solution.py
+++ b/solution.py
@@ -291,9 +291,11 @@
     w_down = pltpu.with_memory_space_constraint(w_down, pltpu.HBM)
     two, one, across = move_z(tokens, 2), move_z(tokens, 1), move_y(tokens)
     up_held = load(w_up, [one, two])
-    one_across, two_across, three = move_y(one), move_y(two), move_z(two, 1)
+    two_across, one_across, three = move_y(two), move_y(one), move_z(two, 1)
+    half_rows = own_rows // 2
+    three_across = [move_y(three[:half_rows]), move_z(two_across[half_rows:], 1)]
     full = jnp.concatenate(
-        [tokens, one, two, three, across, one_across, two_across, move_y(three)]
+        [tokens, one, two, three, across, one_across, two_across, *three_across]
     )
 
     count = w_up.shape[1] // 2
@@ -309,9 +311,9 @@
     b_terms = over_y_terms(hidden, down_rest, total, width)
     b_kept, b_last, b_sent = b_terms[:4], b_terms[4], b_terms[5:]
 
-    a_moved = [move_z(a_sent[k - 1], k) for k in (3, 2, 1)]
-    b_across = [move_y(b_sent[k - 1]) for k in (3, 2, 1)]
-    b_moved = [move_z((b_kept[k] + wide(b_across[3 - k])).astype(half), k) for k in (3, 2, 1)]
+    a_moved = [move_z(a_sent[k - 1], k) for k in (2, 3, 1)]
+    b_across = [move_y(b_sent[k - 1]) for k in (2, 3, 1)]
+    b_moved = [move_z((b_kept[k] + wide(b_across[(2, 3, 1).index(k)])).astype(half), k) for k in (2, 3, 1)]
     a_sum = a_kept + wide(a_moved[0]) + wide(a_moved[1]) + wide(a_moved[2])
     last = move_y(jnp.concatenate([b_last, a_sum[1].astype(half)], axis=1))
     b_sum = b_kept[0] + wide(b_moved[0]) + wide(b_moved[1]) + wide(b_moved[2])

time: 71 us -> 69 us (0.972)
  waiting for transfers between devices: 15.7 us -> 11.6 us
  starting transfers between devices: 26.9 us -> 29 us
    ppermute x8, waiting for transfers between devices: 5.38 us -> 1.82 us  [move_y(): lax.ppermute(x, 'fin', [(z * 2 + y, z * 2 + 1 - y) for z in range(4) for...]
    ppermute x9 -> x10, starting transfers between devices: 16.2 us -> 19.5 us  [move_z(): lax.ppermute(x, 'fin', [(z * 2 + y, (z ^ k) * 2 + y) for z in range(4) fo...]
    ppermute x8, starting transfers between devices: 10.1 us -> 8.87 us  [move_y(): lax.ppermute(x, 'fin', [(z * 2 + y, z * 2 + 1 - y) for z in range(4) for...]
    ppermute x9 -> x10, waiting for transfers between devices: 10.3 us -> 9.81 us  [move_z(): lax.ppermute(x, 'fin', [(z * 2 + y, (z ^ k) * 2 + y) for z in range(4) fo...]
  transfers between devices with their start and end apart: 19 -> 20, of which waited for: 6 -> 6; matrix products, arithmetic and copies ran while one was open for 10% -> 11% of each run, Pallas kernels for 22% -> 23%
where the time goes in v5:
time: 69 us; the launch traced here: 68.8 us
  starting transfers between devices  29 us (42%)
  Pallas kernels  19.7 us (29%)
  waiting for transfers between devices  11.6 us (17%)
  other arithmetic  5.18 us (8%)
  matrix products  1.54 us (2%)
  local copies, waits for them, and re-layouts  1.48 us (2%)
    ppermute x10, starting transfers between devices, move_z(): lax.ppermute(x, 'fin', [(z * 2 + y, (z ^ k) * 2 + y) for z in range(4) fo...  19.5 us
    ppermute x10, waiting for transfers between devices, move_z(): lax.ppermute(x, 'fin', [(z * 2 + y, (z ^ k) * 2 + y) for z in range(4) fo...  9.81 us
    ppermute x8, starting transfers between devices, move_y(): lax.ppermute(x, 'fin', [(z * 2 + y, z * 2 + 1 - y) for z in range(4) for...  8.87 us
    pallas_call x1, Pallas kernels, load(): pl.pallas_call(load_kernel, in_specs=[HBM] + [ANY] * len(after), out_spec...  6.5 us
    pallas_call x2, Pallas kernels, up(): pl.pallas_call(lambda *refs: up_and_load_kernel(start, *refs), in_specs=[...  5.22 us
    pallas_call x1, Pallas kernels, down_first(): pl.pallas_call(down_first_kernel, in_specs=[VMEM] * 5 + [HBM], out_specs=...  4.67 us
    pallas_call x1, Pallas kernels, over_y_terms(): pl.pallas_call(over_y_kernel, in_specs=[VMEM] * 3, out_specs=[VMEM] * 8,...  2.01 us
    another operation x2, other arithmetic  1.83 us
  transfers between devices with their start and end apart: 20, of which 6 were waited for; matrix products, arithmetic and copies ran while one was open for 11% of the time, Pallas kernels for 23%

profile of v5, /device:TPU:0, one launch (start us, length us, event | category | flops | bytes accessed | tf_op | source)
XLA Modules:
  0.0 68.8 jit_solution(9578894390736533206)
XLA Ops:
  0.0 4.0 %collective-permute-start.1 = (bf16[32,3072]{1,0:T(8,128)(2,1)}, bf16[32,3072]{1,0:T(8,128)(2,1)S(1)}, u32[]{:S(2)}, u32[]{:S(2)}) collective-permute-start(bf16[32,3072]{1,0:T(8,128)(2,1)} %param.7), channel_id=1, source_target_pairs={{0,8},{2,10},{4,12},{6,14},{8,0},{10,2},{12,4},{14,6},{1,9},{3,11}... | collective-permute-start | bytes 589832 | tf_op jit(solution)/shard_map/ppermute | solution.py:62
  4.0 1.6 %collective-permute-start = (bf16[32,3072]{1,0:T(8,128)(2,1)}, bf16[32,3072]{1,0:T(8,128)(2,1)S(1)}, u32[]{:S(2)}, u32[]{:S(2)}) collective-permute-start(bf16[32,3072]{1,0:T(8,128)(2,1)} %param.7), channel_id=1, source_target_pairs={{0,4},{2,6},{4,0},{6,2},{8,12},{10,14},{12,8},{14,10},{1,5},{3,7},... | collective-permute-start | bytes 589832 | tf_op jit(solution)/shard_map/ppermute | solution.py:62
  5.6 1.5 %collective-permute-start.3 = (bf16[32,3072]{1,0:T(8,128)(2,1)}, bf16[32,3072]{1,0:T(8,128)(2,1)S(1)}, u32[]{:S(2)}, u32[]{:S(2)}) collective-permute-start(bf16[32,3072]{1,0:T(8,128)(2,1)} %param.7), channel_id=1, source_target_pairs={{0,2},{2,0},{4,6},{6,4},{8,10},{10,8},{12,14},{14,12},{1,3},{3,1},... | collective-permute-start | bytes 589832 | tf_op jit(solution)/shard_map/ppermute | solution.py:56
  7.1 1.0 %constant_dynamic-update-slice_fusion.8 = bf16[256,3072]{1,0:T(8,128)(2,1)S(1)} fusion(bf16[32,3072]{1,0:T(8,128)(2,1)} %param.7), kind=kLoop, calls=%fused_computation.42 | loop fusion | bytes 393216
  14.4 1.3 %collective-permute-start.5 = (bf16[32,3072]{1,0:T(8,128)(2,1)S(1)}, bf16[32,3072]{1,0:T(8,128)(2,1)S(1)}, u32[]{:S(2)}, u32[]{:S(2)}) collective-permute-start(bf16[32,3072]{1,0:T(8,128)(2,1)S(1)} %collective-permute-done.1.refs_2_), channel_id=1, source_target_pairs={{0,2},{2,0},{4,6},{6,4},{8,10},{10,8},{12,14},{14,12},{1,3},{3,1},... | collective-permute-start | bytes 589832 | tf_op jit(solution)/shard_map/ppermute | solution.py:56
  16.5 6.5 %shard_map.73.refs_1_ = bf16[3072,3072]{1,0:T(8,128)(2,1)S(1)} custom-call(bf16[3072,3072]{1,0:T(8,128)(2,1)} %refs_0_.1, bf16[32,3072]{1,0:T(8,128)(2,1)S(1)} %collective-permute-done.refs_1_, bf16[32,3072]{1,0:T(8,128)(2,1)S(1)} %collective-permute-done.1.refs_2_), custom_call_target="tpu_custom_call" | custom-call | bytes 37748736 | tf_op jit(solution)/shard_map/pallas_call | solution.py:101
  23.0 1.3 %collective-permute-start.6 = (bf16[16,3072]{1,0:T(8,128)(2,1)S(1)}, bf16[16,3072]{1,0:T(8,128)(2,1)S(1)}, u32[]{:S(2)}, u32[]{:S(2)}) collective-permute-start(bf16[16,3072]{1,0:T(8,128)(2,1)S(1)} %slice.29), channel_id=1, source_target_pairs={{0,2},{2,0},{4,6},{6,4},{8,10},{10,8},{12,14},{14,12},{1,3},{3,1},... | collective-permute-start | bytes 294920 | tf_op jit(solution)/shard_map/ppermute | solution.py:56
  24.4 1.4 %collective-permute-start.7 = (bf16[16,3072]{1,0:T(8,128)(2,1)S(1)}, bf16[16,3072]{1,0:T(8,128)(2,1)S(1)}, u32[]{:S(2)}, u32[]{:S(2)}) collective-permute-start(bf16[16,3072]{1,0:T(8,128)(2,1)S(1)} %slice.30), channel_id=1, source_target_pairs={{0,4},{2,6},{4,0},{6,2},{8,12},{10,14},{12,8},{14,10},{1,5},{3,7},... | collective-permute-start | bytes 294920 | tf_op jit(solution)/shard_map/ppermute | solution.py:62
  25.9 1.8 %collective-permute-done.6 = bf16[16,3072]{1,0:T(8,128)(2,1)S(1)} collective-permute-done((bf16[16,3072]{1,0:T(8,128)(2,1)S(1)}, bf16[16,3072]{1,0:T(8,128)(2,1)S(1)}, u32[]{:S(2)}, u32[]{:S(2)}) %collective-permute-start.6) | collective-permute-done | bytes 98336 | tf_op jit(solution)/shard_map/ppermute | solution.py:56
  27.7 1.3 %collective-permute-done.7 = bf16[16,3072]{1,0:T(8,128)(2,1)S(1)} collective-permute-done((bf16[16,3072]{1,0:T(8,128)(2,1)S(1)}, bf16[16,3072]{1,0:T(8,128)(2,1)S(1)}, u32[]{:S(2)}, u32[]{:S(2)}) %collective-permute-start.7) | collective-permute-done | bytes 98336 | tf_op jit(solution)/shard_map/ppermute | solution.py:62
  29.1 2.6 %shard_map.75 = (f32[256,1536]{1,0:T(8,128)S(1)}, bf16[256,1536]{1,0:T(8,128)(2,1)S(1)}, bf16[1536,1536]{1,0:T(8,128)(2,1)S(1)}) custom-call(bf16[256,3072]{1,0:T(8,128)(2,1)S(1)} %constant_dynamic-update-slice_fusion.refs_0_, bf16[3072,3072]{1,0:T(8,128)(2,1)S(1)} %shard_map.73.refs_1_, bf16[3072,3072]{1,0:T(8,128)(2,1)} %w_ref.1), custom_call_target="tpu_custom_call" | custom-call | flops 2415919104 | bytes 1572864 | tf_op jit(solution)/shard_map/pallas_call | solution.py:133
  31.8 2.6 %shard_map.74 = (f32[256,1536]{1,0:T(8,128)S(1)}, bf16[256,1536]{1,0:T(8,128)(2,1)S(1)}, bf16[1536,1536]{1,0:T(8,128)(2,1)S(1)}) custom-call(bf16[256,3072]{1,0:T(8,128)(2,1)S(1)} %constant_dynamic-update-slice_fusion.refs_0_, bf16[3072,3072]{1,0:T(8,128)(2,1)S(1)} %shard_map.73.refs_1_, bf16[3072,3072]{1,0:T(8,128)(2,1)} %w_ref.1), custom_call_target="tpu_custom_call" | custom-call | flops 2415919104 | bytes 1572864 | tf_op jit(solution)/shard_map/pallas_call | solution.py:133
  35.2 4.7 %shard_map.76 = (f32[256,3072]{1,0:T(8,128)S(1)}, bf16[1536,3072]{1,0:T(8,128)(2,1)S(1)}) custom-call(f32[256,1536]{1,0:T(8,128)S(1)} %get-tuple-element.28.own_ref, bf16[256,1536]{1,0:T(8,128)(2,1)S(1)} %collective-permute-done.9.other_ref, f32[256,1536]{1,0:T(8,128)S(1)} %get-tuple-element.47.scale_ref, bf16[1536,1536]{1,0:T(8,128)(2,1)S(1)} %get-tuple-element.30.left_ref, ...), custom_call_target="tpu_custom_call" | custom-call | flops 2415919104 | bytes 9437184 | tf_op jit(solution)/shard_map/pallas_call | solution.py:190
  39.9 1.3 %shard_map.77 = (f32[2,32,768]{2,1,0:T(8,128)S(1)}, bf16[2,32,768]{2,1,0:T(8,128)(2,1)S(1)}, bf16[2,32,768]{2,1,0:T(8,128)(2,1)S(1)}, bf16[2,32,768]{2,1,0:T(8,128)(2,1)S(1)}, bf16[256,1536]{1,0:T(8,128)(2,1)S(1)}) custom-call(f32[256,1536]{1,0:T(8,128)S(1)} %get-tuple-element.26.own_ref, bf16[256,1536]{1,0:T(8,128)(2,1)S(1)} %collective-permute-done.8.other_ref, ...), custom_call_target="tpu_custom_call" | custom-call | flops 603979776 | bytes 2359296 | tf_op jit(solution)/shard_map/pallas_call | solution.py:231
  41.1 3.3 %collective-permute-start.16 = (bf16[2,32,768]{2,1,0:T(8,128)(2,1)S(1)}, bf16[2,32,768]{2,1,0:T(8,128)(2,1)S(1)}, u32[]{:S(2)}, u32[]{:S(2)}) collective-permute-start(bf16[2,32,768]{2,1,0:T(8,128)(2,1)S(1)} %get-tuple-element.43), channel_id=1, source_target_pairs={{0,8},{2,10},{4,12},{6,14},{8,0},{10,2},{12,4},{14,6},{1,9},{3,11}... | collective-permute-start | bytes 294920 | tf_op jit(solution)/shard_map/ppermute | solution.py:62
  45.1 2.0 %shard_map.78 = (f32[32,2304]{1,0:T(8,128)S(1)}, f32[32,2304]{1,0:T(8,128)S(1)}, f32[32,2304]{1,0:T(8,128)S(1)}, f32[32,2304]{1,0:T(8,128)S(1)}, bf16[32,2304]{1...) custom-call(bf16[256,1536]{1,0:T(8,128)(2,1)S(1)} %get-tuple-element., ...), custom_call_target="tpu_custom_call" | custom-call | flops 1811939328 | bytes 7077888 | tf_op jit(solution)/shard_map/pallas_call | solution.py:263
  48.0 1.3 %collective-permute-start.12 = (bf16[32,2304]{1,0:T(8,128)(2,1)S(1)}, bf16[32,2304]{1,0:T(8,128)(2,1)S(1)}, u32[]{:S(2)}, u32[]{:S(2)}) collective-permute-start(bf16[32,2304]{1,0:T(8,128)(2,1)S(1)} %get-tuple-element.39), channel_id=1, source_target_pairs={{0,2},{2,0},{4,6},{6,4},{8,10},{10,8},{12,14},{14,12},{1,3},{3,1},... | collective-permute-start | bytes 442376 | tf_op jit(solution)/shard_map/ppermute | solution.py:56
  49.2 2.7 %collective-permute-done.16 = bf16[2,32,768]{2,1,0:T(8,128)(2,1)S(1)} collective-permute-done((bf16[2,32,768]{2,1,0:T(8,128)(2,1)S(1)}, bf16[2,32,768]{2,1,0:T(8,128)(2,1)S(1)}, u32[]{:S(2)}, u32[]{:S(2)}) %collective-permute-start.16) | collective-permute-done | bytes 98336 | tf_op jit(solution)/shard_map/ppermute | solution.py:62
  53.1 1.0 %collective-permute-start.19 = (bf16[32,3072]{1,0:T(8,128)(2,1)S(1)}, bf16[32,3072]{1,0:T(8,128)(2,1)S(1)}, u32[]{:S(2)}, u32[]{:S(2)}) collective-permute-start(bf16[32,3072]{1,0:T(8,128)(2,1)S(1)} %pad_maximum_fusion), channel_id=1, source_target_pairs={{0,2},{2,0},{4,6},{6,4},{8,10},{10,8},{12,14},{14,12},{1,3},{3,1},... | collective-permute-start | bytes 589832 | tf_op jit(solution)/shard_map/ppermute | solution.py:56
  54.2 3.6 %collective-permute-start.11 = (bf16[32,2304]{1,0:T(8,128)(2,1)S(1)}, bf16[32,2304]{1,0:T(8,128)(2,1)S(1)}, u32[]{:S(2)}, u32[]{:S(2)}) collective-permute-start(bf16[32,2304]{1,0:T(8,128)(2,1)S(1)} %add_convert_fusion.2), channel_id=1, source_target_pairs={{0,8},{2,10},{4,12},{6,14},{8,0},{10,2},{12,4},{14,6},{1,9},{3,11}... | collective-permute-start | bytes 442376 | tf_op jit(solution)/shard_map/ppermute | solution.py:62
  57.9 2.6 %collective-permute-start.13 = (bf16[32,2304]{1,0:T(8,128)(2,1)S(1)}, bf16[32,2304]{1,0:T(8,128)(2,1)S(1)}, u32[]{:S(2)}, u32[]{:S(2)}) collective-permute-start(bf16[32,2304]{1,0:T(8,128)(2,1)S(1)} %add_convert_fusion.1), channel_id=1, source_target_pairs={{0,12},{2,14},{4,8},{6,10},{8,4},{10,6},{12,0},{14,2},{1,13},{3,15... | collective-permute-start | bytes 442376 | tf_op jit(solution)/shard_map/ppermute | solution.py:62
  60.5 1.8 %collective-permute-start.15 = (bf16[32,2304]{1,0:T(8,128)(2,1)S(1)}, bf16[32,2304]{1,0:T(8,128)(2,1)S(1)}, u32[]{:S(2)}, u32[]{:S(2)}) collective-permute-start(bf16[32,2304]{1,0:T(8,128)(2,1)S(1)} %add_convert_fusion), channel_id=1, source_target_pairs={{0,4},{2,6},{4,0},{6,2},{8,12},{10,14},{12,8},{14,10},{1,5},{3,7},... | collective-permute-start | bytes 442376 | tf_op jit(solution)/shard_map/ppermute | solution.py:62
  62.2 4.9 %collective-permute-done.11 = bf16[32,2304]{1,0:T(8,128)(2,1)S(1)} collective-permute-done((bf16[32,2304]{1,0:T(8,128)(2,1)S(1)}, bf16[32,2304]{1,0:T(8,128)(2,1)S(1)}, u32[]{:S(2)}, u32[]{:S(2)}) %collective-permute-start.11) | collective-permute-done | bytes 147488 | tf_op jit(solution)/shard_map/ppermute | solution.py:62
  67.8 0.9 %fusion.1 = bf16[32,3072]{1,0:T(8,128)(2,1)} fusion(f32[32,768]{1,0:T(8,128)S(1)} %slice_bitcast_fusion, f32[32,2304]{1,0:T(8,128)S(1)} %convert_add_fusion, bf16[32,3072]{1,0:T(8,128)(2,1)S(1)} %collective-permute-done.19, bf16[8,3072]{1,0:T(8,128)(2,1)S(1)} %get-tuple-element.50, bf16[8,3072]{1,0:T(8,128)(2,1)S(1)} %get-tuple-element.51, ...), kind=kOutput, calls=%fused_computation.2 | convolution fusion | flops 5657088 | bytes 934400 | tf_op jit(solution)/shard_map/dot_general | solution.py:25
  (59 shorter events, 11.4 us)
Async XLA Ops:
  0.0 13.9 %collective-permute-start.1 = (bf16[32,3072]{1,0:T(8,128)(2,1)}, bf16[32,3072]{1,0:T(8,128)(2,1)S(1)}, u32[]{:S(2)}, u32[]{:S(2)}) collective-permute-start(bf16[32,3072]{1,0:T(8,128)(2,1)} %param.7), channel_id=1, source_target_pairs={{0,8},{2,10},{4,12},{6,14},{8,0},{10,2},{12,4},{14,6},{1,9},{3,11}... | collective-permute-start | bytes 589832 | tf_op jit(solution)/shard_map/ppermute | solution.py:62
  4.0 11.7 %collective-permute-start = (bf16[32,3072]{1,0:T(8,128)(2,1)}, bf16[32,3072]{1,0:T(8,128)(2,1)S(1)}, u32[]{:S(2)}, u32[]{:S(2)}) collective-permute-start(bf16[32,3072]{1,0:T(8,128)(2,1)} %param.7), channel_id=1, source_target_pairs={{0,4},{2,6},{4,0},{6,2},{8,12},{10,14},{12,8},{14,10},{1,5},{3,7},... | collective-permute-start | bytes 589832 | tf_op jit(solution)/shard_map/ppermute | solution.py:62
  5.6 20.2 %collective-permute-start.3 = (bf16[32,3072]{1,0:T(8,128)(2,1)}, bf16[32,3072]{1,0:T(8,128)(2,1)S(1)}, u32[]{:S(2)}, u32[]{:S(2)}) collective-permute-start(bf16[32,3072]{1,0:T(8,128)(2,1)} %param.7), channel_id=1, source_target_pairs={{0,2},{2,0},{4,6},{6,4},{8,10},{10,8},{12,14},{14,12},{1,3},{3,1},... | collective-permute-start | bytes 589832 | tf_op jit(solution)/shard_map/ppermute | solution.py:56
  13.9 9.1 %collective-permute-start.2 = (bf16[32,3072]{1,0:T(8,128)(2,1)S(1)}, bf16[32,3072]{1,0:T(8,128)(2,1)S(1)}, u32[]{:S(2)}, u32[]{:S(2)}) collective-permute-start(bf16[32,3072]{1,0:T(8,128)(2,1)S(1)} %collective-permute-done.1.refs_2_), channel_id=1, source_target_pairs={{0,4},{2,6},{4,0},{6,2},{8,12},{10,14},{12,8},{14,10},{1,5},{3,7},... | collective-permute-start | bytes 589832 | tf_op jit(solution)/shard_map/ppermute | solution.py:62
  14.4 9.9 %collective-permute-start.5 = (bf16[32,3072]{1,0:T(8,128)(2,1)S(1)}, bf16[32,3072]{1,0:T(8,128)(2,1)S(1)}, u32[]{:S(2)}, u32[]{:S(2)}) collective-permute-start(bf16[32,3072]{1,0:T(8,128)(2,1)S(1)} %collective-permute-done.1.refs_2_), channel_id=1, source_target_pairs={{0,2},{2,0},{4,6},{6,4},{8,10},{10,8},{12,14},{14,12},{1,3},{3,1},... | collective-permute-start | bytes 589832 | tf_op jit(solution)/shard_map/ppermute | solution.py:56
  15.7 10.2 %collective-permute-start.4 = (bf16[32,3072]{1,0:T(8,128)(2,1)S(1)}, bf16[32,3072]{1,0:T(8,128)(2,1)S(1)}, u32[]{:S(2)}, u32[]{:S(2)}) collective-permute-start(bf16[32,3072]{1,0:T(8,128)(2,1)S(1)} %collective-permute-done.refs_1_), channel_id=1, source_target_pairs={{0,2},{2,0},{4,6},{6,4},{8,10},{10,8},{12,14},{14,12},{1,3},{3,1},... | collective-permute-start | bytes 589832 | tf_op jit(solution)/shard_map/ppermute | solution.py:56
  23.0 4.7 %collective-permute-start.6 = (bf16[16,3072]{1,0:T(8,128)(2,1)S(1)}, bf16[16,3072]{1,0:T(8,128)(2,1)S(1)}, u32[]{:S(2)}, u32[]{:S(2)}) collective-permute-start(bf16[16,3072]{1,0:T(8,128)(2,1)S(1)} %slice.29), channel_id=1, source_target_pairs={{0,2},{2,0},{4,6},{6,4},{8,10},{10,8},{12,14},{14,12},{1,3},{3,1},... | collective-permute-start | bytes 294920 | tf_op jit(solution)/shard_map/ppermute | solution.py:56
  24.4 4.7 %collective-permute-start.7 = (bf16[16,3072]{1,0:T(8,128)(2,1)S(1)}, bf16[16,3072]{1,0:T(8,128)(2,1)S(1)}, u32[]{:S(2)}, u32[]{:S(2)}) collective-permute-start(bf16[16,3072]{1,0:T(8,128)(2,1)S(1)} %slice.30), channel_id=1, source_target_pairs={{0,4},{2,6},{4,0},{6,2},{8,12},{10,14},{12,8},{14,10},{1,5},{3,7},... | collective-permute-start | bytes 294920 | tf_op jit(solution)/shard_map/ppermute | solution.py:62
  31.7 3.5 %collective-permute-start.9 = (bf16[256,1536]{1,0:T(8,128)(2,1)S(1)}, bf16[256,1536]{1,0:T(8,128)(2,1)S(1)}, u32[]{:S(2)}, u32[]{:S(2)}) collective-permute-start(bf16[256,1536]{1,0:T(8,128)(2,1)S(1)} %get-tuple-element.29), channel_id=1, source_target_pairs={{0,1},{1,0},{2,3},{3,2},{4,5},{5,4},{6,7},{7,6},{8,9},{9,8},{10,11... | collective-permute-start | bytes 2359304 | tf_op jit(solution)/shard_map/ppermute | solution.py:275
  34.4 5.5 %collective-permute-start.8 = (bf16[256,1536]{1,0:T(8,128)(2,1)S(1)}, bf16[256,1536]{1,0:T(8,128)(2,1)S(1)}, u32[]{:S(2)}, u32[]{:S(2)}) collective-permute-start(bf16[256,1536]{1,0:T(8,128)(2,1)S(1)} %get-tuple-element.27), channel_id=1, source_target_pairs={{0,1},{1,0},{2,3},{3,2},{4,5},{5,4},{6,7},{7,6},{8,9},{9,8},{10,11... | collective-permute-start | bytes 2359304 | tf_op jit(solution)/shard_map/ppermute | solution.py:275
  41.1 10.8 %collective-permute-start.16 = (bf16[2,32,768]{2,1,0:T(8,128)(2,1)S(1)}, bf16[2,32,768]{2,1,0:T(8,128)(2,1)S(1)}, u32[]{:S(2)}, u32[]{:S(2)}) collective-permute-start(bf16[2,32,768]{2,1,0:T(8,128)(2,1)S(1)} %get-tuple-element.43), channel_id=1, source_target_pairs={{0,8},{2,10},{4,12},{6,14},{8,0},{10,2},{12,4},{14,6},{1,9},{3,11}... | collective-permute-start | bytes 294920 | tf_op jit(solution)/shard_map/ppermute | solution.py:62
  44.5 8.4 %collective-permute-start.17 = (bf16[2,32,768]{2,1,0:T(8,128)(2,1)S(1)}, bf16[2,32,768]{2,1,0:T(8,128)(2,1)S(1)}, u32[]{:S(2)}, u32[]{:S(2)}) collective-permute-start(bf16[2,32,768]{2,1,0:T(8,128)(2,1)S(1)} %get-tuple-element.44), channel_id=1, source_target_pairs={{0,12},{2,14},{4,8},{6,10},{8,4},{10,6},{12,0},{14,2},{1,13},{3,15... | collective-permute-start | bytes 294920 | tf_op jit(solution)/shard_map/ppermute | solution.py:62
  44.9 8.1 %collective-permute-start.18 = (bf16[2,32,768]{2,1,0:T(8,128)(2,1)S(1)}, bf16[2,32,768]{2,1,0:T(8,128)(2,1)S(1)}, u32[]{:S(2)}, u32[]{:S(2)}) collective-permute-start(bf16[2,32,768]{2,1,0:T(8,128)(2,1)S(1)} %get-tuple-element.45), channel_id=1, source_target_pairs={{0,4},{2,6},{4,0},{6,2},{8,12},{10,14},{12,8},{14,10},{1,5},{3,7},... | collective-permute-start | bytes 294920 | tf_op jit(solution)/shard_map/ppermute | solution.py:62
  47.1 7.0 %collective-permute-start.10 = (bf16[32,2304]{1,0:T(8,128)(2,1)S(1)}, bf16[32,2304]{1,0:T(8,128)(2,1)S(1)}, u32[]{:S(2)}, u32[]{:S(2)}) collective-permute-start(bf16[32,2304]{1,0:T(8,128)(2,1)S(1)} %get-tuple-element.37), channel_id=1, source_target_pairs={{0,2},{2,0},{4,6},{6,4},{8,10},{10,8},{12,14},{14,12},{1,3},{3,1},... | collective-permute-start | bytes 442376 | tf_op jit(solution)/shard_map/ppermute | solution.py:56
  48.0 9.9 %collective-permute-start.12 = (bf16[32,2304]{1,0:T(8,128)(2,1)S(1)}, bf16[32,2304]{1,0:T(8,128)(2,1)S(1)}, u32[]{:S(2)}, u32[]{:S(2)}) collective-permute-start(bf16[32,2304]{1,0:T(8,128)(2,1)S(1)} %get-tuple-element.39), channel_id=1, source_target_pairs={{0,2},{2,0},{4,6},{6,4},{8,10},{10,8},{12,14},{14,12},{1,3},{3,1},... | collective-permute-start | bytes 442376 | tf_op jit(solution)/shard_map/ppermute | solution.py:56
  52.0 8.5 %collective-permute-start.14 = (bf16[32,2304]{1,0:T(8,128)(2,1)S(1)}, bf16[32,2304]{1,0:T(8,128)(2,1)S(1)}, u32[]{:S(2)}, u32[]{:S(2)}) collective-permute-start(bf16[32,2304]{1,0:T(8,128)(2,1)S(1)} %get-tuple-element.41), channel_id=1, source_target_pairs={{0,2},{2,0},{4,6},{6,4},{8,10},{10,8},{12,14},{14,12},{1,3},{3,1},... | collective-permute-start | bytes 442376 | tf_op jit(solution)/shard_map/ppermute | solution.py:56
  53.1 14.7 %collective-permute-start.19 = (bf16[32,3072]{1,0:T(8,128)(2,1)S(1)}, bf16[32,3072]{1,0:T(8,128)(2,1)S(1)}, u32[]{:S(2)}, u32[]{:S(2)}) collective-permute-start(bf16[32,3072]{1,0:T(8,128)(2,1)S(1)} %pad_maximum_fusion), channel_id=1, source_target_pairs={{0,2},{2,0},{4,6},{6,4},{8,10},{10,8},{12,14},{14,12},{1,3},{3,1},... | collective-permute-start | bytes 589832 | tf_op jit(solution)/shard_map/ppermute | solution.py:56
  54.2 12.9 %collective-permute-start.11 = (bf16[32,2304]{1,0:T(8,128)(2,1)S(1)}, bf16[32,2304]{1,0:T(8,128)(2,1)S(1)}, u32[]{:S(2)}, u32[]{:S(2)}) collective-permute-start(bf16[32,2304]{1,0:T(8,128)(2,1)S(1)} %add_convert_fusion.2), channel_id=1, source_target_pairs={{0,8},{2,10},{4,12},{6,14},{8,0},{10,2},{12,4},{14,6},{1,9},{3,11}... | collective-permute-start | bytes 442376 | tf_op jit(solution)/shard_map/ppermute | solution.py:62
  57.9 9.2 %collective-permute-start.13 = (bf16[32,2304]{1,0:T(8,128)(2,1)S(1)}, bf16[32,2304]{1,0:T(8,128)(2,1)S(1)}, u32[]{:S(2)}, u32[]{:S(2)}) collective-permute-start(bf16[32,2304]{1,0:T(8,128)(2,1)S(1)} %add_convert_fusion.1), channel_id=1, source_target_pairs={{0,12},{2,14},{4,8},{6,10},{8,4},{10,6},{12,0},{14,2},{1,13},{3,15... | collective-permute-start | bytes 442376 | tf_op jit(solution)/shard_map/ppermute | solution.py:62
  60.5 7.3 %collective-permute-start.15 = (bf16[32,2304]{1,0:T(8,128)(2,1)S(1)}, bf16[32,2304]{1,0:T(8,128)(2,1)S(1)}, u32[]{:S(2)}, u32[]{:S(2)}) collective-permute-start(bf16[32,2304]{1,0:T(8,128)(2,1)S(1)} %add_convert_fusion), channel_id=1, source_target_pairs={{0,4},{2,6},{4,0},{6,2},{8,12},{10,14},{12,8},{14,10},{1,5},{3,7},... | collective-permute-start | bytes 442376 | tf_op jit(solution)/shard_map/ppermute | solution.py:62

commit v6 on v5

--- a/solution.py
+++ b/solution.py
@@ -312,8 +312,8 @@
     b_kept, b_last, b_sent = b_terms[:4], b_terms[4], b_terms[5:]
 
     a_moved = [move_z(a_sent[k - 1], k) for k in (2, 3, 1)]
-    b_across = [move_y(b_sent[k - 1]) for k in (2, 3, 1)]
-    b_moved = [move_z((b_kept[k] + wide(b_across[(2, 3, 1).index(k)])).astype(half), k) for k in (2, 3, 1)]
+    b_across = [move_y(b_sent[k - 1]) for k in (3, 2, 1)]
+    b_moved = [move_z((b_kept[k] + wide(b_across[(3, 2, 1).index(k)])).astype(half), k) for k in (3, 2, 1)]
     a_sum = a_kept + wide(a_moved[0]) + wide(a_moved[1]) + wide(a_moved[2])
     last = move_y(jnp.concatenate([b_last, a_sum[1].astype(half)], axis=1))
     b_sum = b_kept[0] + wide(b_moved[0]) + wide(b_moved[1]) + wide(b_moved[2])

time: 69 us -> 70.6 us (1.023)
  waiting for transfers between devices: 11.6 us -> 13.2 us
    ppermute x10, waiting for transfers between devices: 9.81 us -> 11.4 us  [move_z(): lax.ppermute(x, 'fin', [(z * 2 + y, (z ^ k) * 2 + y) for z in range(4) fo...]
  transfers between devices with their start and end apart: 20 -> 20, of which waited for: 6 -> 5; matrix products, arithmetic and copies ran while one was open for 11% -> 10% of each run, Pallas kernels for 23% -> 22%
where the time goes in v6:
time: 70.6 us; the launch traced here: 70.4 us
  starting transfers between devices  29 us (41%)
  Pallas kernels  19.7 us (28%)
  waiting for transfers between devices  13.2 us (19%)
  other arithmetic  5.18 us (7%)
  matrix products  1.54 us (2%)
  local copies, waits for them, and re-layouts  1.48 us (2%)
    ppermute x10, starting transfers between devices, move_z(): lax.ppermute(x, 'fin', [(z * 2 + y, (z ^ k) * 2 + y) for z in range(4) fo...  19.5 us
    ppermute x10, waiting for transfers between devices, move_z(): lax.ppermute(x, 'fin', [(z * 2 + y, (z ^ k) * 2 + y) for z in range(4) fo...  11.4 us
    ppermute x8, starting transfers between devices, move_y(): lax.ppermute(x, 'fin', [(z * 2 + y, z * 2 + 1 - y) for z in range(4) for...  8.87 us
    pallas_call x1, Pallas kernels, load(): pl.pallas_call(load_kernel, in_specs=[HBM] + [ANY] * len(after), out_spec...  6.5 us
    pallas_call x2, Pallas kernels, up(): pl.pallas_call(lambda *refs: up_and_load_kernel(start, *refs), in_specs=[...  5.22 us
    pallas_call x1, Pallas kernels, down_first(): pl.pallas_call(down_first_kernel, in_specs=[VMEM] * 5 + [HBM], out_specs=...  4.67 us
    pallas_call x1, Pallas kernels, over_y_terms(): pl.pallas_call(over_y_kernel, in_specs=[VMEM] * 3, out_specs=[VMEM] * 8,...  2.01 us
    another operation x2, other arithmetic  1.83 us
  transfers between devices with their start and end apart: 20, of which 5 were waited for; matrix products, arithmetic and copies ran while one was open for 10% of the time, Pallas kernels for 22%

profile of v6, /device:TPU:0, one launch (start us, length us, event | category | flops | bytes accessed | tf_op | source)
XLA Modules:
  0.0 70.4 jit_solution(17991599205899389088)
XLA Ops:
  0.0 4.0 %collective-permute-start.1 = (bf16[32,3072]{1,0:T(8,128)(2,1)}, bf16[32,3072]{1,0:T(8,128)(2,1)S(1)}, u32[]{:S(2)}, u32[]{:S(2)}) collective-permute-start(bf16[32,3072]{1,0:T(8,128)(2,1)} %param.7), channel_id=1, source_target_pairs={{0,8},{2,10},{4,12},{6,14},{8,0},{10,2},{12,4},{14,6},{1,9},{3,11}... | collective-permute-start | bytes 589832 | tf_op jit(solution)/shard_map/ppermute | solution.py:62
  4.0 1.6 %collective-permute-start = (bf16[32,3072]{1,0:T(8,128)(2,1)}, bf16[32,3072]{1,0:T(8,128)(2,1)S(1)}, u32[]{:S(2)}, u32[]{:S(2)}) collective-permute-start(bf16[32,3072]{1,0:T(8,128)(2,1)} %param.7), channel_id=1, source_target_pairs={{0,4},{2,6},{4,0},{6,2},{8,12},{10,14},{12,8},{14,10},{1,5},{3,7},... | collective-permute-start | bytes 589832 | tf_op jit(solution)/shard_map/ppermute | solution.py:62
  5.6 1.5 %collective-permute-start.3 = (bf16[32,3072]{1,0:T(8,128)(2,1)}, bf16[32,3072]{1,0:T(8,128)(2,1)S(1)}, u32[]{:S(2)}, u32[]{:S(2)}) collective-permute-start(bf16[32,3072]{1,0:T(8,128)(2,1)} %param.7), channel_id=1, source_target_pairs={{0,2},{2,0},{4,6},{6,4},{8,10},{10,8},{12,14},{14,12},{1,3},{3,1},... | collective-permute-start | bytes 589832 | tf_op jit(solution)/shard_map/ppermute | solution.py:56
  7.1 1.0 %constant_dynamic-update-slice_fusion.8 = bf16[256,3072]{1,0:T(8,128)(2,1)S(1)} fusion(bf16[32,3072]{1,0:T(8,128)(2,1)} %param.7), kind=kLoop, calls=%fused_computation.42 | loop fusion | bytes 393216
  14.4 1.3 %collective-permute-start.5 = (bf16[32,3072]{1,0:T(8,128)(2,1)S(1)}, bf16[32,3072]{1,0:T(8,128)(2,1)S(1)}, u32[]{:S(2)}, u32[]{:S(2)}) collective-permute-start(bf16[32,3072]{1,0:T(8,128)(2,1)S(1)} %collective-permute-done.1.refs_2_), channel_id=1, source_target_pairs={{0,2},{2,0},{4,6},{6,4},{8,10},{10,8},{12,14},{14,12},{1,3},{3,1},... | collective-permute-start | bytes 589832 | tf_op jit(solution)/shard_map/ppermute | solution.py:56
  16.5 6.5 %shard_map.73.refs_1_ = bf16[3072,3072]{1,0:T(8,128)(2,1)S(1)} custom-call(bf16[3072,3072]{1,0:T(8,128)(2,1)} %refs_0_.1, bf16[32,3072]{1,0:T(8,128)(2,1)S(1)} %collective-permute-done.refs_1_, bf16[32,3072]{1,0:T(8,128)(2,1)S(1)} %collective-permute-done.1.refs_2_), custom_call_target="tpu_custom_call" | custom-call | bytes 37748736 | tf_op jit(solution)/shard_map/pallas_call | solution.py:101
  23.0 1.3 %collective-permute-start.6 = (bf16[16,3072]{1,0:T(8,128)(2,1)S(1)}, bf16[16,3072]{1,0:T(8,128)(2,1)S(1)}, u32[]{:S(2)}, u32[]{:S(2)}) collective-permute-start(bf16[16,3072]{1,0:T(8,128)(2,1)S(1)} %slice.29), channel_id=1, source_target_pairs={{0,2},{2,0},{4,6},{6,4},{8,10},{10,8},{12,14},{14,12},{1,3},{3,1},... | collective-permute-start | bytes 294920 | tf_op jit(solution)/shard_map/ppermute | solution.py:56
  24.4 1.4 %collective-permute-start.7 = (bf16[16,3072]{1,0:T(8,128)(2,1)S(1)}, bf16[16,3072]{1,0:T(8,128)(2,1)S(1)}, u32[]{:S(2)}, u32[]{:S(2)}) collective-permute-start(bf16[16,3072]{1,0:T(8,128)(2,1)S(1)} %slice.30), channel_id=1, source_target_pairs={{0,4},{2,6},{4,0},{6,2},{8,12},{10,14},{12,8},{14,10},{1,5},{3,7},... | collective-permute-start | bytes 294920 | tf_op jit(solution)/shard_map/ppermute | solution.py:62
  25.9 1.8 %collective-permute-done.6 = bf16[16,3072]{1,0:T(8,128)(2,1)S(1)} collective-permute-done((bf16[16,3072]{1,0:T(8,128)(2,1)S(1)}, bf16[16,3072]{1,0:T(8,128)(2,1)S(1)}, u32[]{:S(2)}, u32[]{:S(2)}) %collective-permute-start.6) | collective-permute-done | bytes 98336 | tf_op jit(solution)/shard_map/ppermute | solution.py:56
  27.7 1.3 %collective-permute-done.7 = bf16[16,3072]{1,0:T(8,128)(2,1)S(1)} collective-permute-done((bf16[16,3072]{1,0:T(8,128)(2,1)S(1)}, bf16[16,3072]{1,0:T(8,128)(2,1)S(1)}, u32[]{:S(2)}, u32[]{:S(2)}) %collective-permute-start.7) | collective-permute-done | bytes 98336 | tf_op jit(solution)/shard_map/ppermute | solution.py:62
  29.1 2.6 %shard_map.75 = (f32[256,1536]{1,0:T(8,128)S(1)}, bf16[256,1536]{1,0:T(8,128)(2,1)S(1)}, bf16[1536,1536]{1,0:T(8,128)(2,1)S(1)}) custom-call(bf16[256,3072]{1,0:T(8,128)(2,1)S(1)} %constant_dynamic-update-slice_fusion.refs_0_, bf16[3072,3072]{1,0:T(8,128)(2,1)S(1)} %shard_map.73.refs_1_, bf16[3072,3072]{1,0:T(8,128)(2,1)} %w_ref.1), custom_call_target="tpu_custom_call" | custom-call | flops 2415919104 | bytes 1572864 | tf_op jit(solution)/shard_map/pallas_call | solution.py:133
  31.8 2.6 %shard_map.74 = (f32[256,1536]{1,0:T(8,128)S(1)}, bf16[256,1536]{1,0:T(8,128)(2,1)S(1)}, bf16[1536,1536]{1,0:T(8,128)(2,1)S(1)}) custom-call(bf16[256,3072]{1,0:T(8,128)(2,1)S(1)} %constant_dynamic-update-slice_fusion.refs_0_, bf16[3072,3072]{1,0:T(8,128)(2,1)S(1)} %shard_map.73.refs_1_, bf16[3072,3072]{1,0:T(8,128)(2,1)} %w_ref.1), custom_call_target="tpu_custom_call" | custom-call | flops 2415919104 | bytes 1572864 | tf_op jit(solution)/shard_map/pallas_call | solution.py:133
  35.2 4.7 %shard_map.76 = (f32[256,3072]{1,0:T(8,128)S(1)}, bf16[1536,3072]{1,0:T(8,128)(2,1)S(1)}) custom-call(f32[256,1536]{1,0:T(8,128)S(1)} %get-tuple-element.28.own_ref, bf16[256,1536]{1,0:T(8,128)(2,1)S(1)} %collective-permute-done.9.other_ref, f32[256,1536]{1,0:T(8,128)S(1)} %get-tuple-element.47.scale_ref, bf16[1536,1536]{1,0:T(8,128)(2,1)S(1)} %get-tuple-element.30.left_ref, ...), custom_call_target="tpu_custom_call" | custom-call | flops 2415919104 | bytes 9437184 | tf_op jit(solution)/shard_map/pallas_call | solution.py:190
  39.9 1.3 %shard_map.77 = (f32[2,32,768]{2,1,0:T(8,128)S(1)}, bf16[2,32,768]{2,1,0:T(8,128)(2,1)S(1)}, bf16[2,32,768]{2,1,0:T(8,128)(2,1)S(1)}, bf16[2,32,768]{2,1,0:T(8,128)(2,1)S(1)}, bf16[256,1536]{1,0:T(8,128)(2,1)S(1)}) custom-call(f32[256,1536]{1,0:T(8,128)S(1)} %get-tuple-element.26.own_ref, bf16[256,1536]{1,0:T(8,128)(2,1)S(1)} %collective-permute-done.8.other_ref, ...), custom_call_target="tpu_custom_call" | custom-call | flops 603979776 | bytes 2359296 | tf_op jit(solution)/shard_map/pallas_call | solution.py:231
  41.1 3.3 %collective-permute-start.16 = (bf16[2,32,768]{2,1,0:T(8,128)(2,1)S(1)}, bf16[2,32,768]{2,1,0:T(8,128)(2,1)S(1)}, u32[]{:S(2)}, u32[]{:S(2)}) collective-permute-start(bf16[2,32,768]{2,1,0:T(8,128)(2,1)S(1)} %get-tuple-element.43), channel_id=1, source_target_pairs={{0,8},{2,10},{4,12},{6,14},{8,0},{10,2},{12,4},{14,6},{1,9},{3,11}... | collective-permute-start | bytes 294920 | tf_op jit(solution)/shard_map/ppermute | solution.py:62
  45.1 2.0 %shard_map.78 = (f32[32,2304]{1,0:T(8,128)S(1)}, f32[32,2304]{1,0:T(8,128)S(1)}, f32[32,2304]{1,0:T(8,128)S(1)}, f32[32,2304]{1,0:T(8,128)S(1)}, bf16[32,2304]{1...) custom-call(bf16[256,1536]{1,0:T(8,128)(2,1)S(1)} %get-tuple-element., ...), custom_call_target="tpu_custom_call" | custom-call | flops 1811939328 | bytes 7077888 | tf_op jit(solution)/shard_map/pallas_call | solution.py:263
  48.0 1.3 %collective-permute-start.12 = (bf16[32,2304]{1,0:T(8,128)(2,1)S(1)}, bf16[32,2304]{1,0:T(8,128)(2,1)S(1)}, u32[]{:S(2)}, u32[]{:S(2)}) collective-permute-start(bf16[32,2304]{1,0:T(8,128)(2,1)S(1)} %get-tuple-element.39), channel_id=1, source_target_pairs={{0,2},{2,0},{4,6},{6,4},{8,10},{10,8},{12,14},{14,12},{1,3},{3,1},... | collective-permute-start | bytes 442376 | tf_op jit(solution)/shard_map/ppermute | solution.py:56
  49.2 2.7 %collective-permute-done.16 = bf16[2,32,768]{2,1,0:T(8,128)(2,1)S(1)} collective-permute-done((bf16[2,32,768]{2,1,0:T(8,128)(2,1)S(1)}, bf16[2,32,768]{2,1,0:T(8,128)(2,1)S(1)}, u32[]{:S(2)}, u32[]{:S(2)}) %collective-permute-start.16) | collective-permute-done | bytes 98336 | tf_op jit(solution)/shard_map/ppermute | solution.py:62
  53.1 1.0 %collective-permute-start.19 = (bf16[32,3072]{1,0:T(8,128)(2,1)S(1)}, bf16[32,3072]{1,0:T(8,128)(2,1)S(1)}, u32[]{:S(2)}, u32[]{:S(2)}) collective-permute-start(bf16[32,3072]{1,0:T(8,128)(2,1)S(1)} %pad_maximum_fusion), channel_id=1, source_target_pairs={{0,2},{2,0},{4,6},{6,4},{8,10},{10,8},{12,14},{14,12},{1,3},{3,1},... | collective-permute-start | bytes 589832 | tf_op jit(solution)/shard_map/ppermute | solution.py:56
  54.2 3.1 %collective-permute-start.11 = (bf16[32,2304]{1,0:T(8,128)(2,1)S(1)}, bf16[32,2304]{1,0:T(8,128)(2,1)S(1)}, u32[]{:S(2)}, u32[]{:S(2)}) collective-permute-start(bf16[32,2304]{1,0:T(8,128)(2,1)S(1)} %add_convert_fusion.2), channel_id=1, source_target_pairs={{0,12},{2,14},{4,8},{6,10},{8,4},{10,6},{12,0},{14,2},{1,13},{3,15... | collective-permute-start | bytes 442376 | tf_op jit(solution)/shard_map/ppermute | solution.py:62
  57.3 3.7 %collective-permute-start.13 = (bf16[32,2304]{1,0:T(8,128)(2,1)S(1)}, bf16[32,2304]{1,0:T(8,128)(2,1)S(1)}, u32[]{:S(2)}, u32[]{:S(2)}) collective-permute-start(bf16[32,2304]{1,0:T(8,128)(2,1)S(1)} %add_convert_fusion.1), channel_id=1, source_target_pairs={{0,8},{2,10},{4,12},{6,14},{8,0},{10,2},{12,4},{14,6},{1,9},{3,11}... | collective-permute-start | bytes 442376 | tf_op jit(solution)/shard_map/ppermute | solution.py:62
  61.0 1.2 %collective-permute-start.15 = (bf16[32,2304]{1,0:T(8,128)(2,1)S(1)}, bf16[32,2304]{1,0:T(8,128)(2,1)S(1)}, u32[]{:S(2)}, u32[]{:S(2)}) collective-permute-start(bf16[32,2304]{1,0:T(8,128)(2,1)S(1)} %add_convert_fusion), channel_id=1, source_target_pairs={{0,4},{2,6},{4,0},{6,2},{8,12},{10,14},{12,8},{14,10},{1,5},{3,7},... | collective-permute-start | bytes 442376 | tf_op jit(solution)/shard_map/ppermute | solution.py:62
  62.2 7.1 %collective-permute-done.13 = bf16[32,2304]{1,0:T(8,128)(2,1)S(1)} collective-permute-done((bf16[32,2304]{1,0:T(8,128)(2,1)S(1)}, bf16[32,2304]{1,0:T(8,128)(2,1)S(1)}, u32[]{:S(2)}, u32[]{:S(2)}) %collective-permute-start.13) | collective-permute-done | bytes 147488 | tf_op jit(solution)/shard_map/ppermute | solution.py:62
  69.4 0.9 %fusion.1 = bf16[32,3072]{1,0:T(8,128)(2,1)} fusion(f32[32,768]{1,0:T(8,128)S(1)} %slice_bitcast_fusion, f32[32,2304]{1,0:T(8,128)S(1)} %convert_add_fusion, bf16[32,3072]{1,0:T(8,128)(2,1)S(1)} %collective-permute-done.19, bf16[8,3072]{1,0:T(8,128)(2,1)S(1)} %get-tuple-element.50, bf16[8,3072]{1,0:T(8,128)(2,1)S(1)} %get-tuple-element.51, ...), kind=kOutput, calls=%fused_computation.2 | convolution fusion | flops 5657088 | bytes 934400 | tf_op jit(solution)/shard_map/dot_general | solution.py:25
  (59 shorter events, 10.8 us)
Async XLA Ops:
  0.0 13.9 %collective-permute-start.1 = (bf16[32,3072]{1,0:T(8,128)(2,1)}, bf16[32,3072]{1,0:T(8,128)(2,1)S(1)}, u32[]{:S(2)}, u32[]{:S(2)}) collective-permute-start(bf16[32,3072]{1,0:T(8,128)(2,1)} %param.7), channel_id=1, source_target_pairs={{0,8},{2,10},{4,12},{6,14},{8,0},{10,2},{12,4},{14,6},{1,9},{3,11}... | collective-permute-start | bytes 589832 | tf_op jit(solution)/shard_map/ppermute | solution.py:62
  4.0 11.7 %collective-permute-start = (bf16[32,3072]{1,0:T(8,128)(2,1)}, bf16[32,3072]{1,0:T(8,128)(2,1)S(1)}, u32[]{:S(2)}, u32[]{:S(2)}) collective-permute-start(bf16[32,3072]{1,0:T(8,128)(2,1)} %param.7), channel_id=1, source_target_pairs={{0,4},{2,6},{4,0},{6,2},{8,12},{10,14},{12,8},{14,10},{1,5},{3,7},... | collective-permute-start | bytes 589832 | tf_op jit(solution)/shard_map/ppermute | solution.py:62
  5.6 20.2 %collective-permute-start.3 = (bf16[32,3072]{1,0:T(8,128)(2,1)}, bf16[32,3072]{1,0:T(8,128)(2,1)S(1)}, u32[]{:S(2)}, u32[]{:S(2)}) collective-permute-start(bf16[32,3072]{1,0:T(8,128)(2,1)} %param.7), channel_id=1, source_target_pairs={{0,2},{2,0},{4,6},{6,4},{8,10},{10,8},{12,14},{14,12},{1,3},{3,1},... | collective-permute-start | bytes 589832 | tf_op jit(solution)/shard_map/ppermute | solution.py:56
  13.9 9.1 %collective-permute-start.2 = (bf16[32,3072]{1,0:T(8,128)(2,1)S(1)}, bf16[32,3072]{1,0:T(8,128)(2,1)S(1)}, u32[]{:S(2)}, u32[]{:S(2)}) collective-permute-start(bf16[32,3072]{1,0:T(8,128)(2,1)S(1)} %collective-permute-done.1.refs_2_), channel_id=1, source_target_pairs={{0,4},{2,6},{4,0},{6,2},{8,12},{10,14},{12,8},{14,10},{1,5},{3,7},... | collective-permute-start | bytes 589832 | tf_op jit(solution)/shard_map/ppermute | solution.py:62
  14.4 9.9 %collective-permute-start.5 = (bf16[32,3072]{1,0:T(8,128)(2,1)S(1)}, bf16[32,3072]{1,0:T(8,128)(2,1)S(1)}, u32[]{:S(2)}, u32[]{:S(2)}) collective-permute-start(bf16[32,3072]{1,0:T(8,128)(2,1)S(1)} %collective-permute-done.1.refs_2_), channel_id=1, source_target_pairs={{0,2},{2,0},{4,6},{6,4},{8,10},{10,8},{12,14},{14,12},{1,3},{3,1},... | collective-permute-start | bytes 589832 | tf_op jit(solution)/shard_map/ppermute | solution.py:56
  15.7 10.2 %collective-permute-start.4 = (bf16[32,3072]{1,0:T(8,128)(2,1)S(1)}, bf16[32,3072]{1,0:T(8,128)(2,1)S(1)}, u32[]{:S(2)}, u32[]{:S(2)}) collective-permute-start(bf16[32,3072]{1,0:T(8,128)(2,1)S(1)} %collective-permute-done.refs_1_), channel_id=1, source_target_pairs={{0,2},{2,0},{4,6},{6,4},{8,10},{10,8},{12,14},{14,12},{1,3},{3,1},... | collective-permute-start | bytes 589832 | tf_op jit(solution)/shard_map/ppermute | solution.py:56
  23.0 4.7 %collective-permute-start.6 = (bf16[16,3072]{1,0:T(8,128)(2,1)S(1)}, bf16[16,3072]{1,0:T(8,128)(2,1)S(1)}, u32[]{:S(2)}, u32[]{:S(2)}) collective-permute-start(bf16[16,3072]{1,0:T(8,128)(2,1)S(1)} %slice.29), channel_id=1, source_target_pairs={{0,2},{2,0},{4,6},{6,4},{8,10},{10,8},{12,14},{14,12},{1,3},{3,1},... | collective-permute-start | bytes 294920 | tf_op jit(solution)/shard_map/ppermute | solution.py:56
  24.4 4.7 %collective-permute-start.7 = (bf16[16,3072]{1,0:T(8,128)(2,1)S(1)}, bf16[16,3072]{1,0:T(8,128)(2,1)S(1)}, u32[]{:S(2)}, u32[]{:S(2)}) collective-permute-start(bf16[16,3072]{1,0:T(8,128)(2,1)S(1)} %slice.30), channel_id=1, source_target_pairs={{0,4},{2,6},{4,0},{6,2},{8,12},{10,14},{12,8},{14,10},{1,5},{3,7},... | collective-permute-start | bytes 294920 | tf_op jit(solution)/shard_map/ppermute | solution.py:62
  31.7 3.5 %collective-permute-start.9 = (bf16[256,1536]{1,0:T(8,128)(2,1)S(1)}, bf16[256,1536]{1,0:T(8,128)(2,1)S(1)}, u32[]{:S(2)}, u32[]{:S(2)}) collective-permute-start(bf16[256,1536]{1,0:T(8,128)(2,1)S(1)} %get-tuple-element.29), channel_id=1, source_target_pairs={{0,1},{1,0},{2,3},{3,2},{4,5},{5,4},{6,7},{7,6},{8,9},{9,8},{10,11... | collective-permute-start | bytes 2359304 | tf_op jit(solution)/shard_map/ppermute | solution.py:275
  34.4 5.5 %collective-permute-start.8 = (bf16[256,1536]{1,0:T(8,128)(2,1)S(1)}, bf16[256,1536]{1,0:T(8,128)(2,1)S(1)}, u32[]{:S(2)}, u32[]{:S(2)}) collective-permute-start(bf16[256,1536]{1,0:T(8,128)(2,1)S(1)} %get-tuple-element.27), channel_id=1, source_target_pairs={{0,1},{1,0},{2,3},{3,2},{4,5},{5,4},{6,7},{7,6},{8,9},{9,8},{10,11... | collective-permute-start | bytes 2359304 | tf_op jit(solution)/shard_map/ppermute | solution.py:275
  41.1 10.8 %collective-permute-start.16 = (bf16[2,32,768]{2,1,0:T(8,128)(2,1)S(1)}, bf16[2,32,768]{2,1,0:T(8,128)(2,1)S(1)}, u32[]{:S(2)}, u32[]{:S(2)}) collective-permute-start(bf16[2,32,768]{2,1,0:T(8,128)(2,1)S(1)} %get-tuple-element.43), channel_id=1, source_target_pairs={{0,8},{2,10},{4,12},{6,14},{8,0},{10,2},{12,4},{14,6},{1,9},{3,11}... | collective-permute-start | bytes 294920 | tf_op jit(solution)/shard_map/ppermute | solution.py:62
  44.5 8.4 %collective-permute-start.17 = (bf16[2,32,768]{2,1,0:T(8,128)(2,1)S(1)}, bf16[2,32,768]{2,1,0:T(8,128)(2,1)S(1)}, u32[]{:S(2)}, u32[]{:S(2)}) collective-permute-start(bf16[2,32,768]{2,1,0:T(8,128)(2,1)S(1)} %get-tuple-element.44), channel_id=1, source_target_pairs={{0,12},{2,14},{4,8},{6,10},{8,4},{10,6},{12,0},{14,2},{1,13},{3,15... | collective-permute-start | bytes 294920 | tf_op jit(solution)/shard_map/ppermute | solution.py:62
  44.9 8.1 %collective-permute-start.18 = (bf16[2,32,768]{2,1,0:T(8,128)(2,1)S(1)}, bf16[2,32,768]{2,1,0:T(8,128)(2,1)S(1)}, u32[]{:S(2)}, u32[]{:S(2)}) collective-permute-start(bf16[2,32,768]{2,1,0:T(8,128)(2,1)S(1)} %get-tuple-element.45), channel_id=1, source_target_pairs={{0,4},{2,6},{4,0},{6,2},{8,12},{10,14},{12,8},{14,10},{1,5},{3,7},... | collective-permute-start | bytes 294920 | tf_op jit(solution)/shard_map/ppermute | solution.py:62
  47.1 7.0 %collective-permute-start.10 = (bf16[32,2304]{1,0:T(8,128)(2,1)S(1)}, bf16[32,2304]{1,0:T(8,128)(2,1)S(1)}, u32[]{:S(2)}, u32[]{:S(2)}) collective-permute-start(bf16[32,2304]{1,0:T(8,128)(2,1)S(1)} %get-tuple-element.37), channel_id=1, source_target_pairs={{0,2},{2,0},{4,6},{6,4},{8,10},{10,8},{12,14},{14,12},{1,3},{3,1},... | collective-permute-start | bytes 442376 | tf_op jit(solution)/shard_map/ppermute | solution.py:56
  48.0 9.3 %collective-permute-start.12 = (bf16[32,2304]{1,0:T(8,128)(2,1)S(1)}, bf16[32,2304]{1,0:T(8,128)(2,1)S(1)}, u32[]{:S(2)}, u32[]{:S(2)}) collective-permute-start(bf16[32,2304]{1,0:T(8,128)(2,1)S(1)} %get-tuple-element.39), channel_id=1, source_target_pairs={{0,2},{2,0},{4,6},{6,4},{8,10},{10,8},{12,14},{14,12},{1,3},{3,1},... | collective-permute-start | bytes 442376 | tf_op jit(solution)/shard_map/ppermute | solution.py:56
  52.0 9.0 %collective-permute-start.14 = (bf16[32,2304]{1,0:T(8,128)(2,1)S(1)}, bf16[32,2304]{1,0:T(8,128)(2,1)S(1)}, u32[]{:S(2)}, u32[]{:S(2)}) collective-permute-start(bf16[32,2304]{1,0:T(8,128)(2,1)S(1)} %get-tuple-element.41), channel_id=1, source_target_pairs={{0,2},{2,0},{4,6},{6,4},{8,10},{10,8},{12,14},{14,12},{1,3},{3,1},... | collective-permute-start | bytes 442376 | tf_op jit(solution)/shard_map/ppermute | solution.py:56
  53.1 16.3 %collective-permute-start.19 = (bf16[32,3072]{1,0:T(8,128)(2,1)S(1)}, bf16[32,3072]{1,0:T(8,128)(2,1)S(1)}, u32[]{:S(2)}, u32[]{:S(2)}) collective-permute-start(bf16[32,3072]{1,0:T(8,128)(2,1)S(1)} %pad_maximum_fusion), channel_id=1, source_target_pairs={{0,2},{2,0},{4,6},{6,4},{8,10},{10,8},{12,14},{14,12},{1,3},{3,1},... | collective-permute-start | bytes 589832 | tf_op jit(solution)/shard_map/ppermute | solution.py:56
  54.2 8.1 %collective-permute-start.11 = (bf16[32,2304]{1,0:T(8,128)(2,1)S(1)}, bf16[32,2304]{1,0:T(8,128)(2,1)S(1)}, u32[]{:S(2)}, u32[]{:S(2)}) collective-permute-start(bf16[32,2304]{1,0:T(8,128)(2,1)S(1)} %add_convert_fusion.2), channel_id=1, source_target_pairs={{0,12},{2,14},{4,8},{6,10},{8,4},{10,6},{12,0},{14,2},{1,13},{3,15... | collective-permute-start | bytes 442376 | tf_op jit(solution)/shard_map/ppermute | solution.py:62
  57.3 12.0 %collective-permute-start.13 = (bf16[32,2304]{1,0:T(8,128)(2,1)S(1)}, bf16[32,2304]{1,0:T(8,128)(2,1)S(1)}, u32[]{:S(2)}, u32[]{:S(2)}) collective-permute-start(bf16[32,2304]{1,0:T(8,128)(2,1)S(1)} %add_convert_fusion.1), channel_id=1, source_target_pairs={{0,8},{2,10},{4,12},{6,14},{8,0},{10,2},{12,4},{14,6},{1,9},{3,11}... | collective-permute-start | bytes 442376 | tf_op jit(solution)/shard_map/ppermute | solution.py:62
  61.0 8.3 %collective-permute-start.15 = (bf16[32,2304]{1,0:T(8,128)(2,1)S(1)}, bf16[32,2304]{1,0:T(8,128)(2,1)S(1)}, u32[]{:S(2)}, u32[]{:S(2)}) collective-permute-start(bf16[32,2304]{1,0:T(8,128)(2,1)S(1)} %add_convert_fusion), channel_id=1, source_target_pairs={{0,4},{2,6},{4,0},{6,2},{8,12},{10,14},{12,8},{14,10},{1,5},{3,7},... | collective-permute-start | bytes 442376 | tf_op jit(solution)/shard_map/ppermute | solution.py:62
